TPU v7x, 32 devices: a whole 2x2x4 slice. The times are simulated.
32 devices in a mesh: rows: 8 (over z, x), cols: 4 (over y, core).
Axes of the slice: x: 2, y: 2, z: 4, core: 2. Of those that a mesh axis runs over, the one named last changes fastest.
Arguments:
- pin_feats: bfloat16 [4096, 1024], P('rows', 'cols'), may hold values from -6 to 6
- board_feats: bfloat16 [4096, 512], P('rows', 'cols'), may hold values from -6 to 6
- node_kinds: int32 [4096], P('rows'), may hold values from 0 to 1
- neighbours: int32 [4096, 50], P('rows'), may hold values from 0 to 2047
- visit_counts: int32 [4096, 50], P('rows'), may hold values from 1 to 32
- pull_rows: int32 [8, 2048], P('rows'), may hold values from 0 to 511, as said below
- proj_weight: bfloat16 [512, 1024], P(None, 'cols'), may hold values from -0.25 to 0.25
- proj_bias: float32 [1024], P('cols'), may hold values from -3 to 3
- neigh_weight: bfloat16 [2, 1024, 1024], P(None, None, 'cols'), may hold values from -0.1875 to 0.1875
- neigh_bias: float32 [2, 1024], P(None, 'cols'), may hold values from -3 to 3
- combine_weight: bfloat16 [2, 2048, 1024], P(None, None, 'cols')
- combine_bias: float32 [2, 1024], P(None, 'cols'), may hold values from -3 to 3
- head_weight: bfloat16 [1024, 1024], P(None, 'cols'), may hold values from -0.1875 to 0.1875
- head_bias: float32 [1024], P('cols'), may hold values from -3 to 3
- tail_weight: bfloat16 [1024, 1024], P(None, 'cols'), may hold values from -0.1875 to 0.1875
- tail_bias: float32 [1024], P('cols'), may hold values from -3 to 3
- cotangent: bfloat16 [4096, 1024], P('rows', 'cols'), may hold values from -6 to 6
Outputs:
- embeddings: float32 [4096, 1024], P('rows', 'cols')
- grad_pin: float32 [4096, 1024], P('rows', 'cols')
- grad_board: float32 [4096, 512], P('rows', 'cols')
- grad_proj_weight: float32 [512, 1024], P('rows', 'cols')
- grad_proj_bias: float32 [1024], P('cols')
- grad_neigh_weight: float32 [2, 1024, 1024], P(None, 'rows', 'cols')
- grad_neigh_bias: float32 [2, 1024], P(None, 'cols')
- grad_combine_weight: float32 [2, 2048, 1024], P(None, 'rows', 'cols')
- grad_combine_bias: float32 [2, 1024], P(None, 'cols')
- grad_head_weight: float32 [1024, 1024], P('rows', 'cols')
- grad_head_bias: float32 [1024], P('cols')
- grad_tail_weight: float32 [1024, 1024], P('rows', 'cols')
- grad_tail_bias: float32 [1024], P('cols')
Inputs may be any that keep to these rules, and one draw needn't show every extreme that they name: `pull_rows`: row r's entries s * 256 to (s + 1) * 256 - 1 are 256 distinct local row numbers of row shard s.
All inputs are finite; a program needn't handle non-finite values.
Results may differ from a plain program's by a relative error of at most 0.029.
Values may be sent and summed in bfloat16 or wider, within the bound.
No kernel may reach another device: no remote copies, remote signals or barrier semaphores. Data moves between devices by JAX's collectives and lax.ppermute only.
A program may use at most 128 MiB of HBM per device.

v0:
```python
import jax
import jax.numpy as jnp
from jax import lax
from jax.sharding import PartitionSpec as P

eps = 1e-06
highest = lax.Precision.HIGHEST


def product(left_side, right_side):
    return jnp.dot(left_side, right_side, preferred_element_type=jnp.float32)


def product_t(left_side, right_side):
    return lax.dot_general(
        left_side, right_side, (((0,), (0,)), ((), ())), preferred_element_type=jnp.float32
    )


def product_rt(left_side, right_side):
    return lax.dot_general(
        left_side, right_side, (((1,), (1,)), ((), ())), preferred_element_type=jnp.float32
    )


def act_grad(pre_act, upstream):
    return jax.vjp(jax.nn.gelu, pre_act)[1](upstream)[0]


def spread(shard):
    return lax.all_gather(shard, "cols", axis=1, tiled=True)


def col_sum(partial_term):
    return lax.psum_scatter(
        partial_term.astype(jnp.bfloat16), "cols", scatter_dimension=1, tiled=True
    ).astype(jnp.float32)


def split_pair(values):
    high_part = values.astype(jnp.bfloat16)
    low_part = (values - high_part.astype(jnp.float32)).astype(jnp.bfloat16)
    return (high_part, low_part)


def share_matrix(neighbours, shares, pool_size):
    row_total, fan = neighbours.shape
    low_width = 128
    high_width = pool_size // low_width
    upper_idx = neighbours // low_width
    lower_idx = neighbours % low_width
    upper_hot = jnp.where(
        upper_idx[:, :, None] == jnp.arange(high_width, dtype=jnp.int32)[None, None, :],
        shares[:, :, None],
        0.0,
    )
    lower_hot = (
        lower_idx[:, :, None] == jnp.arange(low_width, dtype=jnp.int32)[None, None, :]
    ).astype(jnp.float32)
    weights_dense = jnp.einsum(
        "vkh,vkl->vhl", upper_hot, lower_hot, precision=highest, preferred_element_type=jnp.float32
    )
    return split_pair(weights_dense.reshape(row_total, pool_size))


def aggregate(pooled, share_pair):
    return product(share_pair[0], pooled) + product(share_pair[1], pooled)


def scatter_back(upstream, share_pair):
    grad_high, grad_low = split_pair(upstream)
    return (
        product_t(share_pair[0], grad_high)
        + product_t(share_pair[0], grad_low)
        + product_t(share_pair[1], grad_high)
    )


def forward_layer(hidden, neigh_w, neigh_b, combine_w, combine_b, graph, capacity):
    selector, share_pair = graph
    whole = spread(hidden)
    width = whole.shape[1]
    neigh_pre = product(whole, neigh_w) + neigh_b
    shipped = jax.nn.gelu(neigh_pre).astype(jnp.bfloat16)
    channels = shipped.shape[1]
    outgoing = product(selector, shipped).astype(jnp.bfloat16).reshape(-1, capacity, channels)
    pooled = lax.all_to_all(outgoing, "rows", split_axis=0, concat_axis=0, tiled=True).reshape(
        -1, channels
    )
    gathered = aggregate(pooled, share_pair).astype(jnp.bfloat16)
    gathered_whole = spread(gathered)
    combine_pre = (
        product(whole, combine_w[:width]) + product(gathered_whole, combine_w[width:]) + combine_b
    )
    activated = jax.nn.gelu(combine_pre)
    squares = lax.psum(jnp.sum(activated * activated, axis=1), "cols")
    inv_scale = lax.rsqrt(squares / width + eps)
    output = (activated * inv_scale[:, None]).astype(jnp.bfloat16)
    return (output, (whole, gathered_whole, neigh_pre, combine_pre, inv_scale))


def backward_layer(upstream, saved, neigh_w, combine_w, graph, capacity):
    selector, share_pair = graph
    whole, gathered_whole, neigh_pre, combine_pre, inv_scale = saved
    width = whole.shape[1]
    activated = jax.nn.gelu(combine_pre)
    inner_prod = lax.psum(jnp.sum(activated * upstream, axis=1), "cols")
    act_upstream = (
        inv_scale[:, None] * upstream
        - activated * (inv_scale * inv_scale * inv_scale * inner_prod / width)[:, None]
    )
    combine_grad = act_grad(combine_pre, act_upstream).astype(jnp.bfloat16)
    combine_bias_grad = jnp.sum(combine_grad.astype(jnp.float32), axis=0)
    combine_term = jnp.concatenate(
        [product_t(whole, combine_grad), product_t(gathered_whole, combine_grad)], axis=0
    )
    self_part = product_rt(combine_grad, combine_w[:width])
    neigh_grad = col_sum(product_rt(combine_grad, combine_w[width:]))
    channels = neigh_grad.shape[1]
    pool_grad = scatter_back(neigh_grad, share_pair)
    returned = (
        lax.all_to_all(
            pool_grad.reshape(-1, capacity, channels).astype(jnp.bfloat16),
            "rows",
            split_axis=0,
            concat_axis=0,
            tiled=True,
        )
        .astype(jnp.float32)
        .reshape(-1, channels)
    )
    back_high, back_low = split_pair(returned)
    moved_grad = product_t(selector, back_high) + product_t(selector, back_low)
    neigh_grad_pre = act_grad(neigh_pre, moved_grad).astype(jnp.bfloat16)
    neigh_bias_grad = jnp.sum(neigh_grad_pre.astype(jnp.float32), axis=0)
    neigh_term = product_t(whole, neigh_grad_pre)
    lower_grad = col_sum(self_part + product_rt(neigh_grad_pre, neigh_w))
    neigh_out, combine_out = (
        lax.psum_scatter(
            neigh_term.astype(jnp.bfloat16), "rows", scatter_dimension=0, tiled=True
        ).astype(jnp.float32),
        lax.psum_scatter(
            combine_term.astype(jnp.bfloat16), "rows", scatter_dimension=0, tiled=True
        ).astype(jnp.float32),
    )
    return (lower_grad, (neigh_out, combine_out, neigh_bias_grad, combine_bias_grad))


def body(
    pin_feats,
    board_feats,
    node_kinds,
    neighbours,
    visit_counts,
    pull_rows,
    proj_weight,
    proj_bias,
    neigh_weight,
    neigh_bias,
    combine_weight,
    combine_bias,
    head_weight,
    head_bias,
    tail_weight,
    tail_bias,
    cotangent,
):
    row_count = lax.axis_size("rows")
    capacity = pull_rows.shape[1] // row_count
    pool_size = pull_rows.shape[1]
    local_rows = pin_feats.shape[0]
    requested = lax.all_to_all(
        pull_rows.reshape(row_count, capacity), "rows", split_axis=0, concat_axis=0, tiled=True
    ).reshape(-1)
    selector = (requested[:, None] == jnp.arange(local_rows, dtype=jnp.int32)[None, :]).astype(
        jnp.bfloat16
    )
    counts = visit_counts.astype(jnp.float32)
    shares = counts / jnp.sum(counts, axis=1, keepdims=True)
    graph = (selector, share_matrix(neighbours, shares, pool_size))
    is_board = (node_kinds == 1)[:, None]
    depth = neigh_weight.shape[0]
    board_whole = spread(board_feats)
    board_pre = product(board_whole, proj_weight) + proj_bias
    hidden = jnp.where(is_board, jax.nn.gelu(board_pre), pin_feats.astype(jnp.float32)).astype(
        jnp.bfloat16
    )
    kept = []
    for layer_idx in range(depth):
        hidden, saved = forward_layer(
            hidden,
            neigh_weight[layer_idx],
            neigh_bias[layer_idx],
            combine_weight[layer_idx],
            combine_bias[layer_idx],
            graph,
            capacity,
        )
        kept.append(saved)
    last_whole = spread(hidden)
    head_pre = product(last_whole, head_weight) + head_bias
    inner_act = jax.nn.gelu(head_pre).astype(jnp.bfloat16)
    inner_whole = spread(inner_act)
    embeddings = product(inner_whole, tail_weight) + tail_bias
    tail_bias_grad = jnp.sum(cotangent.astype(jnp.float32), axis=0)
    tail_term = product_t(inner_whole, cotangent)
    inner_grad = col_sum(product_rt(cotangent, tail_weight))
    head_grad_pre = act_grad(head_pre, inner_grad).astype(jnp.bfloat16)
    head_bias_grad = jnp.sum(head_grad_pre.astype(jnp.float32), axis=0)
    head_term = product_t(last_whole, head_grad_pre)
    hidden_grad = col_sum(product_rt(head_grad_pre, head_weight))
    results = [None] * depth
    for layer_idx in reversed(range(depth)):
        hidden_grad, results[layer_idx] = backward_layer(
            hidden_grad,
            kept[layer_idx],
            neigh_weight[layer_idx],
            combine_weight[layer_idx],
            graph,
            capacity,
        )
    grad_pin = jnp.where(is_board, 0.0, hidden_grad)
    board_upstream = jnp.where(is_board, hidden_grad, 0.0)
    board_grad_pre = act_grad(board_pre, board_upstream).astype(jnp.bfloat16)
    proj_bias_grad = jnp.sum(board_grad_pre.astype(jnp.float32), axis=0)
    proj_term = product_t(board_whole, board_grad_pre)
    grad_board = col_sum(product_rt(board_grad_pre, proj_weight))
    tail_out, head_out, proj_out = (
        lax.psum_scatter(
            tail_term.astype(jnp.bfloat16), "rows", scatter_dimension=0, tiled=True
        ).astype(jnp.float32),
        lax.psum_scatter(
            head_term.astype(jnp.bfloat16), "rows", scatter_dimension=0, tiled=True
        ).astype(jnp.float32),
        lax.psum_scatter(
            proj_term.astype(jnp.bfloat16), "rows", scatter_dimension=0, tiled=True
        ).astype(jnp.float32),
    )
    neigh_bias_all = jnp.stack([entry[2] for entry in results])
    combine_bias_all = jnp.stack([entry[3] for entry in results])
    neigh_bias_sum, combine_bias_sum, head_bias_sum, tail_bias_sum, proj_bias_sum = lax.psum(
        (neigh_bias_all, combine_bias_all, head_bias_grad, tail_bias_grad, proj_bias_grad), "rows"
    )
    neigh_out = jnp.stack([entry[0] for entry in results])
    combine_out = jnp.stack([entry[1] for entry in results])
    return (
        embeddings,
        grad_pin,
        grad_board,
        proj_out,
        proj_bias_sum,
        neigh_out,
        neigh_bias_sum,
        combine_out,
        combine_bias_sum,
        head_out,
        head_bias_sum,
        tail_out,
        tail_bias_sum,
    )


def solution(mesh):
    placed = (
        P("rows", "cols"),
        P("rows", "cols"),
        P("rows"),
        P("rows", None),
        P("rows", None),
        P("rows", None),
        P(None, "cols"),
        P("cols"),
        P(None, None, "cols"),
        P(None, "cols"),
        P(None, None, "cols"),
        P(None, "cols"),
        P(None, "cols"),
        P("cols"),
        P(None, "cols"),
        P("cols"),
        P("rows", "cols"),
    )
    return jax.shard_map(
        body,
        mesh=mesh,
        in_specs=placed,
        out_specs=(
            P("rows", "cols"),
            P("rows", "cols"),
            P("rows", "cols"),
            P("rows", "cols"),
            P("cols"),
            P(None, "rows", "cols"),
            P(None, "cols"),
            P(None, "rows", "cols"),
            P(None, "cols"),
            P("rows", "cols"),
            P("cols"),
            P("rows", "cols"),
            P("cols"),
        ),
        check_vma=False,
    )
```

profile of v0, /device:TPU:0, one launch (start us, length us, event | category | flops | bytes accessed | tf_op | source)
XLA Modules:
  0.0 956.1 jit_solution(8828863778824062594)
XLA Ops:
  25.2 12.0 %all-gather.7.cloned.1.call-done = bf16[512,1024]{1,0:T(8,128)(2,1)} async-done(((bf16[512,256]{1,0:T(8,128)(2,1)}), bf16[512,1024]{1,0:T(8,128)(2,1)}) %all-gather.7.cloned.1.call-update) | async-done | bytes 1048592 | tf_op jit(solution)/shard_map/all_gather | solution.py:31
  48.1 12.1 %subtract_convert_fusion = (bf16[512,16,128]{2,1,0:T(8,128)(2,1)}, bf16[512,16,128]{2,1,0:T(8,128)(2,1)}, f32[512,16,128]{2,1,0:T(8,128)}) fusion(s32[512,50]{1,0:T(8,128)S(1)} %copy.40, f32[512,50]{1,0:T(8,128)S(1)} %copy.39, s32[512,50]{1,0:T(8,128)S(1)} %copy.38), kind=kOutput, calls=%fused_computation.6 | convolution fusion | flops 637435904 | bytes 8695808 | tf_op jit(solution)/shard_map/vkh,vkl->vhl/dot_general | solution.py:60
  60.2 13.5 %all-to-all-done.1 = bf16[8,256,256]{2,1,0:T(8,128)(2,1)S(1)} async-done(((bf16[8,256,256]{2,1,0:T(8,128)(2,1)}), bf16[8,256,256]{2,1,0:T(8,128)(2,1)S(1)}, u32[]{:S(2)}, u32[]{:S(2)}) %all-to-all-start.1) | async-done | bytes 1048608 | tf_op jit(solution)/shard_map/all_to_all | solution.py:87
  81.8 12.6 %all-gather.9.cloned.1.call-done = bf16[512,1024]{1,0:T(8,128)(2,1)} async-done(((bf16[512,256]{1,0:T(8,128)(2,1)}), bf16[512,1024]{1,0:T(8,128)(2,1)}) %all-gather.9.cloned.1.call-update) | async-done | bytes 1048592 | tf_op jit(solution)/shard_map/all_gather | solution.py:31
  103.2 18.0 %all-gather.11.cloned.1.call-done = bf16[512,1024]{1,0:T(8,128)(2,1)} async-done(((bf16[512,256]{1,0:T(8,128)(2,1)}), bf16[512,1024]{1,0:T(8,128)(2,1)}) %all-gather.11.cloned.1.call-update) | async-done | bytes 1048592 | tf_op jit(solution)/shard_map/all_gather | solution.py:31
  124.4 31.6 %all_to_all.29 = bf16[8,256,256]{2,1,0:T(8,128)(2,1)S(1)} all-to-all(bf16[8,256,256]{2,1,0:T(8,128)(2,1)S(1)} %bitcast.162), channel_id=1, replica_groups=mesh['rows'=8,'cols'=4] {'rows'}, dimensions={0} | all-to-all | bytes 2097152 | tf_op jit(solution)/shard_map/all_to_all | solution.py:87
  164.1 10.1 %all-gather.13.cloned.1.call-done = bf16[512,1024]{1,0:T(8,128)(2,1)} async-done(((bf16[512,256]{1,0:T(8,128)(2,1)}), bf16[512,1024]{1,0:T(8,128)(2,1)}) %all-gather.13.cloned.1.call-update) | async-done | bytes 1048592 | tf_op jit(solution)/shard_map/all_gather | solution.py:31
  183.2 18.2 %reduce-scatter.19.cloned.1.call-done = bf16[512,256]{1,0:T(8,128)(2,1)} async-done(((bf16[512,1024]{1,0:T(8,128)(2,1)}), bf16[512,256]{1,0:T(8,128)(2,1)}) %reduce-scatter.19.cloned.1.call-update) | async-done | bytes 262160 | tf_op jit(solution)/shard_map/reduce_scatter | solution.py:35
  201.4 19.0 %all-gather.15.cloned.1.call-done = bf16[512,1024]{1,0:T(8,128)(2,1)} async-done(((bf16[512,256]{1,0:T(8,128)(2,1)}), bf16[512,1024]{1,0:T(8,128)(2,1)}) %all-gather.15.cloned.1.call-update) | async-done | bytes 1048592 | tf_op jit(solution)/shard_map/all_gather | solution.py:31
  224.6 25.0 %reduce-scatter.21.cloned.1.call-done = bf16[512,256]{1,0:T(8,128)(2,1)} async-done(((bf16[512,1024]{1,0:T(8,128)(2,1)}), bf16[512,256]{1,0:T(8,128)(2,1)}) %reduce-scatter.21.cloned.1.call-update) | async-done | bytes 262160 | tf_op jit(solution)/shard_map/reduce_scatter | solution.py:35
  260.7 26.1 %reduce-scatter.23.cloned.1.call-done = bf16[512,256]{1,0:T(8,128)(2,1)} async-done(((bf16[512,1024]{1,0:T(8,128)(2,1)}), bf16[512,256]{1,0:T(8,128)(2,1)}) %reduce-scatter.23.cloned.1.call-update) | async-done | bytes 262160 | tf_op jit(solution)/shard_map/reduce_scatter | solution.py:35
  304.2 24.3 %all-to-all-done.3 = bf16[8,256,256]{2,1,0:T(8,128)(2,1)} async-done(((bf16[8,256,256]{2,1,0:T(8,128)(2,1)}), bf16[8,256,256]{2,1,0:T(8,128)(2,1)}, u32[]{:S(2)}, u32[]{:S(2)}) %all-to-all-start.3) | async-done | bytes 1048608 | tf_op jit(solution)/shard_map/all_to_all | solution.py:122
  336.2 23.1 %reduce-scatter.25.cloned.1.call-done = bf16[512,256]{1,0:T(8,128)(2,1)} async-done(((bf16[512,1024]{1,0:T(8,128)(2,1)}), bf16[512,256]{1,0:T(8,128)(2,1)}) %reduce-scatter.25.cloned.1.call-update) | async-done | bytes 262160 | tf_op jit(solution)/shard_map/reduce_scatter | solution.py:35
  370.4 26.1 %reduce-scatter.27.cloned.1.call-done = bf16[512,256]{1,0:T(8,128)(2,1)} async-done(((bf16[512,1024]{1,0:T(8,128)(2,1)}), bf16[512,256]{1,0:T(8,128)(2,1)}) %reduce-scatter.27.cloned.1.call-update) | async-done | bytes 262160 | tf_op jit(solution)/shard_map/reduce_scatter | solution.py:35
  414.8 23.3 %all-to-all-done.4 = bf16[8,256,256]{2,1,0:T(8,128)(2,1)} async-done(((bf16[8,256,256]{2,1,0:T(8,128)(2,1)}), bf16[8,256,256]{2,1,0:T(8,128)(2,1)}, u32[]{:S(2)}, u32[]{:S(2)}) %all-to-all-start.4) | async-done | bytes 1048608 | tf_op jit(solution)/shard_map/all_to_all | solution.py:122
  473.8 60.9 %reduce-scatter.39.cloned.1.call-done = bf16[128,256]{1,0:T(8,128)(2,1)} async-done(((bf16[1024,256]{1,0:T(8,128)(2,1)}), bf16[128,256]{1,0:T(8,128)(2,1)}) %reduce-scatter.39.cloned.1.call-update) | async-done | bytes 65552 | tf_op jit(solution)/shard_map/reduce_scatter | solution.py:232
  537.6 61.7 %reduce-scatter.41.cloned.1.call-done = bf16[128,256]{1,0:T(8,128)(2,1)} async-done(((bf16[1024,256]{1,0:T(8,128)(2,1)}), bf16[128,256]{1,0:T(8,128)(2,1)}) %reduce-scatter.41.cloned.1.call-update) | async-done | bytes 65552 | tf_op jit(solution)/shard_map/reduce_scatter | solution.py:229
  600.7 64.3 %reduce-scatter.37.cloned.1.call-done = bf16[256,256]{1,0:T(8,128)(2,1)} async-done(((bf16[2048,256]{1,0:T(8,128)(2,1)}), bf16[256,256]{1,0:T(8,128)(2,1)}) %reduce-scatter.37.cloned.1.call-update) | async-done | bytes 131088 | tf_op jit(solution)/shard_map/reduce_scatter | solution.py:142
  665.1 66.0 %reduce-scatter.35.cloned.1.call-done = bf16[256,256]{1,0:T(8,128)(2,1)} async-done(((bf16[2048,256]{1,0:T(8,128)(2,1)}), bf16[256,256]{1,0:T(8,128)(2,1)}) %reduce-scatter.35.cloned.1.call-update) | async-done | bytes 131088 | tf_op jit(solution)/shard_map/reduce_scatter | solution.py:142
  732.9 62.3 %reduce-scatter.33.cloned.1.call-done = bf16[128,256]{1,0:T(8,128)(2,1)} async-done(((bf16[1024,256]{1,0:T(8,128)(2,1)}), bf16[128,256]{1,0:T(8,128)(2,1)}) %reduce-scatter.33.cloned.1.call-update) | async-done | bytes 65552 | tf_op jit(solution)/shard_map/reduce_scatter | solution.py:139
  795.2 64.6 %reduce-scatter.31.cloned.1.call-done = bf16[128,256]{1,0:T(8,128)(2,1)} async-done(((bf16[1024,256]{1,0:T(8,128)(2,1)}), bf16[128,256]{1,0:T(8,128)(2,1)}) %reduce-scatter.31.cloned.1.call-update) | async-done | bytes 65552 | tf_op jit(solution)/shard_map/reduce_scatter | solution.py:139
  861.3 20.3 %all-reduce = (f32[256]{0:T(256)}, f32[2,256]{1,0:T(2,128)}, f32[2,256]{1,0:T(2,128)}, f32[256]{0:T(256)}, f32[256]{0:T(256)}) all-reduce(f32[256]{0:T(256)S(1)} %get-tuple-element.50, f32[2,256]{1,0:T(2,128)S(1)} %get-tuple-element.73, f32[2,256]{1,0:T(2,128)S(1)} %get-tuple-element.74, ...), channel_id=1, replica_groups=mesh['rows'=8,'cols'=4] {'rows'}, use_global_device_ids=true, to_apply=%region_18.19 | all-reduce | flops 1792 | bytes 14336 | tf_op jit(solution)/shard_map/psum | solution.py:241
  881.6 42.4 %reduce-scatter.45.cloned.1.call-done = bf16[64,256]{1,0:T(8,128)(2,1)} async-done(((bf16[512,256]{1,0:T(8,128)(2,1)}), bf16[64,256]{1,0:T(8,128)(2,1)}) %reduce-scatter.45.cloned.1.call-update) | async-done | bytes 32784
  925.5 21.5 %reduce-scatter.43.cloned.1.call-done = bf16[128,512]{1,0:T(8,128)(2,1)} async-done(((bf16[512,512]{1,0:T(8,128)(2,1)}), bf16[128,512]{1,0:T(8,128)(2,1)}) %reduce-scatter.43.cloned.1.call-update) | async-done | bytes 131088
  (205 shorter events, 181.9 us)
Async XLA Ops:
  7.2 30.0 %all-gather.7.cloned.1.call-start = ((), (), s32[]{:S(2)}) async-start(), calls=%async_computation.19 | async-start | bytes 1310720 | tf_op jit(solution)/shard_map/all_gather | solution.py:31
  19.4 19.6 %all-to-all-start = ((s32[8,1,256]{2,1,0:T(1,128)}), s32[8,1,256]{2,1,0:T(1,128)S(1)}, u32[]{:S(2)}, u32[]{:S(2)}) async-start(s32[8,1,256]{2,1,0:T(1,128)} %bitcast.1), calls=%async_computation | async-start | bytes 16384 | tf_op jit(solution)/shard_map/all_to_all | solution.py:172
  41.8 31.8 %all-to-all-start.1 = ((bf16[8,256,256]{2,1,0:T(8,128)(2,1)}), bf16[8,256,256]{2,1,0:T(8,128)(2,1)S(1)}, u32[]{:S(2)}, u32[]{:S(2)}) async-start(bf16[8,256,256]{2,1,0:T(8,128)(2,1)} %bitcast.5), calls=%async_computation.1 | async-start | bytes 2097152 | tf_op jit(solution)/shard_map/all_to_all | solution.py:87
  47.5 46.9 %all-gather.9.cloned.1.call-start = ((), (), s32[]{:S(2)}) async-start(), calls=%async_computation.20 | async-start | bytes 1310720 | tf_op jit(solution)/shard_map/all_gather | solution.py:31
  79.2 42.0 %all-gather.11.cloned.1.call-start = ((), (), s32[]{:S(2)}) async-start(), calls=%async_computation.21 | async-start | bytes 1310720 | tf_op jit(solution)/shard_map/all_gather | solution.py:31
  103.2 70.9 %all-gather.13.cloned.1.call-start = ((), (), s32[]{:S(2)}) async-start(), calls=%async_computation.22 | async-start | bytes 1310720 | tf_op jit(solution)/shard_map/all_gather | solution.py:31
  159.0 42.4 %reduce-scatter.19.cloned.1.call-start = ((), (), s32[]{:S(2)}) async-start(), calls=%async_computation.25 | async-start | bytes 1310720 | tf_op jit(solution)/shard_map/reduce_scatter | solution.py:35
  161.5 58.8 %all-gather.15.cloned.1.call-start = ((), (), s32[]{:S(2)}) async-start(), calls=%async_computation.23 | async-start | bytes 1310720 | tf_op jit(solution)/shard_map/all_gather | solution.py:31
  183.1 66.5 %reduce-scatter.21.cloned.1.call-start = ((), (), s32[]{:S(2)}) async-start(), calls=%async_computation.26 | async-start | bytes 1310720 | tf_op jit(solution)/shard_map/reduce_scatter | solution.py:35
  224.6 62.3 %reduce-scatter.23.cloned.1.call-start = ((), (), s32[]{:S(2)}) async-start(), calls=%async_computation.27 | async-start | bytes 1310720 | tf_op jit(solution)/shard_map/reduce_scatter | solution.py:35
  297.1 31.4 %all-to-all-start.3 = ((bf16[8,256,256]{2,1,0:T(8,128)(2,1)}), bf16[8,256,256]{2,1,0:T(8,128)(2,1)}, u32[]{:S(2)}, u32[]{:S(2)}) async-start(bf16[8,256,256]{2,1,0:T(8,128)(2,1)} %bitcast.16), calls=%async_computation.6 | async-start | bytes 2097152 | tf_op jit(solution)/shard_map/all_to_all | solution.py:122
  302.7 56.6 %reduce-scatter.25.cloned.1.call-start = ((), (), s32[]{:S(2)}) async-start(), calls=%async_computation.28 | async-start | bytes 1310720 | tf_op jit(solution)/shard_map/reduce_scatter | solution.py:35
  336.1 60.4 %reduce-scatter.27.cloned.1.call-start = ((), (), s32[]{:S(2)}) async-start(), calls=%async_computation.29 | async-start | bytes 1310720 | tf_op jit(solution)/shard_map/reduce_scatter | solution.py:35
  406.7 31.4 %all-to-all-start.4 = ((bf16[8,256,256]{2,1,0:T(8,128)(2,1)}), bf16[8,256,256]{2,1,0:T(8,128)(2,1)}, u32[]{:S(2)}, u32[]{:S(2)}) async-start(bf16[8,256,256]{2,1,0:T(8,128)(2,1)} %bitcast.18), calls=%async_computation.9 | async-start | bytes 2097152 | tf_op jit(solution)/shard_map/all_to_all | solution.py:122
  412.3 36.2 %all-gather.17.cloned.1.call-start = ((), (), s32[]{:S(2)}) async-start(), calls=%async_computation.24 | async-start | bytes 1310720 | tf_op jit(solution)/shard_map/all_gather | solution.py:31
  413.0 55.9 %reduce-scatter.29.cloned.1.call-start = ((), (), s32[]{:S(2)}) async-start(), calls=%async_computation.30 | async-start | bytes 1310720 | tf_op jit(solution)/shard_map/reduce_scatter | solution.py:35
  445.8 89.0 %reduce-scatter.39.cloned.1.call-start = ((), (), s32[]{:S(2)}) async-start(), calls=%async_computation.35 | async-start | bytes 589824 | tf_op jit(solution)/shard_map/reduce_scatter | solution.py:232
  448.4 150.9 %reduce-scatter.41.cloned.1.call-start = ((), (), s32[]{:S(2)}) async-start(), calls=%async_computation.36 | async-start | bytes 589824 | tf_op jit(solution)/shard_map/reduce_scatter | solution.py:229
  451.2 213.8 %reduce-scatter.37.cloned.1.call-start = ((), (), s32[]{:S(2)}) async-start(), calls=%async_computation.34 | async-start | bytes 1179648 | tf_op jit(solution)/shard_map/reduce_scatter | solution.py:142
  453.5 277.6 %reduce-scatter.35.cloned.1.call-start = ((), (), s32[]{:S(2)}) async-start(), calls=%async_computation.33 | async-start | bytes 1179648 | tf_op jit(solution)/shard_map/reduce_scatter | solution.py:142
  457.0 338.2 %reduce-scatter.33.cloned.1.call-start = ((), (), s32[]{:S(2)}) async-start(), calls=%async_computation.32 | async-start | bytes 589824 | tf_op jit(solution)/shard_map/reduce_scatter | solution.py:139
  459.6 400.1 %reduce-scatter.31.cloned.1.call-start = ((), (), s32[]{:S(2)}) async-start(), calls=%async_computation.31 | async-start | bytes 589824 | tf_op jit(solution)/shard_map/reduce_scatter | solution.py:139
  461.0 463.0 %reduce-scatter.45.cloned.1.call-start = ((), (), s32[]{:S(2)}) async-start(), calls=%async_computation.38 | async-start | bytes 294912
  472.3 474.8 %reduce-scatter.43.cloned.1.call-start = ((), (), s32[]{:S(2)}) async-start(), calls=%async_computation.37 | async-start | bytes 655360
  (38 other events, 1087.3 us)
Sparse Core Ops, SparseCore 0:
  19.5 17.7 all-gather.6
  79.4 14.9 all-gather.8
  103.3 17.8 all-gather.10
  159.1 14.9 all-gather.12
  176.5 24.8 reduce-scatter.18
  203.4 16.8 all-gather.14
  224.7 24.8 reduce-scatter.20
  260.9 25.9 reduce-scatter.22
  336.2 22.9 reduce-scatter.24
  370.6 25.9 reduce-scatter.26
  415.3 17.3 all-gather.16
  445.9 22.9 reduce-scatter.28
  472.8 61.9 reduce-scatter.38
  538.3 60.8 reduce-scatter.40
  602.5 62.5 reduce-scatter.36
  668.7 62.3 reduce-scatter.34
  734.3 60.8 reduce-scatter.32
  798.7 60.9 reduce-scatter.30
  863.6 60.2 reduce-scatter.44
  926.3 20.7 reduce-scatter.42
where the time goes:
time: 966 us; the launch traced here: 956 us
  waiting for transfers between devices  704 us (73%)
  matrix products  102 us (11%)
  blocking collectives  84.5 us (9%)
  starting transfers between devices  23.6 us (2%)
  other arithmetic  19.8 us (2%)
  between operations  15.4 us (2%)
    reduce_scatter x2, waiting for transfers between devices, backward_layer(): lax.psum_scatter(combine_term.astype(jnp.bfloat16), 'rows', scatter_dimen...  130 us
    reduce_scatter x2, waiting for transfers between devices, backward_layer(): lax.psum_scatter(neigh_term.astype(jnp.bfloat16), 'rows', scatter_dimensi...  127 us
    reduce_scatter x6, waiting for transfers between devices, col_sum(): lax.psum_scatter(partial_term.astype(jnp.bfloat16), 'cols', scatter_dimen...  126 us
    all_gather x6, waiting for transfers between devices, spread(): return lax.all_gather(shard, 'cols', axis=1, tiled=True)  71.7 us
    unnamed x22, waiting for transfers between devices  64.8 us
    reduce_scatter x1, waiting for transfers between devices, body(): lax.psum_scatter(tail_term.astype(jnp.bfloat16), 'rows', scatter_dimensio...  61.7 us
    reduce_scatter x1, waiting for transfers between devices, body(): lax.psum_scatter(head_term.astype(jnp.bfloat16), 'rows', scatter_dimensio...  60.9 us
    all_to_all x2, waiting for transfers between devices, backward_layer(): lax.all_to_all(pool_grad.reshape(-1, capacity, channels).astype(jnp.bfloa...  47.6 us
  transfers between devices with their start and end apart: 24, of which 22 were waited for; matrix products, arithmetic and copies ran while one was open for 7% of the time, Pallas kernels for 0%

commit v1 on v0

v1 whole, which is shorter than its diff:
```python
import jax
import jax.numpy as jnp
from jax import lax
from jax.sharding import PartitionSpec as P

eps = 1e-06
bf16 = jnp.bfloat16
f32 = jnp.float32


def product(left_side, right_side):
    return jnp.dot(left_side, right_side, preferred_element_type=f32)


def product_t(left_side, right_side):
    return lax.dot_general(
        left_side, right_side, (((0,), (0,)), ((), ())), preferred_element_type=f32
    )


def product_rt(left_side, right_side):
    return lax.dot_general(
        left_side, right_side, (((1,), (1,)), ((), ())), preferred_element_type=f32
    )


def act_grad(pre_act, upstream):
    return jax.vjp(jax.nn.gelu, pre_act)[1](upstream)[0]


def swap(array, axis, distance):
    size = lax.axis_size(axis)
    return lax.ppermute(array, axis, [(i, i ^ distance) for i in range(size)])


def gather_cols(shard):
    size = lax.axis_size("cols")
    even = [shard] + [swap(shard, "cols", far) for far in range(2, size, 2)]
    blocks = []
    for block in even:
        blocks += [block, swap(block, "cols", 1)]
    return blocks


def natural(blocks):
    me = lax.axis_index("cols")
    step = 1
    while step < len(blocks):
        flip = (me & step) != 0
        blocks = [
            jnp.where(flip, blocks[j ^ step], blocks[j]) for j in range(len(blocks))
        ]
        step *= 2
    return blocks


def spread(shard):
    return jnp.concatenate(natural(gather_cols(shard)), axis=1)


def col_sum(partial_term):
    size = lax.axis_size("cols")
    blocks = natural(jnp.split(partial_term.astype(bf16), size, axis=1))
    total = blocks[0].astype(f32) + swap(blocks[1], "cols", 1).astype(f32)
    for far in range(2, size, 2):
        pair = blocks[far].astype(f32) + swap(blocks[far + 1], "cols", 1).astype(f32)
        total = total + swap(pair.astype(bf16), "cols", far).astype(f32)
    return total


def row_exchange(chunks, groups=None):
    return lax.all_to_all(
        chunks, "rows", split_axis=0, concat_axis=0, tiled=True, axis_index_groups=groups
    )


def chunked(terms):
    row_count = lax.axis_size("rows")
    return jnp.concatenate(
        [t.astype(bf16).reshape(row_count, -1, t.shape[-1]) for t in terms], axis=1
    )


def unchunked(kept, terms):
    row_count = lax.axis_size("rows")
    sizes = [t.shape[0] // row_count for t in terms]
    outs, at = [], 0
    for size in sizes:
        outs.append(kept[at : at + size])
        at += size
    return outs


def sum_rows_far(terms):
    kept = lax.psum_scatter(chunked(terms), "rows", scatter_dimension=0, tiled=True)
    return unchunked(kept[0].astype(f32), terms)


def sum_rows_near(terms):
    row_count = lax.axis_size("rows")
    chunks = chunked(terms)
    chunks = chunks.reshape((row_count // 2, 2) + chunks.shape[1:])
    odd = (lax.axis_index("rows") & 1) != 0
    mine = jnp.where(odd, chunks[:, 1], chunks[:, 0])
    other = jnp.where(odd, chunks[:, 0], chunks[:, 1])
    pair = (mine.astype(f32) + swap(other, "rows", 1).astype(f32)).astype(bf16)
    groups = [list(range(start, row_count, 2)) for start in range(2)]
    kept = jnp.sum(row_exchange(pair, groups).astype(f32), axis=0)
    return unchunked(kept, terms)


def sum_rows_last(terms, biases):
    row_count = lax.axis_size("rows")
    chunks = chunked(terms)
    stacked = jnp.concatenate(biases, axis=0)
    high_part = stacked.astype(bf16)
    low_part = (stacked - high_part.astype(f32)).astype(bf16)
    pad = (-2 * stacked.shape[0]) % 16
    tail = jnp.concatenate(
        [high_part, low_part, jnp.zeros((pad, stacked.shape[1]), bf16)], axis=0
    )
    tail = jnp.broadcast_to(tail[None], (row_count,) + tail.shape)
    kept = jnp.sum(
        row_exchange(jnp.concatenate([chunks, tail], axis=1)).astype(f32), axis=0
    )
    outs = unchunked(kept, terms)
    at = chunks.shape[1]
    count = stacked.shape[0]
    bias_sum = kept[at : at + count] + kept[at + count : at + 2 * count]
    return outs, bias_sum


def count_matrix(neighbours, visit_counts, pool_size):
    row_total, fan = neighbours.shape
    low_width = 128
    high_width = pool_size // low_width
    upper_idx = neighbours // low_width
    lower_idx = neighbours % low_width
    upper_hot = jnp.where(
        upper_idx[:, :, None] == jnp.arange(high_width, dtype=jnp.int32)[None, None, :],
        visit_counts[:, :, None],
        0,
    ).astype(bf16)
    lower_hot = (
        lower_idx[:, :, None] == jnp.arange(low_width, dtype=jnp.int32)[None, None, :]
    ).astype(bf16)
    dense = jnp.einsum("vkh,vkl->vhl", upper_hot, lower_hot, preferred_element_type=f32)
    return dense.astype(bf16).reshape(row_total, pool_size)


def row_scale(whole):
    wide = whole.astype(f32)
    return lax.rsqrt(jnp.sum(wide * wide, axis=1, keepdims=True) / whole.shape[1] + eps)


def body(
    pin_feats,
    board_feats,
    node_kinds,
    neighbours,
    visit_counts,
    pull_rows,
    proj_weight,
    proj_bias,
    neigh_weight,
    neigh_bias,
    combine_weight,
    combine_bias,
    head_weight,
    head_bias,
    tail_weight,
    tail_bias,
    cotangent,
):
    row_count = lax.axis_size("rows")
    capacity = pull_rows.shape[1] // row_count
    pool_size = pull_rows.shape[1]
    local_rows, channels = pin_feats.shape
    width = neigh_weight.shape[1]
    depth = neigh_weight.shape[0]
    is_board = (node_kinds == 1)[:, None]

    board_whole = spread(board_feats)
    board_pre = product(board_whole, proj_weight) + proj_bias
    hidden = jnp.where(is_board, jax.nn.gelu(board_pre), pin_feats.astype(f32)).astype(bf16)
    requested = row_exchange(pull_rows.reshape(row_count, capacity)).reshape(-1)
    selector = (
        requested[:, None] == jnp.arange(local_rows, dtype=jnp.int32)[None, :]
    ).astype(bf16)
    counts = count_matrix(neighbours, visit_counts, pool_size)
    inv_total = 1.0 / jnp.sum(visit_counts.astype(f32), axis=1, keepdims=True)

    kept = []
    act = hidden
    act_f32 = None
    scale = jnp.ones((local_rows, 1), f32)
    for l in range(depth):
        whole = spread(act)
        if l > 0:
            scale = row_scale(whole)
            kept[-1]["scale"] = scale
        neigh_raw = product(whole, neigh_weight[l])
        neigh_pre = scale * neigh_raw + neigh_bias[l]
        shipped = jax.nn.gelu(neigh_pre).astype(bf16)
        outgoing = product(selector, shipped).astype(bf16).reshape(-1, capacity, channels)
        pooled = row_exchange(outgoing).reshape(-1, channels)
        gathered = (product(counts, pooled) * inv_total).astype(bf16)
        gathered_whole = spread(gathered)
        self_raw = product(whole, combine_weight[l, :width])
        combine_pre = (
            scale * self_raw
            + product(gathered_whole, combine_weight[l, width:])
            + combine_bias[l]
        )
        act_f32 = jax.nn.gelu(combine_pre)
        act = act_f32.astype(bf16)
        kept.append(
            dict(
                whole=whole,
                in_scale=scale,
                neigh_raw=neigh_raw,
                neigh_pre=neigh_pre,
                self_raw=self_raw,
                combine_pre=combine_pre,
                gathered_whole=gathered_whole,
                act=act_f32,
            )
        )
    last_whole = spread(act)
    scale = row_scale(last_whole)
    kept[-1]["scale"] = scale
    head_raw = product(last_whole, head_weight)
    head_pre = scale * head_raw + head_bias
    inner_act = jax.nn.gelu(head_pre).astype(bf16)
    inner_grad = col_sum(product_rt(cotangent, tail_weight))
    head_grad = act_grad(head_pre, inner_grad).astype(bf16)
    head_wide = head_grad.astype(f32)
    upstream = col_sum(product_rt(head_grad, head_weight))
    dot = lax.psum(jnp.sum(head_raw * head_wide, axis=1, keepdims=True), "cols")
    inner_whole = spread(inner_act)
    embeddings = product(inner_whole, tail_weight) + tail_bias
    tail_bias_grad = jnp.sum(cotangent.astype(f32), axis=0, keepdims=True)
    head_bias_grad = jnp.sum(head_wide, axis=0, keepdims=True)
    tail_term = product_t(inner_whole, cotangent)
    head_term = product_t(last_whole, (scale * head_wide).astype(bf16))
    tail_out, head_out = sum_rows_far([tail_term, head_term])

    neigh_outs, combine_outs = [None] * depth, [None] * depth
    neigh_biases, combine_biases = [None] * depth, [None] * depth
    for l in reversed(range(depth)):
        saved = kept[l]
        scale = saved["scale"]
        in_scale = saved["in_scale"]
        act_upstream = scale * upstream - saved["act"] * (
            scale * scale * scale * dot / width
        )
        combine_grad = act_grad(saved["combine_pre"], act_upstream).astype(bf16)
        combine_wide = combine_grad.astype(f32)
        neigh_grad = col_sum(product_rt(combine_grad, combine_weight[l, width:]))
        pool_grad = product_t(counts, (neigh_grad * inv_total).astype(bf16))
        returned = row_exchange(
            pool_grad.astype(bf16).reshape(-1, capacity, channels)
        ).reshape(-1, channels)
        moved_grad = product_t(selector, returned)
        neigh_grad_pre = act_grad(saved["neigh_pre"], moved_grad).astype(bf16)
        neigh_wide = neigh_grad_pre.astype(f32)
        upstream = col_sum(
            product_rt(combine_grad, combine_weight[l, :width])
            + product_rt(neigh_grad_pre, neigh_weight[l])
        )
        if l > 0:
            dot = lax.psum(
                jnp.sum(
                    saved["self_raw"] * combine_wide + saved["neigh_raw"] * neigh_wide,
                    axis=1,
                    keepdims=True,
                ),
                "cols",
            )
        combine_biases[l] = jnp.sum(combine_wide, axis=0, keepdims=True)
        neigh_biases[l] = jnp.sum(neigh_wide, axis=0, keepdims=True)
        self_term = product_t(saved["whole"], (in_scale * combine_wide).astype(bf16))
        gathered_term = product_t(saved["gathered_whole"], combine_grad)
        neigh_term = product_t(saved["whole"], (in_scale * neigh_wide).astype(bf16))
        combine_term = jnp.concatenate([self_term, gathered_term], axis=0)
        reduce_rows = sum_rows_far if l > 0 else sum_rows_near
        combine_outs[l], neigh_outs[l] = reduce_rows([combine_term, neigh_term])

    grad_pin = jnp.where(is_board, 0.0, upstream)
    board_grad_pre = act_grad(board_pre, jnp.where(is_board, upstream, 0.0)).astype(bf16)
    proj_bias_grad = jnp.sum(board_grad_pre.astype(f32), axis=0, keepdims=True)
    grad_board = col_sum(product_rt(board_grad_pre, proj_weight))
    proj_term = product_t(board_whole, board_grad_pre)
    (proj_out,), biases = sum_rows_last(
        [proj_term],
        neigh_biases
        + combine_biases
        + [head_bias_grad, tail_bias_grad, proj_bias_grad],
    )
    return (
        embeddings,
        grad_pin,
        grad_board,
        proj_out,
        biases[2 * depth + 2],
        jnp.stack(neigh_outs),
        biases[:depth],
        jnp.stack(combine_outs),
        biases[depth : 2 * depth],
        head_out,
        biases[2 * depth],
        tail_out,
        biases[2 * depth + 1],
    )


def solution(mesh):
    placed = (
        P("rows", "cols"),
        P("rows", "cols"),
        P("rows"),
        P("rows", None),
        P("rows", None),
        P("rows", None),
        P(None, "cols"),
        P("cols"),
        P(None, None, "cols"),
        P(None, "cols"),
        P(None, None, "cols"),
        P(None, "cols"),
        P(None, "cols"),
        P("cols"),
        P(None, "cols"),
        P("cols"),
        P("rows", "cols"),
    )
    return jax.shard_map(
        body,
        mesh=mesh,
        in_specs=placed,
        out_specs=(
            P("rows", "cols"),
            P("rows", "cols"),
            P("rows", "cols"),
            P("rows", "cols"),
            P("cols"),
            P(None, "rows", "cols"),
            P(None, "cols"),
            P(None, "rows", "cols"),
            P(None, "cols"),
            P("rows", "cols"),
            P("cols"),
            P("rows", "cols"),
            P("cols"),
        ),
        check_vma=False,
    )
```

time: 966 us -> 398 us (0.41)
  waiting for transfers between devices: 704 us -> 197 us
  matrix products: 102 us -> 51.1 us
  blocking collectives: 84.5 us -> 47.7 us
  starting transfers between devices: 23.6 us -> 52.6 us
    reduce_scatter x12 -> x2, waiting for transfers between devices: 506 us -> 61.5 us  [sum_rows_far(): lax.psum_scatter(chunked(terms), 'rows', scatter_dimension=0, tiled=True)]
    all_gather x6 -> x0, waiting for transfers between devices: 71.7 us -> none  [spread(): return lax.all_gather(shard, 'cols', axis=1, tiled=True)]
    ppermute x0 -> x43, waiting for transfers between devices: none -> 70.2 us  [swap(): return lax.ppermute(array, axis, [(i, i ^ distance) for i in range(size)])]
    unnamed x22 -> x2, waiting for transfers between devices: 64.8 us -> 0.03 us
    psum x5 -> x2, blocking collectives: 44 us -> 16.6 us  [the longest x1 9.42 us: body(): dot = lax.psum(jnp.sum(head_raw * head_wide, axis=1, keepdims=True), 'cols')]
    dot_general x19 -> x13, matrix products: 45.1 us -> 18.1 us  [product_t(): lax.dot_general(left_side, right_side, (((0,), (0,)), ((), ())), preferre...]
    ppermute x0 -> x43, starting transfers between devices: none -> 26.4 us  [swap(): return lax.ppermute(array, axis, [(i, i ^ distance) for i in range(size)])]
    dot_general x16 -> x14, matrix products: 41.8 us -> 24.4 us  [the longest x13 16.1 us: product(): return jnp.dot(left_side, right_side, preferred_element_type=f32)]
  transfers between devices with their start and end apart: 24 -> 51, of which waited for: 22 -> 23; matrix products, arithmetic and copies ran while one was open for 7% -> 14% of each run, Pallas kernels for 0% -> 0%
where the time goes in v1:
time: 398 us; the launch traced here: 397 us
  waiting for transfers between devices  197 us (49%)
  starting transfers between devices  52.6 us (13%)
  matrix products  51.1 us (13%)
  blocking collectives  47.7 us (12%)
  other arithmetic  21.9 us (6%)
  between operations  15.5 us (4%)
  local copies, waits for them, and re-layouts  11.4 us (3%)
    ppermute x43, waiting for transfers between devices, swap(): return lax.ppermute(array, axis, [(i, i ^ distance) for i in range(size)])  70.2 us
    all_to_all x6, waiting for transfers between devices, row_exchange(): lax.all_to_all(chunks, 'rows', split_axis=0, concat_axis=0, tiled=True, a...  64.9 us
    reduce_scatter x2, waiting for transfers between devices, sum_rows_far(): lax.psum_scatter(chunked(terms), 'rows', scatter_dimension=0, tiled=True)  61.5 us
    all_to_all x1, blocking collectives, row_exchange(): lax.all_to_all(chunks, 'rows', split_axis=0, concat_axis=0, tiled=True, a...  31.1 us
    ppermute x43, starting transfers between devices, swap(): return lax.ppermute(array, axis, [(i, i ^ distance) for i in range(size)])  26.4 us
    all_to_all x6, starting transfers between devices, row_exchange(): lax.all_to_all(chunks, 'rows', split_axis=0, concat_axis=0, tiled=True, a...  25.7 us
    dot_general x13, matrix products, product_t(): lax.dot_general(left_side, right_side, (((0,), (0,)), ((), ())), preferre...  18.1 us
    dot_general x13, matrix products, product(): return jnp.dot(left_side, right_side, preferred_element_type=f32)  16.1 us
  transfers between devices with their start and end apart: 51, of which 23 were waited for; matrix products, arithmetic and copies ran while one was open for 14% of the time, Pallas kernels for 0%

profile of v1, /device:TPU:0, one launch (start us, length us, event | category | flops | bytes accessed | tf_op | source)
XLA Modules:
  0.0 396.9 jit_solution(12309452045782037898)
XLA Ops:
  10.2 3.7 collective-permute-done
  20.4 6.6 %collective-permute-done.3 = bf16[512,256]{1,0:T(8,128)(2,1)S(1)} collective-permute-done((bf16[512,256]{1,0:T(8,128)(2,1)S(1)}, bf16[512,256]{1,0:T(8,128)(2,1)S(1)}, u32[]{:S(2)}, u32[]{:S(2)}) %collective-permute-start.3) | collective-permute-done | bytes 262176 | tf_op jit(solution)/shard_map/ppermute | solution.py:33
  27.1 6.0 %all-to-all-start = ((s32[8,1,256]{2,1,0:T(1,128)}), s32[8,1,256]{2,1,0:T(1,128)S(1)}, u32[]{:S(2)}, u32[]{:S(2)}) async-start(s32[8,1,256]{2,1,0:T(1,128)} %bitcast.1), calls=%async_computation | async-start | bytes 16384 | tf_op jit(solution)/shard_map/all_to_all | solution.py:72
  34.7 5.0 %all-to-all-done = s32[8,1,256]{2,1,0:T(1,128)S(1)} async-done(((s32[8,1,256]{2,1,0:T(1,128)}), s32[8,1,256]{2,1,0:T(1,128)S(1)}, u32[]{:S(2)}, u32[]{:S(2)}) %all-to-all-start) | async-done | bytes 8224 | tf_op jit(solution)/shard_map/all_to_all | solution.py:72
  46.7 8.3 %fusion.21 = bf16[512,16,128]{2,1,0:T(8,128)(2,1)} fusion(s32[512,50]{1,0:T(8,128)S(1)} %copy.60, s32[512,50]{1,0:T(8,128)} %copy.59, s32[512,50]{1,0:T(8,128)S(1)} %copy.58), kind=kOutput, calls=%fused_computation.31 | convolution fusion | flops 110411776 | bytes 2404352 | tf_op jit(solution)/shard_map/vkh,vkl->vhl/dot_general | solution.py:147
  55.0 15.8 %all-to-all-done.1 = bf16[8,256,256]{2,1,0:T(8,128)(2,1)S(1)} async-done(((bf16[8,256,256]{2,1,0:T(8,128)(2,1)}), bf16[8,256,256]{2,1,0:T(8,128)(2,1)S(1)}, u32[]{:S(2)}, u32[]{:S(2)}) %all-to-all-start.1) | async-done | bytes 1048608 | tf_op jit(solution)/shard_map/all_to_all | solution.py:72
  74.7 4.8 %collective-permute-done.6 = bf16[512,256]{1,0:T(8,128)(2,1)S(1)} collective-permute-done((bf16[512,256]{1,0:T(8,128)(2,1)S(1)}, bf16[512,256]{1,0:T(8,128)(2,1)S(1)}, u32[]{:S(2)}, u32[]{:S(2)}) %collective-permute-start.6) | collective-permute-done | bytes 262176 | tf_op jit(solution)/shard_map/ppermute | solution.py:33
  85.6 6.8 %collective-permute-done.9 = bf16[512,256]{1,0:T(8,128)(2,1)S(1)} collective-permute-done((bf16[512,256]{1,0:T(8,128)(2,1)S(1)}, bf16[512,256]{1,0:T(8,128)(2,1)S(1)}, u32[]{:S(2)}, u32[]{:S(2)}) %collective-permute-start.9) | collective-permute-done | bytes 262176 | tf_op jit(solution)/shard_map/ppermute | solution.py:33
  95.9 31.1 %all_to_all.39 = bf16[8,256,256]{2,1,0:T(8,128)(2,1)S(1)} all-to-all(bf16[8,256,256]{2,1,0:T(8,128)(2,1)S(1)} %bitcast.152), channel_id=1, replica_groups=mesh['rows'=8,'cols'=4] {'rows'}, dimensions={0} | all-to-all | bytes 2097152 | tf_op jit(solution)/shard_map/all_to_all | solution.py:72
  129.3 5.4 %collective-permute-done.12 = bf16[512,256]{1,0:T(8,128)(2,1)S(1)} collective-permute-done((bf16[512,256]{1,0:T(8,128)(2,1)S(1)}, bf16[512,256]{1,0:T(8,128)(2,1)S(1)}, u32[]{:S(2)}, u32[]{:S(2)}) %collective-permute-start.12) | collective-permute-done | bytes 262176 | tf_op jit(solution)/shard_map/ppermute | solution.py:33
  139.4 6.2 %collective-permute-done.15 = bf16[512,256]{1,0:T(8,128)(2,1)S(1)} collective-permute-done((bf16[512,256]{1,0:T(8,128)(2,1)S(1)}, bf16[512,256]{1,0:T(8,128)(2,1)S(1)}, u32[]{:S(2)}, u32[]{:S(2)}) %collective-permute-start.15) | collective-permute-done | bytes 262176 | tf_op jit(solution)/shard_map/ppermute | solution.py:33
  148.3 6.3 %collective-permute-done.23 = bf16[512,256]{1,0:T(8,128)(2,1)S(1)} collective-permute-done((bf16[512,256]{1,0:T(8,128)(2,1)S(1)}, bf16[512,256]{1,0:T(8,128)(2,1)S(1)}, u32[]{:S(2)}, u32[]{:S(2)}) %collective-permute-start.23) | collective-permute-done | bytes 262176 | tf_op jit(solution)/shard_map/ppermute | solution.py:33
  160.2 9.4 %psum.14 = f32[512,1]{0,1:T(1,128)S(1)} all-reduce(f32[512,1]{0,1:T(1,128)S(1)} %bitcast.169), channel_id=1, replica_groups=mesh['rows'=8,'cols'=4] {'cols'}, use_global_device_ids=true, to_apply=%region_4.5 | all-reduce | flops 512 | bytes 4096 | tf_op jit(solution)/shard_map/psum | solution.py:239
  174.3 7.8 %collective-permute-done.29 = bf16[512,256]{1,0:T(8,128)(2,1)S(1)} collective-permute-done((bf16[512,256]{1,0:T(8,128)(2,1)S(1)}, bf16[512,256]{1,0:T(8,128)(2,1)S(1)}, u32[]{:S(2)}, u32[]{:S(2)}) %collective-permute-start.29) | collective-permute-done | bytes 262176 | tf_op jit(solution)/shard_map/ppermute | solution.py:33
  184.5 4.4 %all-to-all-start.3 = ((bf16[8,256,256]{2,1,0:T(8,128)(2,1)}), bf16[8,256,256]{2,1,0:T(8,128)(2,1)S(1)}, u32[]{:S(2)}, u32[]{:S(2)}) async-start(bf16[8,256,256]{2,1,0:T(8,128)(2,1)} %bitcast.19), calls=%async_computation.3 | async-start | bytes 2097152 | tf_op jit(solution)/shard_map/all_to_all | solution.py:72
  191.2 23.1 %all-to-all-done.3 = bf16[8,256,256]{2,1,0:T(8,128)(2,1)S(1)} async-done(((bf16[8,256,256]{2,1,0:T(8,128)(2,1)}), bf16[8,256,256]{2,1,0:T(8,128)(2,1)S(1)}, u32[]{:S(2)}, u32[]{:S(2)}) %all-to-all-start.3) | async-done | bytes 1048608 | tf_op jit(solution)/shard_map/all_to_all | solution.py:72
  223.1 7.2 %psum.15 = f32[512,1]{0,1:T(1,128)S(1)} all-reduce(f32[512,1]{0,1:T(1,128)S(1)} %bitcast.168), channel_id=1, replica_groups=mesh['rows'=8,'cols'=4] {'cols'}, use_global_device_ids=true, to_apply=%region_6.7 | all-reduce | flops 512 | bytes 4096 | tf_op jit(solution)/shard_map/psum | solution.py:272
  239.3 6.7 %collective-permute-done.35 = bf16[512,256]{1,0:T(8,128)(2,1)S(1)} collective-permute-done((bf16[512,256]{1,0:T(8,128)(2,1)S(1)}, bf16[512,256]{1,0:T(8,128)(2,1)S(1)}, u32[]{:S(2)}, u32[]{:S(2)}) %collective-permute-start.35) | collective-permute-done | bytes 262176 | tf_op jit(solution)/shard_map/ppermute | solution.py:33
  246.1 3.9 convolution_convert_fusion
  249.9 4.4 %all-to-all-start.4 = ((bf16[8,256,256]{2,1,0:T(8,128)(2,1)}), bf16[8,256,256]{2,1,0:T(8,128)(2,1)}, u32[]{:S(2)}, u32[]{:S(2)}) async-start(bf16[8,256,256]{2,1,0:T(8,128)(2,1)} %bitcast.24), calls=%async_computation.4 | async-start | bytes 2097152 | tf_op jit(solution)/shard_map/all_to_all | solution.py:72
  261.8 21.1 %all-to-all-done.4 = bf16[8,256,256]{2,1,0:T(8,128)(2,1)} async-done(((bf16[8,256,256]{2,1,0:T(8,128)(2,1)}), bf16[8,256,256]{2,1,0:T(8,128)(2,1)}, u32[]{:S(2)}, u32[]{:S(2)}) %all-to-all-start.4) | async-done | bytes 1048608 | tf_op jit(solution)/shard_map/all_to_all | solution.py:72
  292.9 4.0 %collective-permute-done.38 = bf16[512,256]{1,0:T(8,128)(2,1)S(1)} collective-permute-done((bf16[512,256]{1,0:T(8,128)(2,1)S(1)}, bf16[512,256]{1,0:T(8,128)(2,1)S(1)}, u32[]{:S(2)}, u32[]{:S(2)}) %collective-permute-start.38) | collective-permute-done | bytes 262176 | tf_op jit(solution)/shard_map/ppermute | solution.py:33
  310.7 5.1 %collective-permute-done.42 = bf16[4,384,256]{2,1,0:T(8,128)(2,1)} collective-permute-done((bf16[4,384,256]{2,1,0:T(8,128)(2,1)}, bf16[4,384,256]{2,1,0:T(8,128)(2,1)}, u32[]{:S(2)}, u32[]{:S(2)}) %collective-permute-start.42) | collective-permute-done | bytes 786464 | tf_op jit(solution)/shard_map/ppermute | solution.py:33
  322.4 61.5 %reduce-scatter.3.cloned.1.call-done = bf16[1,384,256]{2,1,0:T(8,128)(2,1)} async-done(((bf16[8,384,256]{2,1,0:T(8,128)(2,1)}), bf16[1,384,256]{2,1,0:T(8,128)(2,1)}) %reduce-scatter.3.cloned.1.call-update) | async-done | bytes 196624 | tf_op jit(solution)/shard_map/reduce_scatter | solution.py:95
  (357 shorter events, 116.8 us)
Async XLA Ops:
  18.7 8.4 %collective-permute-start.3 = (bf16[512,256]{1,0:T(8,128)(2,1)S(1)}, bf16[512,256]{1,0:T(8,128)(2,1)S(1)}, u32[]{:S(2)}, u32[]{:S(2)}) collective-permute-start(bf16[512,256]{1,0:T(8,128)(2,1)S(1)} %get-tuple-element.85), channel_id=1, source_target_pairs={{0,2},{1,3},{2,0},{3,1},{4,6},{5,7},{6,4},{7,5},{8,10},{9,11},{10,... | collective-permute-start | bytes 786440 | tf_op jit(solution)/shard_map/ppermute | solution.py:33
  20.4 12.7 %collective-permute-start.5 = (bf16[512,256]{1,0:T(8,128)(2,1)S(1)}, bf16[512,256]{1,0:T(8,128)(2,1)S(1)}, u32[]{:S(2)}, u32[]{:S(2)}) collective-permute-start(bf16[512,256]{1,0:T(8,128)(2,1)S(1)} %get-tuple-element.85), channel_id=1, source_target_pairs={{0,1},{1,0},{2,3},{3,2},{4,5},{5,4},{6,7},{7,6},{8,9},{9,8},{10,11... | collective-permute-start | bytes 786440 | tf_op jit(solution)/shard_map/ppermute | solution.py:33
  27.1 12.6 %all-to-all-start = ((s32[8,1,256]{2,1,0:T(1,128)}), s32[8,1,256]{2,1,0:T(1,128)S(1)}, u32[]{:S(2)}, u32[]{:S(2)}) async-start(s32[8,1,256]{2,1,0:T(1,128)} %bitcast.1), calls=%async_computation | async-start | bytes 16384 | tf_op jit(solution)/shard_map/all_to_all | solution.py:72
  41.7 29.1 %all-to-all-start.1 = ((bf16[8,256,256]{2,1,0:T(8,128)(2,1)}), bf16[8,256,256]{2,1,0:T(8,128)(2,1)S(1)}, u32[]{:S(2)}, u32[]{:S(2)}) async-start(bf16[8,256,256]{2,1,0:T(8,128)(2,1)} %bitcast.150), calls=%async_computation.1 | async-start | bytes 2097152 | tf_op jit(solution)/shard_map/all_to_all | solution.py:72
  84.1 8.3 %collective-permute-start.9 = (bf16[512,256]{1,0:T(8,128)(2,1)S(1)}, bf16[512,256]{1,0:T(8,128)(2,1)S(1)}, u32[]{:S(2)}, u32[]{:S(2)}) collective-permute-start(bf16[512,256]{1,0:T(8,128)(2,1)S(1)} %get-tuple-element.87), channel_id=1, source_target_pairs={{0,2},{1,3},{2,0},{3,1},{4,6},{5,7},{6,4},{7,5},{8,10},{9,11},{10,... | collective-permute-start | bytes 786440 | tf_op jit(solution)/shard_map/ppermute | solution.py:33
  137.2 8.3 %collective-permute-start.15 = (bf16[512,256]{1,0:T(8,128)(2,1)S(1)}, bf16[512,256]{1,0:T(8,128)(2,1)S(1)}, u32[]{:S(2)}, u32[]{:S(2)}) collective-permute-start(bf16[512,256]{1,0:T(8,128)(2,1)S(1)} %get-tuple-element.89), channel_id=1, source_target_pairs={{0,2},{1,3},{2,0},{3,1},{4,6},{5,7},{6,4},{7,5},{8,10},{9,11},{10,... | collective-permute-start | bytes 786440 | tf_op jit(solution)/shard_map/ppermute | solution.py:33
  138.9 9.0 %collective-permute-start.17 = (bf16[512,256]{1,0:T(8,128)(2,1)S(1)}, bf16[512,256]{1,0:T(8,128)(2,1)S(1)}, u32[]{:S(2)}, u32[]{:S(2)}) collective-permute-start(bf16[512,256]{1,0:T(8,128)(2,1)S(1)} %get-tuple-element.89), channel_id=1, source_target_pairs={{0,1},{1,0},{2,3},{3,2},{4,5},{5,4},{6,7},{7,6},{8,9},{9,8},{10,11... | collective-permute-start | bytes 786440 | tf_op jit(solution)/shard_map/ppermute | solution.py:33
  156.9 12.7 %collective-permute-start.24 = (bf16[512,256]{1,0:T(8,128)(2,1)S(1)}, bf16[512,256]{1,0:T(8,128)(2,1)S(1)}, u32[]{:S(2)}, u32[]{:S(2)}) collective-permute-start(bf16[512,256]{1,0:T(8,128)(2,1)S(1)} %get-tuple-element.37), channel_id=1, source_target_pairs={{0,1},{1,0},{2,3},{3,2},{4,5},{5,4},{6,7},{7,6},{8,9},{9,8},{10,11... | collective-permute-start | bytes 786440 | tf_op jit(solution)/shard_map/ppermute | solution.py:33
  158.6 11.0 %collective-permute-start.26 = (bf16[512,256]{1,0:T(8,128)(2,1)S(1)}, bf16[512,256]{1,0:T(8,128)(2,1)S(1)}, u32[]{:S(2)}, u32[]{:S(2)}) collective-permute-start(bf16[512,256]{1,0:T(8,128)(2,1)S(1)} %add_convert_fusion.6), channel_id=1, source_target_pairs={{0,2},{1,3},{2,0},{3,1},{4,6},{5,7},{6,4},{7,5},{8,10},{9,11},{10,... | collective-permute-start | bytes 786440 | tf_op jit(solution)/shard_map/ppermute | solution.py:33
  173.8 8.4 %collective-permute-start.29 = (bf16[512,256]{1,0:T(8,128)(2,1)S(1)}, bf16[512,256]{1,0:T(8,128)(2,1)S(1)}, u32[]{:S(2)}, u32[]{:S(2)}) collective-permute-start(bf16[512,256]{1,0:T(8,128)(2,1)S(1)} %add_convert_fusion.5), channel_id=1, source_target_pairs={{0,2},{1,3},{2,0},{3,1},{4,6},{5,7},{6,4},{7,5},{8,10},{9,11},{10,... | collective-permute-start | bytes 786440 | tf_op jit(solution)/shard_map/ppermute | solution.py:33
  184.5 29.9 %all-to-all-start.3 = ((bf16[8,256,256]{2,1,0:T(8,128)(2,1)}), bf16[8,256,256]{2,1,0:T(8,128)(2,1)S(1)}, u32[]{:S(2)}, u32[]{:S(2)}) async-start(bf16[8,256,256]{2,1,0:T(8,128)(2,1)} %bitcast.19), calls=%async_computation.3 | async-start | bytes 2097152 | tf_op jit(solution)/shard_map/all_to_all | solution.py:72
  188.9 118.7 %reduce-scatter.5.cloned.1.call-start = ((), (), s32[]{:S(2)}) async-start(), calls=%async_computation.10 | async-start | bytes 1179648 | tf_op jit(solution)/shard_map/reduce_scatter | solution.py:95
  189.2 29.8 %collective-permute-start.18 = (bf16[512,256]{1,0:T(8,128)(2,1)}, bf16[512,256]{1,0:T(8,128)(2,1)}, u32[]{:S(2)}, u32[]{:S(2)}) collective-permute-start(bf16[512,256]{1,0:T(8,128)(2,1)} %get-tuple-element.65), channel_id=1, source_target_pairs={{0,2},{1,3},{2,0},{3,1},{4,6},{5,7},{6,4},{7,5},{8,10},{9,11},{10,... | collective-permute-start | bytes 786440 | tf_op jit(solution)/shard_map/ppermute | solution.py:33
  219.7 10.6 %collective-permute-start.30 = (bf16[512,256]{1,0:T(8,128)(2,1)S(1)}, bf16[512,256]{1,0:T(8,128)(2,1)S(1)}, u32[]{:S(2)}, u32[]{:S(2)}) collective-permute-start(bf16[512,256]{1,0:T(8,128)(2,1)S(1)} %get-tuple-element.33), channel_id=1, source_target_pairs={{0,1},{1,0},{2,3},{3,2},{4,5},{5,4},{6,7},{7,6},{8,9},{9,8},{10,11... | collective-permute-start | bytes 786440 | tf_op jit(solution)/shard_map/ppermute | solution.py:33
  220.4 10.0 %collective-permute-start.32 = (bf16[512,256]{1,0:T(8,128)(2,1)S(1)}, bf16[512,256]{1,0:T(8,128)(2,1)S(1)}, u32[]{:S(2)}, u32[]{:S(2)}) collective-permute-start(bf16[512,256]{1,0:T(8,128)(2,1)S(1)} %add_convert_fusion.4), channel_id=1, source_target_pairs={{0,2},{1,3},{2,0},{3,1},{4,6},{5,7},{6,4},{7,5},{8,10},{9,11},{10,... | collective-permute-start | bytes 786440 | tf_op jit(solution)/shard_map/ppermute | solution.py:33
  237.7 8.3 %collective-permute-start.35 = (bf16[512,256]{1,0:T(8,128)(2,1)S(1)}, bf16[512,256]{1,0:T(8,128)(2,1)S(1)}, u32[]{:S(2)}, u32[]{:S(2)}) collective-permute-start(bf16[512,256]{1,0:T(8,128)(2,1)S(1)} %add_convert_fusion.3), channel_id=1, source_target_pairs={{0,2},{1,3},{2,0},{3,1},{4,6},{5,7},{6,4},{7,5},{8,10},{9,11},{10,... | collective-permute-start | bytes 786440 | tf_op jit(solution)/shard_map/ppermute | solution.py:33
  249.9 33.0 %all-to-all-start.4 = ((bf16[8,256,256]{2,1,0:T(8,128)(2,1)}), bf16[8,256,256]{2,1,0:T(8,128)(2,1)}, u32[]{:S(2)}, u32[]{:S(2)}) async-start(bf16[8,256,256]{2,1,0:T(8,128)(2,1)} %bitcast.24), calls=%async_computation.4 | async-start | bytes 2097152 | tf_op jit(solution)/shard_map/all_to_all | solution.py:72
  254.3 129.5 %reduce-scatter.3.cloned.1.call-start = ((), (), s32[]{:S(2)}) async-start(), calls=%async_computation.9 | async-start | bytes 1769472 | tf_op jit(solution)/shard_map/reduce_scatter | solution.py:95
  288.5 8.4 %collective-permute-start.38 = (bf16[512,256]{1,0:T(8,128)(2,1)S(1)}, bf16[512,256]{1,0:T(8,128)(2,1)S(1)}, u32[]{:S(2)}, u32[]{:S(2)}) collective-permute-start(bf16[512,256]{1,0:T(8,128)(2,1)S(1)} %get-tuple-element.24), channel_id=1, source_target_pairs={{0,2},{1,3},{2,0},{3,1},{4,6},{5,7},{6,4},{7,5},{8,10},{9,11},{10,... | collective-permute-start | bytes 786440 | tf_op jit(solution)/shard_map/ppermute | solution.py:33
  291.7 24.1 %collective-permute-start.42 = (bf16[4,384,256]{2,1,0:T(8,128)(2,1)}, bf16[4,384,256]{2,1,0:T(8,128)(2,1)}, u32[]{:S(2)}, u32[]{:S(2)}) collective-permute-start(bf16[4,384,256]{2,1,0:T(8,128)(2,1)} %fusion.41), channel_id=1, source_target_pairs={{0,4},{4,0},{8,12},{12,8},{16,20},{20,16},{24,28},{28,24},{1,5},{5... | collective-permute-start | bytes 2359304 | tf_op jit(solution)/shard_map/ppermute | solution.py:33
  300.8 17.3 %all-to-all-start.5 = ((bf16[8,80,256]{2,1,0:T(8,128)(2,1)}), bf16[8,80,256]{2,1,0:T(8,128)(2,1)S(1)}, u32[]{:S(2)}, u32[]{:S(2)}) async-start(bf16[8,80,256]{2,1,0:T(8,128)(2,1)} %pad_maximum_fusion.13), calls=%async_computation.5 | async-start | bytes 655360 | tf_op jit(solution)/shard_map/all_to_all | solution.py:72
  308.5 77.2 %collective-permute-start.39 = (bf16[512,128]{1,0:T(8,128)(2,1)}, bf16[512,128]{1,0:T(8,128)(2,1)S(1)}, u32[]{:S(2)}, u32[]{:S(2)}) collective-permute-start(bf16[512,128]{1,0:T(8,128)(2,1)} %get-tuple-element.66), channel_id=1, source_target_pairs={{0,1},{1,0},{2,3},{3,2},{4,5},{5,4},{6,7},{7,6},{8,9},{9,8},{10,11... | collective-permute-start | bytes 393224 | tf_op jit(solution)/shard_map/ppermute | solution.py:33
  309.1 76.5 %collective-permute-start.41 = (bf16[512,128]{1,0:T(8,128)(2,1)S(1)}, bf16[512,128]{1,0:T(8,128)(2,1)S(1)}, u32[]{:S(2)}, u32[]{:S(2)}) collective-permute-start(bf16[512,128]{1,0:T(8,128)(2,1)S(1)} %add_convert_fusion.8), channel_id=1, source_target_pairs={{0,2},{1,3},{2,0},{3,1},{4,6},{5,7},{6,4},{7,5},{8,10},{9,11},{10,... | collective-permute-start | bytes 393224 | tf_op jit(solution)/shard_map/ppermute | solution.py:33
  318.2 70.2 %all-to-all-start.6 = ((bf16[4,384,256]{2,1,0:T(8,128)(2,1)}), bf16[4,384,256]{2,1,0:T(8,128)(2,1)S(1)}, u32[]{:S(2)}, u32[]{:S(2)}) async-start(bf16[4,384,256]{2,1,0:T(8,128)(2,1)} %fusion.22), calls=%async_computation.6 | async-start | bytes 1572864 | tf_op jit(solution)/shard_map/all_to_all | solution.py:72
  (112 other events, 814.3 us)
Sparse Core Ops, SparseCore 0:
  236.2 70.5 reduce-scatter.4
  310.6 73.2 reduce-scatter.2

commit v2 on v1

--- a/solution.py
+++ b/solution.py
@@ -58,14 +58,34 @@
     return jnp.concatenate(natural(gather_cols(shard)), axis=1)
 
 
-def col_sum(partial_term):
+def start_col_sum(partial_term):
     size = lax.axis_size("cols")
     blocks = natural(jnp.split(partial_term.astype(bf16), size, axis=1))
-    total = blocks[0].astype(f32) + swap(blocks[1], "cols", 1).astype(f32)
+    near = (blocks[0], swap(blocks[1], "cols", 1))
+    pairs = []
     for far in range(2, size, 2):
         pair = blocks[far].astype(f32) + swap(blocks[far + 1], "cols", 1).astype(f32)
-        total = total + swap(pair.astype(bf16), "cols", far).astype(f32)
+        pairs.append(pair.astype(bf16))
+    return near, pairs
+
+
+def end_col_sum(near, pairs):
+    total = near[0].astype(f32) + near[1].astype(f32)
+    for far, pair in enumerate(pairs):
+        total = total + swap(pair, "cols", 2 * far + 2).astype(f32)
     return total
+
+
+def col_sum(partial_term):
+    return end_col_sum(*start_col_sum(partial_term))
+
+
+def vector_sum(values):
+    step = 1
+    while step < lax.axis_size("cols"):
+        values = values + swap(values, "cols", step)
+        step *= 2
+    return values
 
 
 def row_exchange(chunks, groups=None):
@@ -91,22 +111,24 @@
     return outs
 
 
-def sum_rows_far(terms):
-    kept = lax.psum_scatter(chunked(terms), "rows", scatter_dimension=0, tiled=True)
-    return unchunked(kept[0].astype(f32), terms)
-
-
-def sum_rows_near(terms):
-    row_count = lax.axis_size("rows")
-    chunks = chunked(terms)
-    chunks = chunks.reshape((row_count // 2, 2) + chunks.shape[1:])
-    odd = (lax.axis_index("rows") & 1) != 0
-    mine = jnp.where(odd, chunks[:, 1], chunks[:, 0])
-    other = jnp.where(odd, chunks[:, 0], chunks[:, 1])
-    pair = (mine.astype(f32) + swap(other, "rows", 1).astype(f32)).astype(bf16)
-    groups = [list(range(start, row_count, 2)) for start in range(2)]
-    kept = jnp.sum(row_exchange(pair, groups).astype(f32), axis=0)
-    return unchunked(kept, terms)
+def halve(chunks, distance):
+    chunks = chunks.reshape((chunks.shape[0] // 2, 2) + chunks.shape[1:])
+    bit = jnp.where((lax.axis_index("rows") & distance) != 0, 1, 0)
+    keep = lax.dynamic_index_in_dim(chunks, bit, 1, keepdims=False)
+    send = lax.dynamic_index_in_dim(chunks, 1 - bit, 1, keepdims=False)
+    return (keep.astype(f32) + swap(send, "rows", distance).astype(f32)).astype(bf16)
+
+
+def finish(chunks, terms):
+    distance = lax.axis_size("rows") // chunks.shape[0]
+    while chunks.shape[0] > 1:
+        chunks = halve(chunks, distance)
+        distance *= 2
+    return unchunked(chunks[0].astype(f32), terms)
+
+
+def tie(*arrays):
+    return lax.optimization_barrier(arrays)
 
 
 def sum_rows_last(terms, biases):
@@ -187,12 +209,13 @@
     selector = (
         requested[:, None] == jnp.arange(local_rows, dtype=jnp.int32)[None, :]
     ).astype(bf16)
-    counts = count_matrix(neighbours, visit_counts, pool_size)
     inv_total = 1.0 / jnp.sum(visit_counts.astype(f32), axis=1, keepdims=True)
+
+    hidden, selector, inv_total = tie(hidden, selector, inv_total)
+    inner_grad = None
 
     kept = []
     act = hidden
-    act_f32 = None
     scale = jnp.ones((local_rows, 1), f32)
     for l in range(depth):
         whole = spread(act)
@@ -204,9 +227,16 @@
         shipped = jax.nn.gelu(neigh_pre).astype(bf16)
         outgoing = product(selector, shipped).astype(bf16).reshape(-1, capacity, channels)
         pooled = row_exchange(outgoing).reshape(-1, channels)
+        whole_late, cotangent_late, _ = tie(whole, cotangent, outgoing)
+        self_raw = product(whole_late, combine_weight[l, :width])
+        if l == 0:
+            inner_grad = col_sum(product_rt(cotangent_late, tail_weight))
+            counts = count_matrix(neighbours, visit_counts, pool_size)
+            counts, inner_grad, pooled, self_raw = tie(counts, inner_grad, pooled, self_raw)
+        else:
+            pooled, self_raw = tie(pooled, self_raw)
         gathered = (product(counts, pooled) * inv_total).astype(bf16)
         gathered_whole = spread(gathered)
-        self_raw = product(whole, combine_weight[l, :width])
         combine_pre = (
             scale * self_raw
             + product(gathered_whole, combine_weight[l, width:])
@@ -232,21 +262,20 @@
     head_raw = product(last_whole, head_weight)
     head_pre = scale * head_raw + head_bias
     inner_act = jax.nn.gelu(head_pre).astype(bf16)
-    inner_grad = col_sum(product_rt(cotangent, tail_weight))
     head_grad = act_grad(head_pre, inner_grad).astype(bf16)
     head_wide = head_grad.astype(f32)
-    upstream = col_sum(product_rt(head_grad, head_weight))
-    dot = lax.psum(jnp.sum(head_raw * head_wide, axis=1, keepdims=True), "cols")
-    inner_whole = spread(inner_act)
-    embeddings = product(inner_whole, tail_weight) + tail_bias
-    tail_bias_grad = jnp.sum(cotangent.astype(f32), axis=0, keepdims=True)
-    head_bias_grad = jnp.sum(head_wide, axis=0, keepdims=True)
-    tail_term = product_t(inner_whole, cotangent)
-    head_term = product_t(last_whole, (scale * head_wide).astype(bf16))
-    tail_out, head_out = sum_rows_far([tail_term, head_term])
+    near, pairs = start_col_sum(product_rt(head_grad, head_weight))
+    dot = vector_sum(jnp.sum(head_raw * head_wide, axis=1))
+    dot = dot[:, None]
+    head_late, last_late, _ = tie(head_wide, last_whole, pairs[0])
+    head_term = product_t(last_late, (scale * head_late).astype(bf16))
+    head_bias_grad = jnp.sum(head_late, axis=0, keepdims=True)
+    head_sum = halve(chunked([head_term]), 1)
+    upstream = end_col_sum(near, pairs)
 
     neigh_outs, combine_outs = [None] * depth, [None] * depth
     neigh_biases, combine_biases = [None] * depth, [None] * depth
+    early = [head_sum]
     for l in reversed(range(depth)):
         saved = kept[l]
         scale = saved["scale"]
@@ -255,36 +284,63 @@
             scale * scale * scale * dot / width
         )
         combine_grad = act_grad(saved["combine_pre"], act_upstream).astype(bf16)
+        near, pairs = start_col_sum(product_rt(combine_grad, combine_weight[l, width:]))
+        if l < depth - 1:
+            first, second, _ = tie(early[0], early[1], pairs[0])
+            early = [halve(first, 2), halve(second, 4)]
+        neigh_grad = end_col_sum(near, pairs)
+        pool_grad = product_t(counts, (neigh_grad * inv_total).astype(bf16))
+        pool_grad = pool_grad.astype(bf16).reshape(-1, capacity, channels)
+        pool_grad, *early = tie(pool_grad, *early)
+        returned = row_exchange(pool_grad).reshape(-1, channels)
+
+        combine_grad, inner_act, _ = tie(combine_grad, inner_act, pool_grad)
         combine_wide = combine_grad.astype(f32)
-        neigh_grad = col_sum(product_rt(combine_grad, combine_weight[l, width:]))
-        pool_grad = product_t(counts, (neigh_grad * inv_total).astype(bf16))
-        returned = row_exchange(
-            pool_grad.astype(bf16).reshape(-1, capacity, channels)
-        ).reshape(-1, channels)
+        self_grad = product_rt(combine_grad, combine_weight[l, :width])
+        combine_biases[l] = jnp.sum(combine_wide, axis=0, keepdims=True)
+        self_term = product_t(saved["whole"], (in_scale * combine_wide).astype(bf16))
+        gathered_term = product_t(saved["gathered_whole"], combine_grad)
+        combine_term = jnp.concatenate([self_term, gathered_term], axis=0)
+        combine_sum = halve(chunked([combine_term]), 1)
+        if l == depth - 1:
+            inner_whole = spread(inner_act)
+            embeddings = product(inner_whole, tail_weight) + tail_bias
+            tail_bias_grad = jnp.sum(cotangent.astype(f32), axis=0, keepdims=True)
+            tail_term = product_t(inner_whole, cotangent)
+            (head_out,) = finish(early[0], [head_term])
+            returned, combine_sum, self_grad, tail_term, head_out = tie(
+                returned, combine_sum, self_grad, tail_term, head_out
+            )
+        else:
+            returned, combine_sum, self_grad = tie(returned, combine_sum, self_grad)
+
         moved_grad = product_t(selector, returned)
         neigh_grad_pre = act_grad(saved["neigh_pre"], moved_grad).astype(bf16)
         neigh_wide = neigh_grad_pre.astype(f32)
-        upstream = col_sum(
-            product_rt(combine_grad, combine_weight[l, :width])
-            + product_rt(neigh_grad_pre, neigh_weight[l])
-        )
+        near, pairs = start_col_sum(self_grad + product_rt(neigh_grad_pre, neigh_weight[l]))
         if l > 0:
-            dot = lax.psum(
+            dot = vector_sum(
                 jnp.sum(
                     saved["self_raw"] * combine_wide + saved["neigh_raw"] * neigh_wide,
                     axis=1,
-                    keepdims=True,
-                ),
-                "cols",
+                )
             )
-        combine_biases[l] = jnp.sum(combine_wide, axis=0, keepdims=True)
-        neigh_biases[l] = jnp.sum(neigh_wide, axis=0, keepdims=True)
-        self_term = product_t(saved["whole"], (in_scale * combine_wide).astype(bf16))
-        gathered_term = product_t(saved["gathered_whole"], combine_grad)
-        neigh_term = product_t(saved["whole"], (in_scale * neigh_wide).astype(bf16))
-        combine_term = jnp.concatenate([self_term, gathered_term], axis=0)
-        reduce_rows = sum_rows_far if l > 0 else sum_rows_near
-        combine_outs[l], neigh_outs[l] = reduce_rows([combine_term, neigh_term])
+            dot = dot[:, None]
+        neigh_late, combine_sum, _ = tie(neigh_wide, combine_sum, pairs[0])
+        neigh_biases[l] = jnp.sum(neigh_late, axis=0, keepdims=True)
+        neigh_term = product_t(saved["whole"], (in_scale * neigh_late).astype(bf16))
+        if l == depth - 1:
+            terms = [tail_term, neigh_term]
+            terms_sum = halve(chunked(terms), 1)
+            early = [terms_sum, halve(combine_sum, 2)]
+            upstream, *early = tie(end_col_sum(near, pairs), *early)
+            last_combine = combine_term
+        else:
+            terms_sum = halve(chunked([neigh_term]), 1)
+            combine_sum = halve(combine_sum, 2)
+            upstream, terms_sum, combine_sum = tie(
+                end_col_sum(near, pairs), terms_sum, combine_sum
+            )
 
     grad_pin = jnp.where(is_board, 0.0, upstream)
     board_grad_pre = act_grad(board_pre, jnp.where(is_board, upstream, 0.0)).astype(bf16)
@@ -297,6 +353,10 @@
         + combine_biases
         + [head_bias_grad, tail_bias_grad, proj_bias_grad],
     )
+    tail_out, neigh_outs[1] = finish(early[0], [tail_term, neigh_term])
+    (combine_outs[1],) = finish(early[1], [last_combine])
+    (combine_outs[0],) = finish(combine_sum, [combine_term])
+    (neigh_outs[0],) = finish(terms_sum, [neigh_term])
     return (
         embeddings,
         grad_pin,

time: 398 us -> 339 us (0.85)
  blocking collectives: 47.7 us -> 0 us
  waiting for transfers between devices: 197 us -> 171 us
  starting transfers between devices: 52.6 us -> 73.1 us
  between operations: 15.5 us -> 2.39 us
  other arithmetic: 21.9 us -> 29 us
    ppermute x43 -> x61, waiting for transfers between devices: 70.2 us -> 133 us  [swap(): return lax.ppermute(array, axis, [(i, i ^ distance) for i in range(size)])]
    reduce_scatter x2 -> x0, waiting for transfers between devices: 61.5 us -> none  [sum_rows_far(): lax.psum_scatter(chunked(terms), 'rows', scatter_dimension=0, tiled=True)]
    all_to_all x1 -> x0, blocking collectives: 31.1 us -> none  [row_exchange(): lax.all_to_all(chunks, 'rows', split_axis=0, concat_axis=0, tiled=True, a...]
    all_to_all x6, waiting for transfers between devices: 64.9 us -> 37.5 us  [row_exchange(): lax.all_to_all(chunks, 'rows', split_axis=0, concat_axis=0, tiled=True, a...]
    ppermute x43 -> x61, starting transfers between devices: 26.4 us -> 45.1 us  [swap(): return lax.ppermute(array, axis, [(i, i ^ distance) for i in range(size)])]
    psum x2 -> x0, blocking collectives: 16.6 us -> none  [the longest x1 9.42 us: body(): dot = lax.psum(jnp.sum(head_raw * head_wide, axis=1, keepdims=True), 'cols')]
    convert_element_type x9 -> x25, other arithmetic: 5.41 us -> 11.5 us  [the longest x12 5.6 us: halve(): (keep.astype(f32) + swap(send, 'rows', distance).astype(f32)).astype(bf16)]
  transfers between devices with their start and end apart: 51 -> 67, of which waited for: 23 -> 36; matrix products, arithmetic and copies ran while one was open for 14% -> 13% of each run, Pallas kernels for 0% -> 0%
where the time goes in v2:
time: 339 us; the launch traced here: 338 us
  waiting for transfers between devices  171 us (50%)
  starting transfers between devices  73.1 us (22%)
  matrix products  50.8 us (15%)
  other arithmetic  29 us (9%)
  local copies, waits for them, and re-layouts  11.8 us (3%)
    ppermute x61, waiting for transfers between devices, swap(): return lax.ppermute(array, axis, [(i, i ^ distance) for i in range(size)])  133 us
    ppermute x61, starting transfers between devices, swap(): return lax.ppermute(array, axis, [(i, i ^ distance) for i in range(size)])  45.1 us
    all_to_all x6, waiting for transfers between devices, row_exchange(): lax.all_to_all(chunks, 'rows', split_axis=0, concat_axis=0, tiled=True, a...  37.5 us
    all_to_all x6, starting transfers between devices, row_exchange(): lax.all_to_all(chunks, 'rows', split_axis=0, concat_axis=0, tiled=True, a...  28.1 us
    dot_general x13, matrix products, product_t(): lax.dot_general(left_side, right_side, (((0,), (0,)), ((), ())), preferre...  18.1 us
    dot_general x13, matrix products, product(): return jnp.dot(left_side, right_side, preferred_element_type=f32)  17.6 us
    dot_general x9, matrix products, product_rt(): lax.dot_general(left_side, right_side, (((1,), (1,)), ((), ())), preferre...  8.24 us
    dot_general x1, matrix products, count_matrix(): jnp.einsum('vkh,vkl->vhl', upper_hot, lower_hot, preferred_element_type=f32)  6.86 us
  transfers between devices with their start and end apart: 67, of which 36 were waited for; matrix products, arithmetic and copies ran while one was open for 13% of the time, Pallas kernels for 0%

profile of v2, /device:TPU:0, one launch (start us, length us, event | category | flops | bytes accessed | tf_op | source)
XLA Modules:
  0.0 338.1 jit_solution(8489696328102988749)
XLA Ops:
  3.7 5.8 %all-to-all-start = ((s32[8,1,256]{2,1,0:T(1,128)}), s32[8,1,256]{2,1,0:T(1,128)S(1)}, u32[]{:S(2)}, u32[]{:S(2)}) async-start(s32[8,1,256]{2,1,0:T(1,128)} %bitcast.220), calls=%async_computation | async-start | bytes 16384 | tf_op jit(solution)/shard_map/all_to_all | solution.py:92
  11.5 4.6 %all-to-all-done = s32[8,1,256]{2,1,0:T(1,128)S(1)} async-done(((s32[8,1,256]{2,1,0:T(1,128)}), s32[8,1,256]{2,1,0:T(1,128)S(1)}, u32[]{:S(2)}, u32[]{:S(2)}) %all-to-all-start) | async-done | bytes 8224 | tf_op jit(solution)/shard_map/all_to_all | solution.py:92
  18.5 6.8 %collective-permute-done.3 = bf16[512,256]{1,0:T(8,128)(2,1)S(1)} collective-permute-done((bf16[512,256]{1,0:T(8,128)(2,1)S(1)}, bf16[512,256]{1,0:T(8,128)(2,1)S(1)}, u32[]{:S(2)}, u32[]{:S(2)}) %collective-permute-start.3) | collective-permute-done | bytes 262176 | tf_op jit(solution)/shard_map/ppermute | solution.py:33
  35.6 6.9 %fusion.6 = bf16[512,16,128]{2,1,0:T(8,128)(2,1)S(1)} fusion(s32[512,50]{1,0:T(8,128)S(1)} %copy.66, s32[512,50]{1,0:T(8,128)S(1)} %copy.65, s32[512,50]{1,0:T(8,128)S(1)} %copy.64), kind=kOutput, calls=%fused_computation.19 | convolution fusion | flops 110411776 | bytes 2404352 | tf_op jit(solution)/shard_map/vkh,vkl->vhl/dot_general | solution.py:169
  46.0 7.4 %collective-permute-done.8 = bf16[512,256]{1,0:T(8,128)(2,1)S(1)} collective-permute-done((bf16[512,256]{1,0:T(8,128)(2,1)S(1)}, bf16[512,256]{1,0:T(8,128)(2,1)S(1)}, u32[]{:S(2)}, u32[]{:S(2)}) %collective-permute-start.8) | collective-permute-done | bytes 262176 | tf_op jit(solution)/shard_map/ppermute | solution.py:33
  54.4 5.7 %all-to-all-done.1 = bf16[8,256,256]{2,1,0:T(8,128)(2,1)} async-done(((bf16[8,256,256]{2,1,0:T(8,128)(2,1)}), bf16[8,256,256]{2,1,0:T(8,128)(2,1)}, u32[]{:S(2)}, u32[]{:S(2)}) %all-to-all-start.1) | async-done | bytes 1048608 | tf_op jit(solution)/shard_map/all_to_all | solution.py:92
  63.3 7.0 %collective-permute-done.9 = bf16[512,256]{1,0:T(8,128)(2,1)S(1)} collective-permute-done((bf16[512,256]{1,0:T(8,128)(2,1)S(1)}, bf16[512,256]{1,0:T(8,128)(2,1)S(1)}, u32[]{:S(2)}, u32[]{:S(2)}) %collective-permute-start.9) | collective-permute-done | bytes 262176 | tf_op jit(solution)/shard_map/ppermute | solution.py:33
  73.9 7.8 %collective-permute-done.12 = bf16[512,256]{1,0:T(8,128)(2,1)S(1)} collective-permute-done((bf16[512,256]{1,0:T(8,128)(2,1)S(1)}, bf16[512,256]{1,0:T(8,128)(2,1)S(1)}, u32[]{:S(2)}, u32[]{:S(2)}) %collective-permute-start.12) | collective-permute-done | bytes 262176 | tf_op jit(solution)/shard_map/ppermute | solution.py:33
  87.5 4.4 %all-to-all-start.2 = ((bf16[8,256,256]{2,1,0:T(8,128)(2,1)}), bf16[8,256,256]{2,1,0:T(8,128)(2,1)}, u32[]{:S(2)}, u32[]{:S(2)}) async-start(bf16[8,256,256]{2,1,0:T(8,128)(2,1)} %bitcast.209), calls=%async_computation.2 | async-start | bytes 2097152 | tf_op jit(solution)/shard_map/all_to_all | solution.py:92
  93.6 24.5 %all-to-all-done.2 = bf16[8,256,256]{2,1,0:T(8,128)(2,1)} async-done(((bf16[8,256,256]{2,1,0:T(8,128)(2,1)}), bf16[8,256,256]{2,1,0:T(8,128)(2,1)}, u32[]{:S(2)}, u32[]{:S(2)}) %all-to-all-start.2) | async-done | bytes 1048608 | tf_op jit(solution)/shard_map/all_to_all | solution.py:92
  121.2 6.8 %collective-permute-done.15 = bf16[512,256]{1,0:T(8,128)(2,1)S(1)} collective-permute-done((bf16[512,256]{1,0:T(8,128)(2,1)S(1)}, bf16[512,256]{1,0:T(8,128)(2,1)S(1)}, u32[]{:S(2)}, u32[]{:S(2)}) %collective-permute-start.15) | collective-permute-done | bytes 262176 | tf_op jit(solution)/shard_map/ppermute | solution.py:33
  131.7 7.8 %collective-permute-done.18 = bf16[512,256]{1,0:T(8,128)(2,1)S(1)} collective-permute-done((bf16[512,256]{1,0:T(8,128)(2,1)S(1)}, bf16[512,256]{1,0:T(8,128)(2,1)S(1)}, u32[]{:S(2)}, u32[]{:S(2)}) %collective-permute-start.18) | collective-permute-done | bytes 262176 | tf_op jit(solution)/shard_map/ppermute | solution.py:33
  150.4 5.3 %collective-permute-done.25 = f32[512]{0:T(512)S(1)} collective-permute-done((f32[512]{0:T(512)S(1)}, f32[512]{0:T(512)S(1)}, u32[]{:S(2)}, u32[]{:S(2)}) %collective-permute-start.25) | collective-permute-done | bytes 2080 | tf_op jit(solution)/shard_map/ppermute | solution.py:33
  163.5 6.3 %collective-permute-done.29 = bf16[4,128,256]{2,1,0:T(8,128)(2,1)S(1)} collective-permute-done((bf16[4,128,256]{2,1,0:T(8,128)(2,1)S(1)}, bf16[4,128,256]{2,1,0:T(8,128)(2,1)S(1)}, u32[]{:S(2)}, u32[]{:S(2)}) %collective-permute-start.29) | collective-permute-done | bytes 262176 | tf_op jit(solution)/shard_map/ppermute | solution.py:33
  175.1 4.6 %all-to-all-start.3 = ((bf16[8,256,256]{2,1,0:T(8,128)(2,1)}), bf16[8,256,256]{2,1,0:T(8,128)(2,1)}, u32[]{:S(2)}, u32[]{:S(2)}) async-start(bf16[8,256,256]{2,1,0:T(8,128)(2,1)} %bitcast.18), calls=%async_computation.3 | async-start | bytes 2097152 | tf_op jit(solution)/shard_map/all_to_all | solution.py:92
  185.0 14.4 %collective-permute-done.34 = bf16[2,128,256]{2,1,0:T(8,128)(2,1)S(1)} collective-permute-done((bf16[2,128,256]{2,1,0:T(8,128)(2,1)S(1)}, bf16[2,128,256]{2,1,0:T(8,128)(2,1)S(1)}, u32[]{:S(2)}, u32[]{:S(2)}) %collective-permute-start.34) | collective-permute-done | bytes 131104 | tf_op jit(solution)/shard_map/ppermute | solution.py:33
  199.4 4.4 %collective-permute-start.35 = (bf16[1,128,256]{2,1,0:T(8,128)(2,1)S(1)}, bf16[1,128,256]{2,1,0:T(8,128)(2,1)S(1)}, u32[]{:S(2)}, u32[]{:S(2)}) collective-permute-start(bf16[1,128,256]{2,1,0:T(8,128)(2,1)S(1)} %constant_dynamic-slice_fusion.4), channel_id=1, source_target_pairs={{0,16},{4,20},{8,24},{12,28},{16,0},{20,4},{24,8},{28,12},{1,17},{... | collective-permute-start | bytes 196616 | tf_op jit(solution)/shard_map/ppermute | solution.py:33
  221.0 6.2 %collective-permute-done.40 = bf16[2,256,256]{2,1,0:T(8,128)(2,1)S(1)} collective-permute-done((bf16[2,256,256]{2,1,0:T(8,128)(2,1)S(1)}, bf16[2,256,256]{2,1,0:T(8,128)(2,1)S(1)}, u32[]{:S(2)}, u32[]{:S(2)}) %collective-permute-start.40) | collective-permute-done | bytes 262176 | tf_op jit(solution)/shard_map/ppermute | solution.py:33
  227.5 5.4 %collective-permute-done.39 = bf16[4,256,256]{2,1,0:T(8,128)(2,1)S(1)} collective-permute-done((bf16[4,256,256]{2,1,0:T(8,128)(2,1)S(1)}, bf16[4,256,256]{2,1,0:T(8,128)(2,1)S(1)}, u32[]{:S(2)}, u32[]{:S(2)}) %collective-permute-start.39) | collective-permute-done | bytes 524320 | tf_op jit(solution)/shard_map/ppermute | solution.py:33
  240.5 5.9 %collective-permute-done.47 = bf16[1,256,256]{2,1,0:T(8,128)(2,1)S(1)} collective-permute-done((bf16[1,256,256]{2,1,0:T(8,128)(2,1)S(1)}, bf16[1,256,256]{2,1,0:T(8,128)(2,1)S(1)}, u32[]{:S(2)}, u32[]{:S(2)}) %collective-permute-start.47) | collective-permute-done | bytes 131104 | tf_op jit(solution)/shard_map/ppermute | solution.py:33
  251.1 5.2 %all-to-all-start.4 = ((bf16[8,256,256]{2,1,0:T(8,128)(2,1)}), bf16[8,256,256]{2,1,0:T(8,128)(2,1)}, u32[]{:S(2)}, u32[]{:S(2)}) async-start(bf16[8,256,256]{2,1,0:T(8,128)(2,1)} %bitcast.37), calls=%async_computation.4 | async-start | bytes 2097152 | tf_op jit(solution)/shard_map/all_to_all | solution.py:92
  268.2 13.0 %collective-permute-done.48 = bf16[4,256,256]{2,1,0:T(8,128)(2,1)} collective-permute-done((bf16[4,256,256]{2,1,0:T(8,128)(2,1)}, bf16[4,256,256]{2,1,0:T(8,128)(2,1)}, u32[]{:S(2)}, u32[]{:S(2)}) %collective-permute-start.48) | collective-permute-done | bytes 524320 | tf_op jit(solution)/shard_map/ppermute | solution.py:33
  319.8 5.8 %collective-permute-done.57 = bf16[2,128,256]{2,1,0:T(8,128)(2,1)S(1)} collective-permute-done((bf16[2,128,256]{2,1,0:T(8,128)(2,1)S(1)}, bf16[2,128,256]{2,1,0:T(8,128)(2,1)S(1)}, u32[]{:S(2)}, u32[]{:S(2)}) %collective-permute-start.57) | collective-permute-done | bytes 131104 | tf_op jit(solution)/shard_map/ppermute | solution.py:33
  325.6 4.6 %collective-permute-start.58 = (bf16[1,128,256]{2,1,0:T(8,128)(2,1)S(1)}, bf16[1,128,256]{2,1,0:T(8,128)(2,1)S(1)}, u32[]{:S(2)}, u32[]{:S(2)}) collective-permute-start(bf16[1,128,256]{2,1,0:T(8,128)(2,1)S(1)} %constant_dynamic-slice_fusion.2), channel_id=1, source_target_pairs={{0,16},{4,20},{8,24},{12,28},{16,0},{20,4},{24,8},{28,12},{1,17},{... | collective-permute-start | bytes 196616 | tf_op jit(solution)/shard_map/ppermute | solution.py:33
  (431 shorter events, 158.9 us)
Async XLA Ops:
  0.7 10.5 %collective-permute-start = (bf16[512,128]{1,0:T(8,128)(2,1)}, bf16[512,128]{1,0:T(8,128)(2,1)S(1)}, u32[]{:S(2)}, u32[]{:S(2)}) collective-permute-start(bf16[512,128]{1,0:T(8,128)(2,1)} %param.18), channel_id=1, source_target_pairs={{0,2},{1,3},{2,0},{3,1},{4,6},{5,7},{6,4},{7,5},{8,10},{9,11},{10,... | collective-permute-start | bytes 393224 | tf_op jit(solution)/shard_map/ppermute | solution.py:33
  3.7 12.8 %collective-permute-start.2 = (bf16[512,128]{1,0:T(8,128)(2,1)}, bf16[512,128]{1,0:T(8,128)(2,1)S(1)}, u32[]{:S(2)}, u32[]{:S(2)}) collective-permute-start(bf16[512,128]{1,0:T(8,128)(2,1)} %param.18), channel_id=1, source_target_pairs={{0,1},{1,0},{2,3},{3,2},{4,5},{5,4},{6,7},{7,6},{8,9},{9,8},{10,11... | collective-permute-start | bytes 393224 | tf_op jit(solution)/shard_map/ppermute | solution.py:33
  3.7 12.3 %all-to-all-start = ((s32[8,1,256]{2,1,0:T(1,128)}), s32[8,1,256]{2,1,0:T(1,128)S(1)}, u32[]{:S(2)}, u32[]{:S(2)}) async-start(s32[8,1,256]{2,1,0:T(1,128)} %bitcast.220), calls=%async_computation | async-start | bytes 16384 | tf_op jit(solution)/shard_map/all_to_all | solution.py:92
  29.4 30.7 %all-to-all-start.1 = ((bf16[8,256,256]{2,1,0:T(8,128)(2,1)}), bf16[8,256,256]{2,1,0:T(8,128)(2,1)}, u32[]{:S(2)}, u32[]{:S(2)}) async-start(bf16[8,256,256]{2,1,0:T(8,128)(2,1)} %bitcast.5), calls=%async_computation.1 | async-start | bytes 2097152 | tf_op jit(solution)/shard_map/all_to_all | solution.py:92
  87.5 30.6 %all-to-all-start.2 = ((bf16[8,256,256]{2,1,0:T(8,128)(2,1)}), bf16[8,256,256]{2,1,0:T(8,128)(2,1)}, u32[]{:S(2)}, u32[]{:S(2)}) async-start(bf16[8,256,256]{2,1,0:T(8,128)(2,1)} %bitcast.209), calls=%async_computation.2 | async-start | bytes 2097152 | tf_op jit(solution)/shard_map/all_to_all | solution.py:92
  144.7 11.0 %collective-permute-start.21 = (bf16[512,256]{1,0:T(8,128)(2,1)}, bf16[512,256]{1,0:T(8,128)(2,1)S(1)}, u32[]{:S(2)}, u32[]{:S(2)}) collective-permute-start(bf16[512,256]{1,0:T(8,128)(2,1)} %get-tuple-element.124), channel_id=1, source_target_pairs={{0,1},{1,0},{2,3},{3,2},{4,5},{5,4},{6,7},{7,6},{8,9},{9,8},{10,11... | collective-permute-start | bytes 786440 | tf_op jit(solution)/shard_map/ppermute | solution.py:33
  175.1 35.2 %all-to-all-start.3 = ((bf16[8,256,256]{2,1,0:T(8,128)(2,1)}), bf16[8,256,256]{2,1,0:T(8,128)(2,1)}, u32[]{:S(2)}, u32[]{:S(2)}) async-start(bf16[8,256,256]{2,1,0:T(8,128)(2,1)} %bitcast.18), calls=%async_computation.3 | async-start | bytes 2097152 | tf_op jit(solution)/shard_map/all_to_all | solution.py:92
  179.7 29.0 %collective-permute-start.32 = (bf16[512,256]{1,0:T(8,128)(2,1)S(1)}, bf16[512,256]{1,0:T(8,128)(2,1)S(1)}, u32[]{:S(2)}, u32[]{:S(2)}) collective-permute-start(bf16[512,256]{1,0:T(8,128)(2,1)S(1)} %copy-done.22), channel_id=1, source_target_pairs={{0,1},{1,0},{2,3},{3,2},{4,5},{5,4},{6,7},{7,6},{8,9},{9,8},{10,11... | collective-permute-start | bytes 786440 | tf_op jit(solution)/shard_map/ppermute | solution.py:33
  179.8 25.6 %collective-permute-start.30 = (bf16[512,256]{1,0:T(8,128)(2,1)S(1)}, bf16[512,256]{1,0:T(8,128)(2,1)S(1)}, u32[]{:S(2)}, u32[]{:S(2)}) collective-permute-start(bf16[512,256]{1,0:T(8,128)(2,1)S(1)} %copy-done.22), channel_id=1, source_target_pairs={{0,2},{1,3},{2,0},{3,1},{4,6},{5,7},{6,4},{7,5},{8,10},{9,11},{10,... | collective-permute-start | bytes 786440 | tf_op jit(solution)/shard_map/ppermute | solution.py:33
  181.5 17.8 %collective-permute-start.34 = (bf16[2,128,256]{2,1,0:T(8,128)(2,1)S(1)}, bf16[2,128,256]{2,1,0:T(8,128)(2,1)S(1)}, u32[]{:S(2)}, u32[]{:S(2)}) collective-permute-start(bf16[2,128,256]{2,1,0:T(8,128)(2,1)S(1)} %dynamic-slice_bitcast_fusion.8), channel_id=1, source_target_pairs={{0,8},{4,12},{8,0},{12,4},{16,24},{20,28},{24,16},{28,20},{1,9},{5... | collective-permute-start | bytes 393224 | tf_op jit(solution)/shard_map/ppermute | solution.py:33
  183.4 25.1 %collective-permute-start.33 = (bf16[4,256,256]{2,1,0:T(8,128)(2,1)S(1)}, bf16[4,256,256]{2,1,0:T(8,128)(2,1)S(1)}, u32[]{:S(2)}, u32[]{:S(2)}) collective-permute-start(bf16[4,256,256]{2,1,0:T(8,128)(2,1)S(1)} %dynamic-slice_bitcast_fusion.1), channel_id=1, source_target_pairs={{0,4},{4,0},{8,12},{12,8},{16,20},{20,16},{24,28},{28,24},{1,5},{5... | collective-permute-start | bytes 1572872 | tf_op jit(solution)/shard_map/ppermute | solution.py:33
  215.5 11.8 %collective-permute-start.36 = (bf16[512,256]{1,0:T(8,128)(2,1)S(1)}, bf16[512,256]{1,0:T(8,128)(2,1)S(1)}, u32[]{:S(2)}, u32[]{:S(2)}) collective-permute-start(bf16[512,256]{1,0:T(8,128)(2,1)S(1)} %get-tuple-element.116), channel_id=1, source_target_pairs={{0,1},{1,0},{2,3},{3,2},{4,5},{5,4},{6,7},{7,6},{8,9},{9,8},{10,11... | collective-permute-start | bytes 786440 | tf_op jit(solution)/shard_map/ppermute | solution.py:33
  217.2 10.1 %collective-permute-start.38 = (bf16[512,256]{1,0:T(8,128)(2,1)S(1)}, bf16[512,256]{1,0:T(8,128)(2,1)S(1)}, u32[]{:S(2)}, u32[]{:S(2)}) collective-permute-start(bf16[512,256]{1,0:T(8,128)(2,1)S(1)} %add_convert_fusion.4), channel_id=1, source_target_pairs={{0,2},{1,3},{2,0},{3,1},{4,6},{5,7},{6,4},{7,5},{8,10},{9,11},{10,... | collective-permute-start | bytes 786440 | tf_op jit(solution)/shard_map/ppermute | solution.py:33
  219.5 13.5 %collective-permute-start.39 = (bf16[4,256,256]{2,1,0:T(8,128)(2,1)S(1)}, bf16[4,256,256]{2,1,0:T(8,128)(2,1)S(1)}, u32[]{:S(2)}, u32[]{:S(2)}) collective-permute-start(bf16[4,256,256]{2,1,0:T(8,128)(2,1)S(1)} %fusion.60), channel_id=1, source_target_pairs={{0,4},{4,0},{8,12},{12,8},{16,20},{20,16},{24,28},{28,24},{1,5},{5... | collective-permute-start | bytes 1572872 | tf_op jit(solution)/shard_map/ppermute | solution.py:33
  236.9 9.4 %collective-permute-start.47 = (bf16[1,256,256]{2,1,0:T(8,128)(2,1)S(1)}, bf16[1,256,256]{2,1,0:T(8,128)(2,1)S(1)}, u32[]{:S(2)}, u32[]{:S(2)}) collective-permute-start(bf16[1,256,256]{2,1,0:T(8,128)(2,1)S(1)} %constant_dynamic-slice_fusion.3), channel_id=1, source_target_pairs={{0,16},{4,20},{8,24},{12,28},{16,0},{20,4},{24,8},{28,12},{1,17},{... | collective-permute-start | bytes 393224 | tf_op jit(solution)/shard_map/ppermute | solution.py:33
  238.2 10.9 %collective-permute-start.46 = (bf16[2,256,256]{2,1,0:T(8,128)(2,1)S(1)}, bf16[2,256,256]{2,1,0:T(8,128)(2,1)S(1)}, u32[]{:S(2)}, u32[]{:S(2)}) collective-permute-start(bf16[2,256,256]{2,1,0:T(8,128)(2,1)S(1)} %dynamic-slice_bitcast_fusion.4), channel_id=1, source_target_pairs={{0,8},{4,12},{8,0},{12,4},{16,24},{20,28},{24,16},{28,20},{1,9},{5... | collective-permute-start | bytes 786440 | tf_op jit(solution)/shard_map/ppermute | solution.py:33
  251.1 34.8 %all-to-all-start.4 = ((bf16[8,256,256]{2,1,0:T(8,128)(2,1)}), bf16[8,256,256]{2,1,0:T(8,128)(2,1)}, u32[]{:S(2)}, u32[]{:S(2)}) async-start(bf16[8,256,256]{2,1,0:T(8,128)(2,1)} %bitcast.37), calls=%async_computation.4 | async-start | bytes 2097152 | tf_op jit(solution)/shard_map/all_to_all | solution.py:92
  260.3 21.0 %collective-permute-start.48 = (bf16[4,256,256]{2,1,0:T(8,128)(2,1)}, bf16[4,256,256]{2,1,0:T(8,128)(2,1)}, u32[]{:S(2)}, u32[]{:S(2)}) collective-permute-start(bf16[4,256,256]{2,1,0:T(8,128)(2,1)} %dynamic-slice_bitcast_fusion), channel_id=1, source_target_pairs={{0,4},{4,0},{8,12},{12,8},{16,20},{20,16},{24,28},{28,24},{1,5},{5... | collective-permute-start | bytes 1572872 | tf_op jit(solution)/shard_map/ppermute | solution.py:33
  264.3 26.0 %collective-permute-start.59 = (bf16[1,256,256]{2,1,0:T(8,128)(2,1)}, bf16[1,256,256]{2,1,0:T(8,128)(2,1)}, u32[]{:S(2)}, u32[]{:S(2)}) collective-permute-start(bf16[1,256,256]{2,1,0:T(8,128)(2,1)} %constant_dynamic-slice_fusion.1), channel_id=1, source_target_pairs={{0,16},{4,20},{8,24},{12,28},{16,0},{20,4},{24,8},{28,12},{1,17},{... | collective-permute-start | bytes 393224 | tf_op jit(solution)/shard_map/ppermute | solution.py:33
  293.9 9.4 %collective-permute-start.52 = (bf16[4,128,256]{2,1,0:T(8,128)(2,1)S(1)}, bf16[4,128,256]{2,1,0:T(8,128)(2,1)}, u32[]{:S(2)}, u32[]{:S(2)}) collective-permute-start(bf16[4,128,256]{2,1,0:T(8,128)(2,1)S(1)} %dynamic-slice_bitcast_fusion.3), channel_id=1, source_target_pairs={{0,4},{4,0},{8,12},{12,8},{16,20},{20,16},{24,28},{28,24},{1,5},{5... | collective-permute-start | bytes 786440 | tf_op jit(solution)/shard_map/ppermute | solution.py:33
  311.0 25.2 %all-to-all-start.5 = ((bf16[8,80,256]{2,1,0:T(8,128)(2,1)}), bf16[8,80,256]{2,1,0:T(8,128)(2,1)S(1)}, u32[]{:S(2)}, u32[]{:S(2)}) async-start(bf16[8,80,256]{2,1,0:T(8,128)(2,1)} %pad_maximum_fusion.9), calls=%async_computation.5 | async-start | bytes 655360 | tf_op jit(solution)/shard_map/all_to_all | solution.py:92
  314.7 17.1 %collective-permute-start.60 = (bf16[1,256,256]{2,1,0:T(8,128)(2,1)S(1)}, bf16[1,256,256]{2,1,0:T(8,128)(2,1)S(1)}, u32[]{:S(2)}, u32[]{:S(2)}) collective-permute-start(bf16[1,256,256]{2,1,0:T(8,128)(2,1)S(1)} %constant_dynamic-slice_fusion), channel_id=1, source_target_pairs={{0,16},{4,20},{8,24},{12,28},{16,0},{20,4},{24,8},{28,12},{1,17},{... | collective-permute-start | bytes 393224 | tf_op jit(solution)/shard_map/ppermute | solution.py:33
  319.2 14.8 %collective-permute-start.54 = (bf16[512,128]{1,0:T(8,128)(2,1)S(1)}, bf16[512,128]{1,0:T(8,128)(2,1)S(1)}, u32[]{:S(2)}, u32[]{:S(2)}) collective-permute-start(bf16[512,128]{1,0:T(8,128)(2,1)S(1)} %get-tuple-element.150), channel_id=1, source_target_pairs={{0,1},{1,0},{2,3},{3,2},{4,5},{5,4},{6,7},{7,6},{8,9},{9,8},{10,11... | collective-permute-start | bytes 393224 | tf_op jit(solution)/shard_map/ppermute | solution.py:33
  319.3 11.0 %collective-permute-start.55 = (bf16[512,128]{1,0:T(8,128)(2,1)S(1)}, bf16[512,128]{1,0:T(8,128)(2,1)S(1)}, u32[]{:S(2)}, u32[]{:S(2)}) collective-permute-start(bf16[512,128]{1,0:T(8,128)(2,1)S(1)} %get-tuple-element.151), channel_id=1, source_target_pairs={{0,1},{1,0},{2,3},{3,2},{4,5},{5,4},{6,7},{7,6},{8,9},{9,8},{10,11... | collective-permute-start | bytes 393224 | tf_op jit(solution)/shard_map/ppermute | solution.py:33
  (134 other events, 866.5 us)

commit v3 on v1

v3 whole, which is shorter than its diff:
```python
import jax
import jax.numpy as jnp
from jax import lax
from jax.experimental import pallas as pl
from jax.experimental.pallas import tpu as pltpu
from jax.sharding import PartitionSpec as P

eps = 1e-06
bf16 = jnp.bfloat16
f32 = jnp.float32
MIB = 1 << 20
PLACE = {}


def tie(*arrays):
    return lax.optimization_barrier(arrays)


def gate(arrays, *tokens):
    return list(tie(*arrays, *tokens)[: len(arrays)])


def product(left_side, right_side):
    return jnp.dot(left_side, right_side, preferred_element_type=f32)


def product_t(left_side, right_side):
    return lax.dot_general(
        left_side, right_side, (((0,), (0,)), ((), ())), preferred_element_type=f32
    )


def product_rt(left_side, right_side):
    return lax.dot_general(
        left_side, right_side, (((1,), (1,)), ((), ())), preferred_element_type=f32
    )


def tanh_of(x):
    return jnp.tanh(0.7978845608028654 * (x + 0.044715 * (x * x * x)))


def gelu(x):
    return 0.5 * x * (1.0 + tanh_of(x))


def gelu_grad(x):
    t = tanh_of(x)
    slope = 0.7978845608028654 * (1.0 + 0.134145 * (x * x))
    return 0.5 * (1.0 + t) + 0.5 * x * (1.0 - t * t) * slope


def swap(array, axis, distance):
    size = lax.axis_size(axis)
    return lax.ppermute(array, axis, [(i, i ^ distance) for i in range(size)])


def gather_cols(shard, beside=()):
    size = lax.axis_size("cols")
    far = [swap(shard, "cols", step) for step in range(2, size, 2)]
    if beside:
        tied = tie(*far, *beside)
        far, beside = tied[: len(far)], tied[len(far) :]
    blocks = []
    for block in [shard, *far]:
        blocks += [block, swap(block, "cols", 1)]
    return (blocks, beside) if beside else blocks


def pair_sums(blocks, dot=None):
    evens, odds = blocks[2::2], blocks[3::2]
    came = [swap(odd, "cols", 1) for odd in odds]
    near = [blocks[0], swap(blocks[1], "cols", 1)]
    outs = [(block.shape, bf16) for block in evens]
    if dot is None:
        return near, list(call(pair_kernel, outs, *evens, *came))
    *pairs, dot = call(
        pair_dot_kernel, outs + [(dot.shape, f32)], *evens, *came, dot, swap(dot, "cols", 1)
    )
    return near, pairs, dot


def parts_of(near, pairs, beside=()):
    far = [swap(pair, "cols", 2 * i + 2) for i, pair in enumerate(pairs)]
    parts = tie(*near, *far, *beside)
    count = 2 + len(far)
    return (parts[:count], parts[count:]) if beside else parts


def all_chips(dot):
    return [dot] + [
        swap(dot, "cols", far) for far in range(2, lax.axis_size("cols"), 2)
    ]


def row_exchange(chunks):
    return lax.all_to_all(chunks, "rows", split_axis=0, concat_axis=0, tiled=True)


def row_order():
    return list(reversed(range(lax.axis_size("rows"))))


def exchange(chunks):
    return [
        swap(chunk, "rows", k) if k else chunk for k, chunk in zip(row_order(), chunks)
    ]


class Going:
    def __init__(self, pieces, keep, send, level):
        self.pieces, self.keep, self.level = pieces, keep, level
        self.came = swap(send, "rows", 1 << level)

    def after(self, token):
        self.keep, self.came = gate([self.keep, self.came], token)
        return self


VECTORS = (0, 16)


def halves(pieces):
    return [(n // 2, m) for n, m in pieces]


def rows_of(pieces):
    return sum(n * m if n else m for n, m in pieces)


def fold(*goings):
    pieces = [p for going in goings for p in going.pieces]
    level = goings[0].level + 1
    half = halves(pieces)
    shape = (rows_of(half), goings[0].keep.shape[1])
    arrays = [a for going in goings for a in (going.keep, going.came)]
    kernel = form(fold_kernel, [going.pieces for going in goings], level)
    keep, send = call(kernel, [(shape, bf16)] * 2, *arrays)
    return Going(half, keep, send, level)


def close(going):
    while going.pieces[0][0] > 1:
        going = fold(going)
    total = going.keep.astype(f32) + going.came.astype(f32)
    outs, at = [], 0
    for n, m in going.pieces:
        part = total[at : at + m]
        outs.append(part if n else part[: m // 2] + part[m // 2 :])
        at += m
    return outs


def form(kernel, *options):
    def run(*refs):
        kernel(*options, *refs)

    run.__name__ = kernel.__name__
    return run


def call(kernel, outs, *ins, saved=(), scratch=(), flops=0):
    vmem = pl.BlockSpec(memory_space=pltpu.VMEM)
    shapes = [jax.ShapeDtypeStruct(shape, dtype) for shape, dtype in outs]
    placed = [pltpu.HBM(shape, dtype) for shape, dtype in saved]
    size = sum(a.size * a.dtype.itemsize for a in ins)
    size += sum(jnp.dtype(t).itemsize * n[0] * n[1] for n, t in list(outs) + list(saved))
    extra = sum(jnp.dtype(t).itemsize * n[0] * n[1] for n, t in saved)

    def run(me_ref, *refs):
        if not saved:
            kernel(me_ref, *refs)
            return
        inner = len(ins) + len(outs)
        count = len(saved)
        targets, held = refs[inner : inner + count], refs[inner + count : -1]
        kernel(me_ref, *refs[:inner], *held)
        copies = [
            pltpu.make_async_copy(held[i], targets[i], refs[-1].at[i])
            for i in range(count)
        ]
        for copy in copies:
            copy.start()
        for copy in copies:
            copy.wait()

    return pl.pallas_call(
        run,
        out_shape=shapes + placed,
        in_specs=[pl.BlockSpec(memory_space=pltpu.SMEM)] + [vmem] * len(ins),
        out_specs=[vmem] * len(shapes)
        + [pl.BlockSpec(memory_space=pltpu.HBM)] * len(placed),
        scratch_shapes=[pltpu.VMEM(shape, dtype) for shape, dtype in [*saved, *scratch]]
        + ([pltpu.SemaphoreType.DMA((len(saved),))] if saved else []),
        cost_estimate=pl.CostEstimate(flops=flops, bytes_accessed=size, transcendentals=0),
        compiler_params=pltpu.CompilerParams(
            vmem_limit_bytes=max(12 * MIB, size * 5 // 4 + extra + 6 * MIB)
        ),
        name=kernel.__name__,
    )(PLACE["me"], *ins)


def copy_in(*parts):
    arrays = [part[0] for part in parts]
    count = len(parts)
    shapes = []
    for array, index, rows in parts:
        size = array.shape[-2] if rows is None else rows[1] - rows[0]
        shapes.append(jax.ShapeDtypeStruct((size, array.shape[-1]), array.dtype))

    def run(*refs):
        sems = refs[-1]
        copies = []
        for i, (array, index, rows) in enumerate(parts):
            source = refs[i] if index is None else refs[i].at[index]
            if rows is not None:
                source = source.at[pl.ds(rows[0], rows[1] - rows[0])]
            copies.append(pltpu.make_async_copy(source, refs[count + i], sems.at[i]))
        for copy in copies:
            copy.start()
        for copy in copies:
            copy.wait()

    size = sum(s.size * s.dtype.itemsize for s in shapes)
    return pl.pallas_call(
        run,
        out_shape=shapes,
        in_specs=[pl.BlockSpec(memory_space=pltpu.HBM)] * count,
        out_specs=[pl.BlockSpec(memory_space=pltpu.VMEM)] * count,
        scratch_shapes=[pltpu.SemaphoreType.DMA((count,))],
        cost_estimate=pl.CostEstimate(flops=0, bytes_accessed=size, transcendentals=0),
        compiler_params=pltpu.CompilerParams(vmem_limit_bytes=size * 2 + 4 * MIB),
    )(*[pltpu.with_memory_space_constraint(a, pltpu.HBM) for a in arrays])


def block_rows(me_ref, j, size):
    return pl.ds(pl.multiple_of((me_ref[0] ^ j) * size, size), size)


def sum_refs(refs):
    total = refs[0][...].astype(f32)
    for ref in refs[1:]:
        total = total + ref[...].astype(f32)
    return total


def blocks_product(me_ref, block_refs, weight_ref):
    total = None
    for j, ref in enumerate(block_refs):
        rows = block_rows(me_ref, j, ref.shape[1])
        term = product(ref[...], weight_ref[rows, :])
        total = term if total is None else total + term
    return total


def blocks_scale(block_refs):
    total = None
    for ref in block_refs:
        wide = ref[...].astype(f32)
        term = jnp.sum(wide * wide, axis=1, keepdims=True)
        total = term if total is None else total + term
    return lax.rsqrt(total / (len(block_refs) * block_refs[0].shape[1]) + eps)


def lane_mask():
    return lax.broadcasted_iota(jnp.int32, (128, 128), 0) == lax.broadcasted_iota(
        jnp.int32, (128, 128), 1
    )


def to_lanes(column, out_ref):
    mask = lane_mask()
    for i in range(out_ref.shape[0]):
        part = jnp.where(mask, column[i * 128 : (i + 1) * 128], 0.0)
        out_ref[i : i + 1, :] = jnp.sum(part, axis=0, keepdims=True)


def from_lanes(rows):
    mask = lane_mask()
    return jnp.concatenate(
        [
            jnp.sum(jnp.where(mask, rows[i : i + 1, :], 0.0), axis=1, keepdims=True)
            for i in range(rows.shape[0])
        ],
        axis=0,
    )


def pair_kernel(me_ref, *refs):
    count = len(refs) // 3
    for one, other, out in zip(refs[:count], refs[count : 2 * count], refs[2 * count :]):
        out[...] = (one[...].astype(f32) + other[...].astype(f32)).astype(bf16)


def pair_dot_kernel(me_ref, *refs):
    count = (len(refs) - 3) // 3
    blocks, rest = refs[: 2 * count], refs[2 * count :]
    pair_kernel(me_ref, *blocks, *rest[2 : 2 + count])
    rest[-1][...] = rest[0][...] + rest[1][...]


def flat_kernel(me_ref, dense, out):
    nodes = out.shape[0]
    groups = dense.shape[0] // nodes
    for h in range(groups):
        part = dense[pl.ds(h, nodes, stride=groups), :]
        out[:, h * 128 : (h + 1) * 128] = part.astype(bf16)


def counts_kernel(me_ref, own, other, out, out_t):
    core = me_ref[0] & 1
    size = own.shape[0]
    for ref, place in ((own, core), (other, 1 - core)):
        rows = pl.ds(pl.multiple_of(place * size, size), size)
        value = ref[...]
        out[rows, :] = value
        out_t[:, rows] = value.T


def board_kernel(count, save, me_ref, *refs):
    blocks, refs = refs[:count], refs[count:]
    weight, bias, *refs = refs
    pre = blocks_product(me_ref, blocks, weight) + bias[...]
    if save:
        refs[0][...] = pre
        return
    pin, kinds, hidden_out = refs
    board = from_lanes(kinds) > 0.5
    hidden_out[...] = jnp.where(board, gelu(pre), pin[...].astype(f32)).astype(bf16)


def chunk_span(me_ref, k, size):
    return pl.ds(pl.multiple_of((me_ref[1] ^ k) * size, size), size)


def send_chunks(me_ref, matrix, value, outs, first):
    for i, out in enumerate(outs):
        rows = chunk_span(me_ref, first - i, out.shape[0])
        out[...] = product(matrix[rows, :], value).astype(bf16)


def rest_kernel(me_ref, value, matrix, *outs):
    send_chunks(me_ref, matrix, value[...], outs, len(outs) - 1)


def take_chunks(me_ref, matrix, chunks):
    total = None
    for k, ref in zip(reversed(range(len(chunks))), chunks):
        term = product(matrix[:, chunk_span(me_ref, k, ref.shape[0])], ref[...])
        total = term if total is None else total + term
    return total


def neigh_kernel(count, scaled, me_ref, *refs):
    blocks, refs = refs[:count], refs[count:]
    weight, bias, selector, moved_out, *outs = refs
    pre = blocks_product(me_ref, blocks, weight)
    if scaled:
        pre = blocks_scale(blocks) * pre
    moved = gelu(pre + bias[...]).astype(bf16)
    moved_out[...] = moved
    send_chunks(me_ref, selector, moved, outs, 2 * len(outs) - 1)


def neigh_save_kernel(count, scaled, me_ref, *refs):
    blocks, refs = refs[:count], refs[count:]
    weight, bias, self_w, self_out, pre_out, *refs = refs
    raw = blocks_product(me_ref, blocks, weight)
    if scaled:
        scale_out, raw_out = refs
        scale = blocks_scale(blocks)
        to_lanes(scale, scale_out)
        raw_out[...] = raw
        pre_out[...] = scale * raw + bias[...]
    else:
        pre_out[...] = raw + bias[...]
    self_out[...] = blocks_product(me_ref, blocks, self_w)


def aggregate_kernel(count, me_ref, *refs):
    chunks, (counts, inv_total, out) = refs[:count], refs[count:]
    total = take_chunks(me_ref, counts, chunks)
    out[...] = (total * from_lanes(inv_total)).astype(bf16)


def combine_kernel(count, scaled, save, me_ref, *refs):
    blocks, refs = refs[:count], refs[count:]
    weight, bias, self_raw, *refs = refs
    pre = blocks_product(me_ref, blocks, weight)
    own = self_raw[...]
    if scaled:
        own = from_lanes(refs[0]) * own
    pre = own + pre + bias[...]
    if save:
        refs[-1][...] = pre
    else:
        refs[-1][...] = gelu(pre).astype(bf16)


def blocks_rt(me_ref, pairs, outs):
    for j in reversed(range(len(outs))):
        rows = block_rows(me_ref, j, outs[j].shape[1])
        total = None
        for g, w in pairs:
            term = product_rt(g, w[rows, :])
            total = term if total is None else total + term
        outs[j][...] = total.astype(bf16)


def rt_kernel(me_ref, grad, weight, *outs):
    blocks_rt(me_ref, [(grad[...], weight)], outs)


def head_kernel(count, me_ref, *refs):
    blocks, refs = refs[:count], refs[count:]
    parts, refs = refs[: count // 2 + 1], refs[count // 2 + 1 :]
    weight, bias, *outs = refs
    outs, (dot_out, grad_out, scale_out, inner_out) = outs[:count], outs[count:]
    raw = blocks_product(me_ref, blocks, weight)
    scale = blocks_scale(blocks)
    to_lanes(scale, scale_out)
    pre = scale * raw + bias[...]
    inner_out[...] = gelu(pre).astype(bf16)
    grad = (sum_refs(parts) * gelu_grad(pre)).astype(bf16)
    grad_out[...] = grad
    blocks_rt(me_ref, [(grad, weight)], outs)
    to_lanes(jnp.sum(raw * grad.astype(f32), axis=1, keepdims=True), dot_out)


def combine_back_kernel(count, width, me_ref, *refs):
    parts, refs = refs[: count // 2 + 1], refs[count // 2 + 1 :]
    dots, refs = refs[: count // 2], refs[count // 2 :]
    weight, scale, pre, *outs, grad_out = refs
    dot = sum_refs(dots)
    scale, pre = from_lanes(scale), pre[...]
    factor = scale * scale * scale * from_lanes(dot) / width
    act_grad = scale * sum_refs(parts) - gelu(pre) * factor
    grad = (act_grad * gelu_grad(pre)).astype(bf16)
    grad_out[...] = grad
    blocks_rt(me_ref, [(grad, weight)], outs)


def pool_back_kernel(count, me_ref, *refs):
    parts, refs = refs[: count // 2 + 1], refs[count // 2 + 1 :]
    counts_t, inv_total, grad_out, *outs = refs
    grad = (sum_refs(parts) * from_lanes(inv_total)).astype(bf16)
    grad_out[...] = grad
    send_chunks(me_ref, counts_t, grad, outs, 2 * len(outs) - 1)


def neigh_back_kernel(count, cols, dotted, me_ref, *refs):
    chunks, refs = refs[:count], refs[count:]
    select_t, pre, combine_grad, self_w, weight, *refs = refs
    grad = (take_chunks(me_ref, select_t, chunks) * gelu_grad(pre[...])).astype(bf16)
    own = combine_grad[...]
    if dotted:
        self_raw, raw, *refs = refs
        dot = self_raw[...] * own.astype(f32) + raw[...] * grad.astype(f32)
        to_lanes(jnp.sum(dot, axis=1, keepdims=True), refs[-1])
    refs[cols][...] = grad
    blocks_rt(me_ref, [(own, self_w), (grad, weight)], refs[:cols])


def board_back_kernel(count, row_count, me_ref, *refs):
    parts, refs = refs[: count // 2 + 1], refs[count // 2 + 1 :]
    blocks, refs = refs[:count], refs[count:]
    pre, kinds, weight, *refs = refs
    biases, refs = refs[:6], refs[6:]
    outs, (keep, send, sums, pin_out) = refs[:count], refs[count:]
    total = sum_refs(parts)
    board = from_lanes(kinds) > 0.5
    wide = jnp.where(board, total, 0.0) * gelu_grad(pre[...])
    grad = wide.astype(bf16)
    rows = keep.shape[0] - 16
    terms_kernel(
        [(count, False)],
        row_count,
        me_ref,
        *blocks,
        grad,
        keep.at[pl.ds(0, rows)],
        send.at[pl.ds(0, rows)],
        sums,
    )
    last = sums[...]
    stacked = [ref[...] for ref in biases] + [last, jnp.zeros_like(last)]
    stacked = split_vectors(jnp.concatenate(stacked, axis=0))
    keep[rows : rows + 16, :] = stacked
    send[rows : rows + 16, :] = stacked
    blocks_rt(me_ref, [(grad, weight)], outs)
    pin_out[...] = jnp.where(board, 0.0, total)


def place_piece(stay, keep, send, at, value):
    rows = pl.ds(pl.multiple_of(at, 16), value.shape[0])

    @pl.when(stay)
    def _():
        keep[rows, :] = value

    @pl.when(jnp.logical_not(stay))
    def _():
        send[rows, :] = value


def terms_kernel(sets, row_count, me_ref, *refs):
    *refs, keep, send, sum_out = refs
    count = sum(n for n, _ in sets)
    blocks, refs = refs[:count], refs[count:]
    grad = refs[0][...]
    wide = grad.astype(f32)
    sum_out[...] = jnp.sum(wide, axis=0, keepdims=True)
    total = sum(ref.shape[1] for ref in blocks)
    chunk = total // row_count
    bit = me_ref[1] & 1
    base = 0
    for n, scaled in sets:
        value = (from_lanes(refs[1]) * wide).astype(bf16) if scaled else grad
        for j in range(n):
            ref = blocks[j]
            size = ref.shape[1]
            part = product_t(ref[...], value).astype(bf16)
            step = min(size, chunk)
            first = base + (me_ref[0] ^ j) * size
            for i in range(size // step):
                start = first + i * step
                q = start // chunk
                at = (q // 2) * chunk + start % chunk
                stay = (q & 1) == bit
                place_piece(stay, keep, send, at, part[i * step : (i + 1) * step])
        base += sum(ref.shape[1] for ref in blocks[:n])
        blocks = blocks[n:]


def both_kernel(count, other_count, row_count, me_ref, *refs):
    first, refs = refs[: count + 1], refs[count + 1 :]
    second, (keep, send, sums, other_sums) = refs[: other_count + 2], refs[other_count + 2 :]
    rows = sum(ref.shape[1] for ref in first[:count]) // 2
    rest = keep.shape[0] - rows
    terms_kernel(
        [(count, False)], row_count, me_ref, *first, keep.at[pl.ds(0, rows)], send.at[pl.ds(0, rows)], sums
    )
    terms_kernel(
        [(other_count, True)],
        row_count,
        me_ref,
        *second,
        keep.at[pl.ds(rows, rest)],
        send.at[pl.ds(rows, rest)],
        other_sums,
    )


def tail_kernel(count, row_count, me_ref, *refs):
    blocks, refs = refs[:count], refs[count:]
    weight, bias, cotangent, keep, send, sum_out, out = refs
    out[...] = blocks_product(me_ref, blocks, weight) + bias[...]
    terms_kernel(
        [(count, False)], row_count, me_ref, *blocks, cotangent, keep, send, sum_out
    )


def split_vectors(values):
    high = values.astype(bf16).astype(f32)
    return jnp.concatenate([high, values - high], axis=0).astype(bf16)


def fold_kernel(groups, level, me_ref, *refs):
    *refs, keep, send = refs
    bit = (me_ref[1] >> level) & 1
    base = 0
    for i, pieces in enumerate(groups):
        one, other = refs[2 * i], refs[2 * i + 1]
        at = 0
        for n, m in pieces:
            if n == 0:
                span = slice(at, at + m)
                total = one[span, :].astype(f32) + other[span, :].astype(f32)
                total = split_vectors(total[: m // 2] + total[m // 2 :])
                keep[base : base + m, :] = total
                send[base : base + m, :] = total
                at += m
                base += m
            for q in range(0, n, 2):
                rows = slice(base + (q // 2) * m, base + (q // 2 + 1) * m)
                for out, place in ((keep, bit), (send, 1 - bit)):
                    span = pl.ds(pl.multiple_of(at + (q + place) * m, 16), m)
                    total = one[span, :].astype(f32) + other[span, :].astype(f32)
                    out[rows, :] = total.astype(bf16)
            at += n * m
            base += (n // 2) * m


def dense_counts(neighbours, visit_counts, pool_size):
    low_width = 128
    high_width = pool_size // low_width
    upper_idx = neighbours // low_width
    lower_idx = neighbours % low_width
    upper_hot = jnp.where(
        upper_idx[:, :, None] == jnp.arange(high_width, dtype=jnp.int32)[None, None, :],
        visit_counts[:, :, None],
        0,
    ).astype(bf16)
    lower_hot = (
        lower_idx[:, :, None] == jnp.arange(low_width, dtype=jnp.int32)[None, None, :]
    ).astype(bf16)
    dense = jnp.einsum("vkh,vkl->vhl", upper_hot, lower_hot, preferred_element_type=f32)
    return dense.reshape(-1, low_width)


def body(
    pin_feats,
    board_feats,
    node_kinds,
    neighbours,
    visit_counts,
    pull_rows,
    proj_weight,
    proj_bias,
    neigh_weight,
    neigh_bias,
    combine_weight,
    combine_bias,
    head_weight,
    head_bias,
    tail_weight,
    tail_bias,
    cotangent,
):
    row_count = lax.axis_size("rows")
    cols = lax.axis_size("cols")
    PLACE["me"] = jnp.stack([lax.axis_index("cols"), lax.axis_index("rows")]).astype(
        jnp.int32
    )
    pool_size = pull_rows.shape[1]
    capacity = pool_size // row_count
    nodes, channels = pin_feats.shape
    width = neigh_weight.shape[1]
    square = 2 * nodes * width * channels
    spread_flops = 2 * nodes * pool_size * channels
    block = (nodes, channels)
    lanes = (nodes // 128, 128)
    middle = row_count // 2
    half_outs = [((capacity, channels), bf16)] * (row_count // 2)
    block_outs = [(block, bf16)] * cols
    row_vector = ((1, channels), f32)

    def terms(sets, blocks, grad, scale=None):
        rows = sum(b.shape[1] for b in blocks)
        keep, send, sums = call(
            form(terms_kernel, sets, row_count),
            [((rows // 2, channels), bf16)] * 2 + [row_vector],
            *blocks,
            grad,
            *(() if scale is None else (scale,)),
            flops=2 * nodes * rows * channels,
        )
        return Going([(row_count // 2, rows // row_count)], keep, send, 0), sums

    def both_terms(blocks, grad, other_blocks, other_grad, scale):
        pieces, rows = [], 0
        for run in (blocks, other_blocks):
            count = sum(b.shape[1] for b in run)
            pieces.append((row_count // 2, count // row_count))
            rows += count // 2
        keep, send, sums, other_sums = call(
            form(both_kernel, len(blocks), len(other_blocks), row_count),
            [((rows, channels), bf16)] * 2 + [row_vector] * 2,
            *blocks,
            grad,
            *other_blocks,
            other_grad,
            scale,
            flops=4 * nodes * rows * channels,
        )
        return Going(pieces, keep, send, 0), sums, other_sums

    def both_halves(matrix, first):
        value, *sent = first
        rest = call(rest_kernel, half_outs, value, matrix, flops=spread_flops // 2)
        return sent + list(rest)

    requested = row_exchange(pull_rows.reshape(row_count, capacity)).reshape(-1)
    board_blocks = gather_cols(board_feats)
    kinds = (node_kinds == 1).astype(f32).reshape(lanes)
    proj_in, proj_bias_in, pins = copy_in(
        (proj_weight, None, None), (proj_bias[None], None, None), (pin_feats, None, None)
    )
    (hidden,) = call(
        form(board_kernel, cols, False),
        [(block, bf16)],
        *board_blocks,
        proj_in,
        proj_bias_in,
        pins,
        kinds,
        flops=square // 2,
    )
    hidden, requested = tie(hidden, requested)
    share = nodes // 2
    counted, visits = (
        lax.dynamic_slice_in_dim(a, lax.axis_index("cols") % 2 * share, share)
        for a in gate([neighbours, visit_counts], hidden)
    )
    dense = dense_counts(counted, visits, pool_size)
    (own_counts,) = call(flat_kernel, [((share, pool_size), bf16)], dense)
    local = jnp.arange(nodes, dtype=jnp.int32)
    selector = (requested[:, None] == local[None, :]).astype(bf16)
    (neigh_w0,) = copy_in((gate([neigh_weight], hidden)[0], 0, None))
    inv_total = (1.0 / jnp.sum(visit_counts.astype(f32), axis=1)).reshape(lanes)

    blocks_0, (neigh_w0, selector, own_counts) = gather_cols(
        hidden, (neigh_w0, selector, own_counts)
    )
    sent = both_halves(
        selector,
        call(
            form(neigh_kernel, cols, False),
            [(block, bf16)] + half_outs,
            *blocks_0,
            neigh_w0,
            neigh_bias[0:1],
            selector,
            flops=square + spread_flops // 2,
        ),
    )
    chunks = exchange(sent)
    (
        neigh_w1,
        self_w0,
        self_w1,
        gather_w0,
        gather_w1,
        head_w,
        tail_w,
        neigh_b,
        combine_b,
        head_b,
        tail_b,
        cotangent,
    ) = copy_in(
        (gate([neigh_weight], sent[-1])[0], 1, None),
        (combine_weight, 0, (0, width)),
        (combine_weight, 1, (0, width)),
        (combine_weight, 0, (width, 2 * width)),
        (combine_weight, 1, (width, 2 * width)),
        (head_weight, None, None),
        (tail_weight, None, None),
        (neigh_bias, None, None),
        (combine_bias, None, None),
        (head_bias[None], None, None),
        (tail_bias[None], None, None),
        (cotangent, None, None),
    )
    late = gate(blocks_0, sent[-1])
    counts, counts_t = call(
        counts_kernel,
        [((nodes, pool_size), bf16), ((pool_size, nodes), bf16)],
        own_counts,
        swap(*gate([own_counts], sent[-1]), "cols", 1),
    )
    self_raw_0, neigh_pre_0 = call(
        form(neigh_save_kernel, cols, False),
        [(block, f32), (block, f32)],
        *late,
        neigh_w0,
        neigh_b[0:1],
        self_w0,
        flops=2 * square,
    )
    *chunks, self_raw_0, neigh_pre_0 = tie(*chunks, self_raw_0, neigh_pre_0)
    (gathered,) = call(
        form(aggregate_kernel, row_count),
        [(block, bf16)],
        *chunks,
        counts,
        inv_total,
        flops=spread_flops,
    )
    (board_pre,) = call(
        form(board_kernel, cols, True),
        [(block, f32)],
        *gate(board_blocks, gathered),
        proj_in,
        proj_bias_in,
        flops=square // 2,
    )
    gathered_0, (board_pre,) = gather_cols(gathered, (board_pre,))
    fixed = (gather_w0, combine_b[0:1], self_raw_0)
    (act,) = call(
        form(combine_kernel, cols, False, False),
        [(block, bf16)],
        *gathered_0,
        *fixed,
        flops=square,
    )
    (combine_pre_0,) = call(
        form(combine_kernel, cols, False, True),
        [(block, f32)],
        *gate([*gathered_0, *fixed], act),
        flops=square,
    )

    blocks_1, (combine_pre_0,) = gather_cols(act, (combine_pre_0,))
    sent = both_halves(
        selector,
        call(
            form(neigh_kernel, cols, True),
            [(block, bf16)] + half_outs,
            *blocks_1,
            neigh_w1,
            neigh_b[1:2],
            selector,
            flops=square + spread_flops // 2,
        ),
    )
    chunks = exchange(sent)
    *late, requested_late = gate([*blocks_1, requested], sent[-1])
    inner_near, pairs = pair_sums(
        call(rt_kernel, block_outs, *gate([cotangent], sent[-1]), tail_w, flops=square)
    )
    inner_parts = parts_of(inner_near, pairs)
    self_raw_1, neigh_pre_1, scale_1, neigh_raw_1 = call(
        form(neigh_save_kernel, cols, True),
        [(block, f32), (block, f32), (lanes, f32), (block, f32)],
        *late,
        neigh_w1,
        neigh_b[1:2],
        self_w1,
        flops=2 * square,
    )
    select_t = (local[:, None] == requested_late[None, :]).astype(bf16)
    *chunks, self_raw_1, neigh_pre_1, scale_1, neigh_raw_1, select_t = tie(
        *chunks, self_raw_1, neigh_pre_1, scale_1, neigh_raw_1, select_t
    )
    (gathered,) = call(
        form(aggregate_kernel, row_count),
        [(block, bf16)],
        *chunks,
        counts,
        inv_total,
        flops=spread_flops,
    )
    gathered_1, inner_parts = gather_cols(gathered, inner_parts)
    fixed = (gather_w1, combine_b[1:2], self_raw_1, scale_1)
    (act,) = call(
        form(combine_kernel, cols, True, False),
        [(block, bf16)],
        *gathered_1,
        *fixed,
        flops=square,
    )
    (combine_pre_1,) = call(
        form(combine_kernel, cols, True, True),
        [(block, f32)],
        *gate([*gathered_1, *fixed], act),
        flops=square,
    )

    blocks_2, (combine_pre_1,) = gather_cols(act, (combine_pre_1,))
    *blocks, dot, head_grad, scale_2, inner_act = call(
        form(head_kernel, cols),
        block_outs + [(lanes, f32), (block, bf16), (lanes, f32), (block, bf16)],
        *blocks_2,
        *inner_parts,
        head_w,
        head_b,
        flops=3 * square,
    )
    near, pairs, dot = pair_sums(blocks, dot)
    head_going, head_bias_grad = terms(
        [(cols, True)], blocks_2, *gate([head_grad], pairs[0]), scale_2
    )
    parts, (head_going.keep,) = parts_of(near, pairs, (head_going.keep,))
    dots = all_chips(dot)

    def combine_back(parts, dots, weight, scale, pre):
        *blocks, grad = call(
            form(combine_back_kernel, cols, width),
            block_outs + [(block, bf16)],
            *parts,
            *dots,
            weight,
            scale,
            pre,
            flops=square,
        )
        return grad, *pair_sums(blocks)

    def pool_back(parts):
        return both_halves(
            counts_t,
            call(
                form(pool_back_kernel, cols),
                [(block, bf16)] + half_outs,
                *parts,
                counts_t,
                inv_total,
                flops=spread_flops // 2,
            ),
        )

    combine_grad, near, pairs = combine_back(
        parts, dots, gather_w1, scale_2, combine_pre_1
    )
    head_going = fold(head_going.after(pairs[0]))
    parts, (head_going.keep,) = parts_of(near, pairs, (head_going.keep,))
    sent = pool_back(parts)
    chunks = exchange(sent)
    (inner_late,) = gate([inner_act], sent[-1])
    (combine_late,) = gate([combine_grad], *chunks[: middle + 1])
    combine_going, combine_bias_1 = terms(
        [(cols, True), (cols, False)], [*blocks_1, *gathered_1], combine_late, scale_1
    )
    inner_blocks = gather_cols(inner_late, chunks[: middle + 1])[0]
    tail_rows = (width // 2, channels)
    tail_keep, tail_send, tail_bias_grad, embeddings = call(
        form(tail_kernel, cols, row_count),
        [(tail_rows, bf16), (tail_rows, bf16), row_vector],
        *inner_blocks,
        tail_w,
        tail_b,
        cotangent,
        saved=[(block, f32)],
        flops=2 * square,
    )
    *chunks, combine_going.keep = tie(*chunks, combine_going.keep)

    neigh_in = (select_t, neigh_pre_1, combine_grad, self_w1, neigh_w1)
    *blocks, neigh_grad_1, dot = call(
        form(neigh_back_kernel, row_count, cols, True),
        block_outs + [(block, bf16), (lanes, f32)],
        *chunks,
        *neigh_in,
        self_raw_1,
        neigh_raw_1,
        flops=spread_flops + 2 * square,
    )
    near, pairs, dot = pair_sums(blocks, dot)
    head_going = fold(head_going.after(pairs[0]))
    combine_going = fold(combine_going.after(pairs[0]))
    tail_keep, tail_send = gate([tail_keep, tail_send], pairs[0])
    tail_going = Going([(row_count // 2, width // row_count)], tail_keep, tail_send, 0)
    parts, (combine_going.keep, head_going.keep) = parts_of(
        near, pairs, (combine_going.keep, head_going.keep)
    )
    dots = all_chips(dot)

    combine_grad, near, pairs = combine_back(
        parts, dots, gather_w0, scale_1, combine_pre_0
    )
    first_going = fold(combine_going.after(pairs[0]))
    tail_going = fold(tail_going.after(pairs[0]))
    parts, (tail_going.keep, head_going.came, first_going.keep) = parts_of(
        near, pairs, (tail_going.keep, head_going.came, first_going.keep)
    )
    sent = pool_back(parts)
    chunks = exchange(sent)
    combine_late, neigh_late = gate([combine_grad, neigh_grad_1], sent[-1])
    combine_going, combine_bias_0, neigh_bias_1 = both_terms(
        [*blocks_0, *gathered_0], combine_late, blocks_1, neigh_late, scale_1
    )

    neigh_in = (select_t, neigh_pre_0, combine_grad, self_w0, neigh_w0)
    *blocks, neigh_grad = call(
        form(neigh_back_kernel, row_count, cols, False),
        block_outs + [(block, bf16)],
        *chunks,
        *neigh_in,
        flops=spread_flops + 2 * square,
    )
    near, pairs = pair_sums(blocks)
    second_going = fold(combine_going.after(pairs[0]))
    neigh_going_0, neigh_bias_0 = terms(
        [(cols, False)], blocks_0, *gate([neigh_grad], pairs[0])
    )
    parts, (second_going.keep, neigh_going_0.keep, first_going.came, tail_going.came) = (
        parts_of(
            near,
            pairs,
            (second_going.keep, neigh_going_0.keep, first_going.came, tail_going.came),
        )
    )

    board_block = ((nodes, board_feats.shape[1]), bf16)
    proj_rows = proj_weight.shape[0]
    pieces = [(row_count // 2, proj_rows // row_count), VECTORS]
    *blocks, keep, send, _, grad_pin = call(
        form(board_back_kernel, cols, row_count),
        [board_block] * cols + [((rows_of(pieces), channels), bf16)] * 2 + [row_vector],
        *parts,
        *board_blocks,
        board_pre,
        kinds,
        proj_in,
        neigh_bias_0,
        neigh_bias_1,
        combine_bias_0,
        combine_bias_1,
        head_bias_grad,
        tail_bias_grad,
        saved=[(block, f32)],
        flops=square,
    )
    proj_going = Going(pieces, keep, send, 0)
    third_going = fold(second_going.after(keep), tail_going.after(keep))
    last_going = fold(neigh_going_0.after(keep), proj_going)
    near, pairs = pair_sums(blocks)
    grad_board = sum(p.astype(f32) for p in parts_of(near, pairs))
    (head_out,), (combine_out_1,) = close(head_going), close(first_going)
    combine_out_0, neigh_out_1, tail_out = close(third_going)
    neigh_out_0, proj_out, biases = close(last_going)
    return (
        embeddings,
        grad_pin,
        grad_board,
        proj_out,
        biases[6],
        jnp.stack([neigh_out_0, neigh_out_1]),
        biases[0:2],
        jnp.stack([combine_out_0, combine_out_1]),
        biases[2:4],
        head_out,
        biases[4],
        tail_out,
        biases[5],
    )


def solution(mesh):
    placed = (
        P("rows", "cols"),
        P("rows", "cols"),
        P("rows"),
        P("rows", None),
        P("rows", None),
        P("rows", None),
        P(None, "cols"),
        P("cols"),
        P(None, None, "cols"),
        P(None, "cols"),
        P(None, None, "cols"),
        P(None, "cols"),
        P(None, "cols"),
        P("cols"),
        P(None, "cols"),
        P("cols"),
        P("rows", "cols"),
    )
    return jax.shard_map(
        body,
        mesh=mesh,
        in_specs=placed,
        out_specs=(
            P("rows", "cols"),
            P("rows", "cols"),
            P("rows", "cols"),
            P("rows", "cols"),
            P("cols"),
            P(None, "rows", "cols"),
            P(None, "cols"),
            P(None, "rows", "cols"),
            P(None, "cols"),
            P("rows", "cols"),
            P("cols"),
            P("rows", "cols"),
            P("cols"),
        ),
        check_vma=False,
    )
```

time: 398 us -> 325 us (0.82)
  waiting for transfers between devices: 197 us -> 123 us
  Pallas kernels: 0 us -> 70 us
  starting transfers between devices: 52.6 us -> 115 us
  blocking collectives: 47.7 us -> 0 us
  matrix products: 51.1 us -> 5 us
  other arithmetic: 21.9 us -> 6.03 us
  between operations: 15.5 us -> 1.41 us
  local copies, waits for them, and re-layouts: 11.4 us -> 3.75 us
    ppermute x43 -> x90, starting transfers between devices: 26.4 us -> 109 us  [swap(): return lax.ppermute(array, axis, [(i, i ^ distance) for i in range(size)])]
    pallas_call x0 -> x51, Pallas kernels: none -> 70 us  [the longest x48 65.7 us: call(): pl.pallas_call(run, out_shape=shapes + placed, in_specs=[pl.BlockSpec(mem...]
    all_to_all x6 -> x1, waiting for transfers between devices: 64.9 us -> 2.37 us  [row_exchange(): lax.all_to_all(chunks, 'rows', split_axis=0, concat_axis=0, tiled=True)]
    reduce_scatter x2 -> x0, waiting for transfers between devices: 61.5 us -> none  [sum_rows_far(): lax.psum_scatter(chunked(terms), 'rows', scatter_dimension=0, tiled=True)]
    ppermute x43 -> x90, waiting for transfers between devices: 70.2 us -> 120 us  [swap(): return lax.ppermute(array, axis, [(i, i ^ distance) for i in range(size)])]
    dot_general x36 -> x1, matrix products: 51.1 us -> 5 us  [dense_counts(): jnp.einsum('vkh,vkl->vhl', upper_hot, lower_hot, preferred_element_type=f32)]
    all_to_all x1 -> x0, blocking collectives: 31.1 us -> none  [row_exchange(): lax.all_to_all(chunks, 'rows', split_axis=0, concat_axis=0, tiled=True, a...]
    all_to_all x6 -> x1, starting transfers between devices: 25.7 us -> 5.81 us  [row_exchange(): lax.all_to_all(chunks, 'rows', split_axis=0, concat_axis=0, tiled=True)]
  transfers between devices with their start and end apart: 51 -> 91, of which waited for: 23 -> 42; matrix products, arithmetic and copies ran while one was open for 14% -> 4% of each run, Pallas kernels for 0% -> 17%
where the time goes in v3:
time: 325 us; the launch traced here: 324 us
  waiting for transfers between devices  123 us (38%)
  starting transfers between devices  115 us (35%)
  Pallas kernels  70 us (22%)
  other arithmetic  6.03 us (2%)
  matrix products  5 us (2%)
  local copies, waits for them, and re-layouts  3.75 us (1%)
    ppermute x90, waiting for transfers between devices, swap(): return lax.ppermute(array, axis, [(i, i ^ distance) for i in range(size)])  120 us
    ppermute x90, starting transfers between devices, swap(): return lax.ppermute(array, axis, [(i, i ^ distance) for i in range(size)])  109 us
    pallas_call x48, Pallas kernels, call(): pl.pallas_call(run, out_shape=shapes + placed, in_specs=[pl.BlockSpec(mem...  65.7 us
  transfers between devices with their start and end apart: 91, of which 42 were waited for; matrix products, arithmetic and copies ran while one was open for 4% of the time, Pallas kernels for 17%

profile of v3, /device:TPU:0, one launch (start us, length us, event | category | flops | bytes accessed | tf_op | source)
XLA Modules:
  0.0 324.2 jit_solution(14276081693890803720)
XLA Ops:
  3.7 5.8 %all-to-all-start = ((s32[8,1,256]{2,1,0:T(1,128)}), s32[8,1,256]{2,1,0:T(1,128)S(1)}, u32[]{:S(2)}, u32[]{:S(2)}) async-start(s32[8,1,256]{2,1,0:T(1,128)} %bitcast.26), calls=%async_computation | async-start | bytes 16384 | tf_op jit(solution)/shard_map/all_to_all | solution.py:97
  18.8 5.0 %fusion = f32[256,16,128]{2,1,0:T(8,128)S(1)} fusion(s32[256,50]{1,0:T(8,128)S(1)} %copy.35, s32[256,50]{1,0:T(8,128)S(1)} %copy.34, s32[256,50]{1,0:T(8,128)S(1)} %copy.33), kind=kOutput, calls=%fused_computation.1 | convolution fusion | flops 54681600 | bytes 2250752 | tf_op jit(solution)/shard_map/vkh,vkl->vhl/dot_general | solution.py:607
  35.0 3.8 %collective-permute-start.9 = (bf16[256,256]{1,0:T(8,128)(2,1)S(1)}, bf16[256,256]{1,0:T(8,128)(2,1)S(1)}, u32[]{:S(2)}, u32[]{:S(2)}) collective-permute-start(bf16[256,256]{1,0:T(8,128)(2,1)S(1)} %get-tuple-element.306), channel_id=1, source_target_pairs={{0,16},{4,20},{8,24},{12,28},{16,0},{20,4},{24,8},{28,12},{1,17},{... | collective-permute-start | bytes 393224 | tf_op jit(solution)/shard_map/ppermute | solution.py:55
  41.0 9.2 %collective-permute-start.10 = (bf16[256,256]{1,0:T(8,128)(2,1)S(1)}, bf16[256,256]{1,0:T(8,128)(2,1)S(1)}, u32[]{:S(2)}, u32[]{:S(2)}) collective-permute-start(bf16[256,256]{1,0:T(8,128)(2,1)S(1)} %get-tuple-element.308), channel_id=1, source_target_pairs={{0,12},{4,8},{8,4},{12,0},{16,28},{20,24},{24,20},{28,16},{1,13},{... | collective-permute-start | bytes 393224 | tf_op jit(solution)/shard_map/ppermute | solution.py:55
  65.9 4.4 %collective-permute-done.15.refs_2_.refs_6_ = bf16[512,256]{1,0:T(8,128)(2,1)S(1)} collective-permute-done((bf16[512,256]{1,0:T(8,128)(2,1)S(1)}, bf16[512,256]{1,0:T(8,128)(2,1)S(1)}, u32[]{:S(2)}, u32[]{:S(2)}) %collective-permute-start.15) | collective-permute-done | bytes 262176 | tf_op jit(solution)/shard_map/ppermute | solution.py:55
  75.5 5.8 %collective-permute-done.18.refs_2_.refs_11_ = bf16[512,256]{1,0:T(8,128)(2,1)S(1)} collective-permute-done((bf16[512,256]{1,0:T(8,128)(2,1)S(1)}, bf16[512,256]{1,0:T(8,128)(2,1)S(1)}, u32[]{:S(2)}, u32[]{:S(2)}) %collective-permute-start.18) | collective-permute-done | bytes 262176 | tf_op jit(solution)/shard_map/ppermute | solution.py:55
  94.8 8.0 %collective-permute-start.25 = (bf16[256,256]{1,0:T(8,128)(2,1)S(1)}, bf16[256,256]{1,0:T(8,128)(2,1)S(1)}, u32[]{:S(2)}, u32[]{:S(2)}) collective-permute-start(bf16[256,256]{1,0:T(8,128)(2,1)S(1)} %get-tuple-element.355), channel_id=1, source_target_pairs={{0,8},{4,12},{8,0},{12,4},{16,24},{20,28},{24,16},{28,20},{1,9},{5... | collective-permute-start | bytes 393224 | tf_op jit(solution)/shard_map/ppermute | solution.py:55
  104.1 3.9 %collective-permute-done.22.refs_2_ = bf16[256,256]{1,0:T(8,128)(2,1)S(1)} collective-permute-done((bf16[256,256]{1,0:T(8,128)(2,1)S(1)}, bf16[256,256]{1,0:T(8,128)(2,1)S(1)}, u32[]{:S(2)}, u32[]{:S(2)}) %collective-permute-start.22) | collective-permute-done | bytes 131104 | tf_op jit(solution)/shard_map/ppermute | solution.py:55
  114.9 5.8 %collective-permute-done.31.refs_6_ = bf16[512,256]{1,0:T(8,128)(2,1)S(1)} collective-permute-done((bf16[512,256]{1,0:T(8,128)(2,1)S(1)}, bf16[512,256]{1,0:T(8,128)(2,1)S(1)}, u32[]{:S(2)}, u32[]{:S(2)}) %collective-permute-start.31) | collective-permute-done | bytes 262176 | tf_op jit(solution)/shard_map/ppermute | solution.py:55
  120.7 4.3 %collective-permute-done.28.refs_2_.refs_6_ = bf16[512,256]{1,0:T(8,128)(2,1)S(1)} collective-permute-done((bf16[512,256]{1,0:T(8,128)(2,1)S(1)}, bf16[512,256]{1,0:T(8,128)(2,1)S(1)}, u32[]{:S(2)}, u32[]{:S(2)}) %collective-permute-start.28) | collective-permute-done | bytes 262176 | tf_op jit(solution)/shard_map/ppermute | solution.py:55
  130.4 5.8 %collective-permute-done.34.refs_2_ = bf16[512,256]{1,0:T(8,128)(2,1)S(1)} collective-permute-done((bf16[512,256]{1,0:T(8,128)(2,1)S(1)}, bf16[512,256]{1,0:T(8,128)(2,1)S(1)}, u32[]{:S(2)}, u32[]{:S(2)}) %collective-permute-start.34) | collective-permute-done | bytes 262176 | tf_op jit(solution)/shard_map/ppermute | solution.py:55
  146.5 4.2 %collective-permute-done.39.refs_2_ = bf16[512,256]{1,0:T(8,128)(2,1)S(1)} collective-permute-done((bf16[512,256]{1,0:T(8,128)(2,1)S(1)}, bf16[512,256]{1,0:T(8,128)(2,1)S(1)}, u32[]{:S(2)}, u32[]{:S(2)}) %collective-permute-start.39) | collective-permute-done | bytes 262176 | tf_op jit(solution)/shard_map/ppermute | solution.py:55
  156.0 5.0 %collective-permute-done.44.refs_1_ = bf16[512,256]{1,0:T(8,128)(2,1)S(1)} collective-permute-done((bf16[512,256]{1,0:T(8,128)(2,1)S(1)}, bf16[512,256]{1,0:T(8,128)(2,1)S(1)}, u32[]{:S(2)}, u32[]{:S(2)}) %collective-permute-start.44) | collective-permute-done | bytes 262176 | tf_op jit(solution)/shard_map/ppermute | solution.py:55
  173.3 7.2 %collective-permute-start.53 = (bf16[256,256]{1,0:T(8,128)(2,1)S(1)}, bf16[256,256]{1,0:T(8,128)(2,1)S(1)}, u32[]{:S(2)}, u32[]{:S(2)}) collective-permute-start(bf16[256,256]{1,0:T(8,128)(2,1)S(1)} %get-tuple-element.444), channel_id=1, source_target_pairs={{0,8},{4,12},{8,0},{12,4},{16,24},{20,28},{24,16},{28,20},{1,9},{5... | collective-permute-start | bytes 393224 | tf_op jit(solution)/shard_map/ppermute | solution.py:55
  181.5 5.0 %collective-permute-done.49.refs_2_ = bf16[256,256]{1,0:T(8,128)(2,1)S(1)} collective-permute-done((bf16[256,256]{1,0:T(8,128)(2,1)S(1)}, bf16[256,256]{1,0:T(8,128)(2,1)S(1)}, u32[]{:S(2)}, u32[]{:S(2)}) %collective-permute-start.49) | collective-permute-done | bytes 131104 | tf_op jit(solution)/shard_map/ppermute | solution.py:55
  198.9 5.2 %collective-permute-done.46.refs_2_ = bf16[512,256]{1,0:T(8,128)(2,1)S(1)} collective-permute-done((bf16[512,256]{1,0:T(8,128)(2,1)S(1)}, bf16[512,256]{1,0:T(8,128)(2,1)S(1)}, u32[]{:S(2)}, u32[]{:S(2)}) %collective-permute-start.46) | collective-permute-done | bytes 262176 | tf_op jit(solution)/shard_map/ppermute | solution.py:55
  210.9 3.3 %tail_kernel.1 = (bf16[512,256]{1,0:T(8,128)(2,1)S(1)}, bf16[512,256]{1,0:T(8,128)(2,1)S(1)}, f32[1,256]{1,0:T(1,128)S(1)}, f32[512,256]{1,0:T(8,128)}) custom-call(s32[2]{0:T(128)S(1)} %pad_add_fusion.me_ref, bf16[512,256]{1,0:T(8,128)(2,1)S(1)} %get-tuple-element.435.refs_0_, bf16[512,256]{1,0:T(8,128)(2,1)S(1)} %collective-permute-done.45.refs_1_, ...), custom_call_target="tpu_custom_call" | custom-call | flops 536870912 | bytes 2885632 | tf_op jit(solution)/shard_map/tail_kernel/pallas_call | solution.py:187
  233.0 4.7 %both_kernel.1 = (bf16[1536,256]{1,0:T(8,128)(2,1)S(1)}, bf16[1536,256]{1,0:T(8,128)(2,1)S(1)}, f32[1,256]{1,0:T(1,128)S(1)}, f32[1,256]{1,0:T(1,128)S(1)}) custom-call(s32[2]{0:T(128)S(1)} %pad_add_fusion.me_ref, bf16[512,256]{1,0:T(8,128)(2,1)S(1)} %board_kernel.2.refs_0_, bf16[512,256]{1,0:T(8,128)(2,1)S(1)} %collective-permute-done.3.refs_1_, ...), custom_call_target="tpu_custom_call" | custom-call | flops 805306368 | bytes 5246976 | tf_op jit(solution)/shard_map/both_kernel/pallas_call | solution.py:187
  244.3 4.7 %collective-permute-start.73 = (bf16[256,256]{1,0:T(8,128)(2,1)S(1)}, bf16[256,256]{1,0:T(8,128)(2,1)S(1)}, u32[]{:S(2)}, u32[]{:S(2)}) collective-permute-start(bf16[256,256]{1,0:T(8,128)(2,1)S(1)} %get-tuple-element.507), channel_id=1, source_target_pairs={{0,8},{4,12},{8,0},{12,4},{16,24},{20,28},{24,16},{28,20},{1,9},{5... | collective-permute-start | bytes 393224 | tf_op jit(solution)/shard_map/ppermute | solution.py:55
  255.1 9.3 %collective-permute-done.74.refs_6_ = bf16[256,256]{1,0:T(8,128)(2,1)S(1)} collective-permute-done((bf16[256,256]{1,0:T(8,128)(2,1)S(1)}, bf16[256,256]{1,0:T(8,128)(2,1)S(1)}, u32[]{:S(2)}, u32[]{:S(2)}) %collective-permute-start.74) | collective-permute-done | bytes 131104 | tf_op jit(solution)/shard_map/ppermute | solution.py:55
  280.8 3.8 %board_back_kernel.1 = (bf16[512,128]{1,0:T(8,128)(2,1)S(1)}, bf16[512,128]{1,0:T(8,128)(2,1)S(1)}, bf16[512,128]{1,0:T(8,128)(2,1)S(1)}, bf16[512,128]{1,0:T(8,...) custom-call(s32[2]{0:T(128)S(1)} %pad_add_fusion.me_ref, ...), custom_call_target="tpu_custom_call" | custom-call | flops 268435456 | bytes 3433472 | tf_op jit(solution)/shard_map/board_back_kernel/pallas_call | solution.py:187
  293.0 9.4 %collective-permute-done.86.refs_1_ = bf16[400,256]{1,0:T(8,128)(2,1)S(1)} collective-permute-done((bf16[400,256]{1,0:T(8,128)(2,1)S(1)}, bf16[400,256]{1,0:T(8,128)(2,1)S(1)}, u32[]{:S(2)}, u32[]{:S(2)}) %collective-permute-start.86) | collective-permute-done | bytes 204832 | tf_op jit(solution)/shard_map/ppermute | solution.py:55
  307.4 8.9 %collective-permute-done.87 = bf16[208,256]{1,0:T(8,128)(2,1)S(1)} collective-permute-done((bf16[208,256]{1,0:T(8,128)(2,1)S(1)}, bf16[208,256]{1,0:T(8,128)(2,1)S(1)}, u32[]{:S(2)}, u32[]{:S(2)}) %collective-permute-start.87) | collective-permute-done | bytes 106528 | tf_op jit(solution)/shard_map/ppermute | solution.py:55
  318.2 3.6 %collective-permute-done.89 = bf16[512,256]{1,0:T(8,128)(2,1)S(1)} collective-permute-done((bf16[512,256]{1,0:T(8,128)(2,1)S(1)}, bf16[512,256]{1,0:T(8,128)(2,1)S(1)}, u32[]{:S(2)}, u32[]{:S(2)}) %collective-permute-start.89) | collective-permute-done | bytes 262176 | tf_op jit(solution)/shard_map/ppermute | solution.py:55
  (248 shorter events, 186.4 us)
Async XLA Ops:
  30.6 30.1 %collective-permute-start.13 = (bf16[256,2048]{1,0:T(8,128)(2,1)S(1)}, bf16[256,2048]{1,0:T(8,128)(2,1)S(1)}, u32[]{:S(2)}, u32[]{:S(2)}) collective-permute-start(bf16[256,2048]{1,0:T(8,128)(2,1)S(1)} %flat_kernel.1.refs_0_), channel_id=1, source_target_pairs={{0,1},{1,0},{2,3},{3,2},{4,5},{5,4},{6,7},{7,6},{8,9},{9,8},{10,11... | collective-permute-start | bytes 3145736 | tf_op jit(solution)/shard_map/ppermute | solution.py:55
  33.3 16.9 %collective-permute-start.7 = (bf16[256,256]{1,0:T(8,128)(2,1)S(1)}, bf16[256,256]{1,0:T(8,128)(2,1)S(1)}, u32[]{:S(2)}, u32[]{:S(2)}) collective-permute-start(bf16[256,256]{1,0:T(8,128)(2,1)S(1)} %get-tuple-element.304), channel_id=1, source_target_pairs={{0,24},{4,28},{8,16},{12,20},{16,8},{20,12},{24,0},{28,4},{1,25},{... | collective-permute-start | bytes 393224 | tf_op jit(solution)/shard_map/ppermute | solution.py:55
  35.0 20.3 %collective-permute-start.8 = (bf16[256,256]{1,0:T(8,128)(2,1)S(1)}, bf16[256,256]{1,0:T(8,128)(2,1)S(1)}, u32[]{:S(2)}, u32[]{:S(2)}) collective-permute-start(bf16[256,256]{1,0:T(8,128)(2,1)S(1)} %get-tuple-element.305), channel_id=1, source_target_pairs={{0,20},{4,16},{8,28},{12,24},{16,4},{20,0},{24,12},{28,8},{1,21},{... | collective-permute-start | bytes 393224 | tf_op jit(solution)/shard_map/ppermute | solution.py:55
  35.0 22.2 %collective-permute-start.9 = (bf16[256,256]{1,0:T(8,128)(2,1)S(1)}, bf16[256,256]{1,0:T(8,128)(2,1)S(1)}, u32[]{:S(2)}, u32[]{:S(2)}) collective-permute-start(bf16[256,256]{1,0:T(8,128)(2,1)S(1)} %get-tuple-element.306), channel_id=1, source_target_pairs={{0,16},{4,20},{8,24},{12,28},{16,0},{20,4},{24,8},{28,12},{1,17},{... | collective-permute-start | bytes 393224 | tf_op jit(solution)/shard_map/ppermute | solution.py:55
  41.0 18.4 %collective-permute-start.10 = (bf16[256,256]{1,0:T(8,128)(2,1)S(1)}, bf16[256,256]{1,0:T(8,128)(2,1)S(1)}, u32[]{:S(2)}, u32[]{:S(2)}) collective-permute-start(bf16[256,256]{1,0:T(8,128)(2,1)S(1)} %get-tuple-element.308), channel_id=1, source_target_pairs={{0,12},{4,8},{8,4},{12,0},{16,28},{20,24},{24,20},{28,16},{1,13},{... | collective-permute-start | bytes 393224 | tf_op jit(solution)/shard_map/ppermute | solution.py:55
  87.4 15.5 %collective-permute-start.21 = (bf16[256,256]{1,0:T(8,128)(2,1)S(1)}, bf16[256,256]{1,0:T(8,128)(2,1)S(1)}, u32[]{:S(2)}, u32[]{:S(2)}) collective-permute-start(bf16[256,256]{1,0:T(8,128)(2,1)S(1)} %get-tuple-element.350), channel_id=1, source_target_pairs={{0,24},{4,28},{8,16},{12,20},{16,8},{20,12},{24,0},{28,4},{1,25},{... | collective-permute-start | bytes 393224 | tf_op jit(solution)/shard_map/ppermute | solution.py:55
  89.3 18.7 %collective-permute-start.22 = (bf16[256,256]{1,0:T(8,128)(2,1)S(1)}, bf16[256,256]{1,0:T(8,128)(2,1)S(1)}, u32[]{:S(2)}, u32[]{:S(2)}) collective-permute-start(bf16[256,256]{1,0:T(8,128)(2,1)S(1)} %get-tuple-element.351), channel_id=1, source_target_pairs={{0,20},{4,16},{8,28},{12,24},{16,4},{20,0},{24,12},{28,8},{1,21},{... | collective-permute-start | bytes 393224 | tf_op jit(solution)/shard_map/ppermute | solution.py:55
  90.3 19.6 %collective-permute-start.23 = (bf16[256,256]{1,0:T(8,128)(2,1)S(1)}, bf16[256,256]{1,0:T(8,128)(2,1)S(1)}, u32[]{:S(2)}, u32[]{:S(2)}) collective-permute-start(bf16[256,256]{1,0:T(8,128)(2,1)S(1)} %get-tuple-element.352), channel_id=1, source_target_pairs={{0,16},{4,20},{8,24},{12,28},{16,0},{20,4},{24,8},{28,12},{1,17},{... | collective-permute-start | bytes 393224 | tf_op jit(solution)/shard_map/ppermute | solution.py:55
  93.5 16.9 %collective-permute-start.24 = (bf16[256,256]{1,0:T(8,128)(2,1)S(1)}, bf16[256,256]{1,0:T(8,128)(2,1)S(1)}, u32[]{:S(2)}, u32[]{:S(2)}) collective-permute-start(bf16[256,256]{1,0:T(8,128)(2,1)S(1)} %get-tuple-element.354), channel_id=1, source_target_pairs={{0,12},{4,8},{8,4},{12,0},{16,28},{20,24},{24,20},{28,16},{1,13},{... | collective-permute-start | bytes 393224 | tf_op jit(solution)/shard_map/ppermute | solution.py:55
  94.8 16.0 %collective-permute-start.25 = (bf16[256,256]{1,0:T(8,128)(2,1)S(1)}, bf16[256,256]{1,0:T(8,128)(2,1)S(1)}, u32[]{:S(2)}, u32[]{:S(2)}) collective-permute-start(bf16[256,256]{1,0:T(8,128)(2,1)S(1)} %get-tuple-element.355), channel_id=1, source_target_pairs={{0,8},{4,12},{8,0},{12,4},{16,24},{20,28},{24,16},{28,20},{1,9},{5... | collective-permute-start | bytes 393224 | tf_op jit(solution)/shard_map/ppermute | solution.py:55
  166.7 13.8 %collective-permute-start.48 = (bf16[256,256]{1,0:T(8,128)(2,1)S(1)}, bf16[256,256]{1,0:T(8,128)(2,1)S(1)}, u32[]{:S(2)}, u32[]{:S(2)}) collective-permute-start(bf16[256,256]{1,0:T(8,128)(2,1)S(1)} %get-tuple-element.437), channel_id=1, source_target_pairs={{0,24},{4,28},{8,16},{12,20},{16,8},{20,12},{24,0},{28,4},{1,25},{... | collective-permute-start | bytes 393224 | tf_op jit(solution)/shard_map/ppermute | solution.py:55
  168.7 17.8 %collective-permute-start.49 = (bf16[256,256]{1,0:T(8,128)(2,1)S(1)}, bf16[256,256]{1,0:T(8,128)(2,1)S(1)}, u32[]{:S(2)}, u32[]{:S(2)}) collective-permute-start(bf16[256,256]{1,0:T(8,128)(2,1)S(1)} %get-tuple-element.438), channel_id=1, source_target_pairs={{0,20},{4,16},{8,28},{12,24},{16,4},{20,0},{24,12},{28,8},{1,21},{... | collective-permute-start | bytes 393224 | tf_op jit(solution)/shard_map/ppermute | solution.py:55
  168.7 18.7 %collective-permute-start.50 = (bf16[256,256]{1,0:T(8,128)(2,1)S(1)}, bf16[256,256]{1,0:T(8,128)(2,1)S(1)}, u32[]{:S(2)}, u32[]{:S(2)}) collective-permute-start(bf16[256,256]{1,0:T(8,128)(2,1)S(1)} %get-tuple-element.439), channel_id=1, source_target_pairs={{0,16},{4,20},{8,24},{12,28},{16,0},{20,4},{24,8},{28,12},{1,17},{... | collective-permute-start | bytes 393224 | tf_op jit(solution)/shard_map/ppermute | solution.py:55
  173.0 14.4 %collective-permute-start.51 = (bf16[256,256]{1,0:T(8,128)(2,1)S(1)}, bf16[256,256]{1,0:T(8,128)(2,1)S(1)}, u32[]{:S(2)}, u32[]{:S(2)}) collective-permute-start(bf16[256,256]{1,0:T(8,128)(2,1)S(1)} %get-tuple-element.440), channel_id=1, source_target_pairs={{0,12},{4,8},{8,4},{12,0},{16,28},{20,24},{24,20},{28,16},{1,13},{... | collective-permute-start | bytes 393224 | tf_op jit(solution)/shard_map/ppermute | solution.py:55
  173.3 17.4 %collective-permute-start.53 = (bf16[256,256]{1,0:T(8,128)(2,1)S(1)}, bf16[256,256]{1,0:T(8,128)(2,1)S(1)}, u32[]{:S(2)}, u32[]{:S(2)}) collective-permute-start(bf16[256,256]{1,0:T(8,128)(2,1)S(1)} %get-tuple-element.444), channel_id=1, source_target_pairs={{0,8},{4,12},{8,0},{12,4},{16,24},{20,28},{24,16},{28,20},{1,9},{5... | collective-permute-start | bytes 393224 | tf_op jit(solution)/shard_map/ppermute | solution.py:55
  190.8 13.9 %collective-permute-start.59 = (bf16[1024,256]{1,0:T(8,128)(2,1)S(1)}, bf16[1024,256]{1,0:T(8,128)(2,1)S(1)}, u32[]{:S(2)}, u32[]{:S(2)}) collective-permute-start(bf16[1024,256]{1,0:T(8,128)(2,1)S(1)} %get-tuple-element.467), channel_id=1, source_target_pairs={{0,4},{4,0},{8,12},{12,8},{16,20},{20,16},{24,28},{28,24},{1,5},{5... | collective-permute-start | bytes 1572872 | tf_op jit(solution)/shard_map/ppermute | solution.py:55
  227.7 14.4 %collective-permute-start.68 = (bf16[256,256]{1,0:T(8,128)(2,1)S(1)}, bf16[256,256]{1,0:T(8,128)(2,1)S(1)}, u32[]{:S(2)}, u32[]{:S(2)}) collective-permute-start(bf16[256,256]{1,0:T(8,128)(2,1)S(1)} %get-tuple-element.501), channel_id=1, source_target_pairs={{0,28},{4,24},{8,20},{12,16},{16,12},{20,8},{24,4},{28,0},{1,29},{... | collective-permute-start | bytes 393224 | tf_op jit(solution)/shard_map/ppermute | solution.py:55
  230.1 14.1 %collective-permute-start.69 = (bf16[256,256]{1,0:T(8,128)(2,1)S(1)}, bf16[256,256]{1,0:T(8,128)(2,1)S(1)}, u32[]{:S(2)}, u32[]{:S(2)}) collective-permute-start(bf16[256,256]{1,0:T(8,128)(2,1)S(1)} %get-tuple-element.502), channel_id=1, source_target_pairs={{0,24},{4,28},{8,16},{12,20},{16,8},{20,12},{24,0},{28,4},{1,25},{... | collective-permute-start | bytes 393224 | tf_op jit(solution)/shard_map/ppermute | solution.py:55
  232.0 19.8 %collective-permute-start.70 = (bf16[256,256]{1,0:T(8,128)(2,1)S(1)}, bf16[256,256]{1,0:T(8,128)(2,1)S(1)}, u32[]{:S(2)}, u32[]{:S(2)}) collective-permute-start(bf16[256,256]{1,0:T(8,128)(2,1)S(1)} %get-tuple-element.503), channel_id=1, source_target_pairs={{0,20},{4,16},{8,28},{12,24},{16,4},{20,0},{24,12},{28,8},{1,21},{... | collective-permute-start | bytes 393224 | tf_op jit(solution)/shard_map/ppermute | solution.py:55
  237.7 37.9 %collective-permute-start.78 = (bf16[1536,256]{1,0:T(8,128)(2,1)S(1)}, bf16[1536,256]{1,0:T(8,128)(2,1)S(1)}, u32[]{:S(2)}, u32[]{:S(2)}) collective-permute-start(bf16[1536,256]{1,0:T(8,128)(2,1)S(1)} %get-tuple-element.520), channel_id=1, source_target_pairs={{0,4},{4,0},{8,12},{12,8},{16,20},{20,16},{24,28},{28,24},{1,5},{5... | collective-permute-start | bytes 2359304 | tf_op jit(solution)/shard_map/ppermute | solution.py:55
  238.8 14.1 %collective-permute-start.71 = (bf16[256,256]{1,0:T(8,128)(2,1)S(1)}, bf16[256,256]{1,0:T(8,128)(2,1)S(1)}, u32[]{:S(2)}, u32[]{:S(2)}) collective-permute-start(bf16[256,256]{1,0:T(8,128)(2,1)S(1)} %get-tuple-element.504), channel_id=1, source_target_pairs={{0,16},{4,20},{8,24},{12,28},{16,0},{20,4},{24,8},{28,12},{1,17},{... | collective-permute-start | bytes 393224 | tf_op jit(solution)/shard_map/ppermute | solution.py:55
  286.6 17.9 %collective-permute-start.88 = (bf16[768,256]{1,0:T(8,128)(2,1)S(1)}, bf16[768,256]{1,0:T(8,128)(2,1)S(1)}, u32[]{:S(2)}, u32[]{:S(2)}) collective-permute-start(bf16[768,256]{1,0:T(8,128)(2,1)S(1)} %get-tuple-element.558), channel_id=1, source_target_pairs={{0,8},{4,12},{8,0},{12,4},{16,24},{20,28},{24,16},{28,20},{1,9},{5... | collective-permute-start | bytes 1179656 | tf_op jit(solution)/shard_map/ppermute | solution.py:55
  303.0 13.4 %collective-permute-start.87 = (bf16[208,256]{1,0:T(8,128)(2,1)S(1)}, bf16[208,256]{1,0:T(8,128)(2,1)S(1)}, u32[]{:S(2)}, u32[]{:S(2)}) collective-permute-start(bf16[208,256]{1,0:T(8,128)(2,1)S(1)} %get-tuple-element.556), channel_id=1, source_target_pairs={{0,16},{4,20},{8,24},{12,28},{16,0},{20,4},{24,8},{28,12},{1,17},{... | collective-permute-start | bytes 319496 | tf_op jit(solution)/shard_map/ppermute | solution.py:55
  305.2 16.7 %collective-permute-start.89 = (bf16[512,256]{1,0:T(8,128)(2,1)S(1)}, bf16[512,256]{1,0:T(8,128)(2,1)S(1)}, u32[]{:S(2)}, u32[]{:S(2)}) collective-permute-start(bf16[512,256]{1,0:T(8,128)(2,1)S(1)} %get-tuple-element.566), channel_id=1, source_target_pairs={{0,16},{4,20},{8,24},{12,28},{16,0},{20,4},{24,8},{28,12},{1,17},{... | collective-permute-start | bytes 786440 | tf_op jit(solution)/shard_map/ppermute | solution.py:55
  (72 other events, 525.0 us)

commit v4 on v3

--- a/solution.py
+++ b/solution.py
@@ -464,17 +464,17 @@
 def board_back_kernel(count, row_count, me_ref, *refs):
     parts, refs = refs[: count // 2 + 1], refs[count // 2 + 1 :]
     blocks, refs = refs[:count], refs[count:]
-    pre, kinds, weight, *refs = refs
-    biases, refs = refs[:6], refs[6:]
-    outs, (keep, send, sums, pin_out) = refs[:count], refs[count:]
-    total = sum_refs(parts)
+    pre, kinds, *biases = refs
+    biases, (keep, send, sums, grad_out) = biases[:6], biases[6:]
     board = from_lanes(kinds) > 0.5
-    wide = jnp.where(board, total, 0.0) * gelu_grad(pre[...])
+    wide = jnp.where(board, sum_refs(parts), 0.0) * gelu_grad(pre[...])
     grad = wide.astype(bf16)
+    grad_out[...] = grad
     rows = keep.shape[0] - 16
     terms_kernel(
         [(count, False)],
         row_count,
+        False,
         me_ref,
         *blocks,
         grad,
@@ -487,8 +487,13 @@
     stacked = split_vectors(jnp.concatenate(stacked, axis=0))
     keep[rows : rows + 16, :] = stacked
     send[rows : rows + 16, :] = stacked
-    blocks_rt(me_ref, [(grad, weight)], outs)
-    pin_out[...] = jnp.where(board, 0.0, total)
+
+
+def board_rest_kernel(count, me_ref, *refs):
+    parts, (kinds, grad, weight, *refs) = refs[: count // 2 + 1], refs[count // 2 + 1 :]
+    outs, (pin_out,) = refs[:count], refs[count:]
+    blocks_rt(me_ref, [(grad[...], weight)], outs)
+    pin_out[...] = jnp.where(from_lanes(kinds) > 0.5, 0.0, sum_refs(parts))
 
 
 def place_piece(stay, keep, send, at, value):
@@ -503,10 +508,14 @@
         send[rows, :] = value
 
 
-def terms_kernel(sets, row_count, me_ref, *refs):
+def terms_kernel(sets, row_count, joined, me_ref, *refs):
     *refs, keep, send, sum_out = refs
     count = sum(n for n, _ in sets)
     blocks, refs = refs[:count], refs[count:]
+    if joined:
+        rows = sum(ref.shape[1] for ref in blocks) // 2
+        for other, out in zip(refs[-2:], (keep, send)):
+            out[pl.ds(rows, other.shape[0]), :] = other[...]
     grad = refs[0][...]
     wide = grad.astype(f32)
     sum_out[...] = jnp.sum(wide, axis=0, keepdims=True)
@@ -532,31 +541,20 @@
         blocks = blocks[n:]
 
 
-def both_kernel(count, other_count, row_count, me_ref, *refs):
-    first, refs = refs[: count + 1], refs[count + 1 :]
-    second, (keep, send, sums, other_sums) = refs[: other_count + 2], refs[other_count + 2 :]
-    rows = sum(ref.shape[1] for ref in first[:count]) // 2
-    rest = keep.shape[0] - rows
-    terms_kernel(
-        [(count, False)], row_count, me_ref, *first, keep.at[pl.ds(0, rows)], send.at[pl.ds(0, rows)], sums
-    )
-    terms_kernel(
-        [(other_count, True)],
-        row_count,
-        me_ref,
-        *second,
-        keep.at[pl.ds(rows, rest)],
-        send.at[pl.ds(rows, rest)],
-        other_sums,
-    )
-
-
 def tail_kernel(count, row_count, me_ref, *refs):
     blocks, refs = refs[:count], refs[count:]
     weight, bias, cotangent, keep, send, sum_out, out = refs
     out[...] = blocks_product(me_ref, blocks, weight) + bias[...]
     terms_kernel(
-        [(count, False)], row_count, me_ref, *blocks, cotangent, keep, send, sum_out
+        [(count, False)],
+        row_count,
+        False,
+        me_ref,
+        *blocks,
+        cotangent,
+        keep,
+        send,
+        sum_out,
     )
 
 
@@ -645,35 +643,24 @@
     block_outs = [(block, bf16)] * cols
     row_vector = ((1, channels), f32)
 
-    def terms(sets, blocks, grad, scale=None):
+    def term_halves(sets, blocks, grad, scale=None, joined=None):
         rows = sum(b.shape[1] for b in blocks)
+        pieces, others = ([], ()) if joined is None else joined
+        pieces = [(row_count // 2, rows // row_count), *pieces]
         keep, send, sums = call(
-            form(terms_kernel, sets, row_count),
-            [((rows // 2, channels), bf16)] * 2 + [row_vector],
+            form(terms_kernel, sets, row_count, joined is not None),
+            [((rows_of(pieces), channels), bf16)] * 2 + [row_vector],
             *blocks,
             grad,
             *(() if scale is None else (scale,)),
+            *others,
             flops=2 * nodes * rows * channels,
         )
-        return Going([(row_count // 2, rows // row_count)], keep, send, 0), sums
-
-    def both_terms(blocks, grad, other_blocks, other_grad, scale):
-        pieces, rows = [], 0
-        for run in (blocks, other_blocks):
-            count = sum(b.shape[1] for b in run)
-            pieces.append((row_count // 2, count // row_count))
-            rows += count // 2
-        keep, send, sums, other_sums = call(
-            form(both_kernel, len(blocks), len(other_blocks), row_count),
-            [((rows, channels), bf16)] * 2 + [row_vector] * 2,
-            *blocks,
-            grad,
-            *other_blocks,
-            other_grad,
-            scale,
-            flops=4 * nodes * rows * channels,
-        )
-        return Going(pieces, keep, send, 0), sums, other_sums
+        return pieces, [keep, send], sums
+
+    def terms(*args, joined=None):
+        pieces, halves_of, sums = term_halves(*args, joined=joined)
+        return Going(pieces, *halves_of, 0), sums
 
     def both_halves(matrix, first):
         value, *sent = first
@@ -703,15 +690,19 @@
         for a in gate([neighbours, visit_counts], hidden)
     )
     dense = dense_counts(counted, visits, pool_size)
-    (own_counts,) = call(flat_kernel, [((share, pool_size), bf16)], dense)
     local = jnp.arange(nodes, dtype=jnp.int32)
     selector = (requested[:, None] == local[None, :]).astype(bf16)
     (neigh_w0,) = copy_in((gate([neigh_weight], hidden)[0], 0, None))
     inv_total = (1.0 / jnp.sum(visit_counts.astype(f32), axis=1)).reshape(lanes)
 
-    blocks_0, (neigh_w0, selector, own_counts) = gather_cols(
-        hidden, (neigh_w0, selector, own_counts)
-    )
+    blocks_0, (neigh_w0, selector, dense) = gather_cols(
+        hidden, (neigh_w0, selector, dense)
+    )
+    (own_counts,) = call(
+        flat_kernel, [((share, pool_size), bf16)], *gate([dense], blocks_0[2])
+    )
+    *blocks_0, own_counts = tie(*blocks_0, own_counts)
+    other_counts = swap(own_counts, "cols", 1)
     sent = both_halves(
         selector,
         call(
@@ -725,50 +716,12 @@
         ),
     )
     chunks = exchange(sent)
-    (
-        neigh_w1,
-        self_w0,
-        self_w1,
-        gather_w0,
-        gather_w1,
-        head_w,
-        tail_w,
-        neigh_b,
-        combine_b,
-        head_b,
-        tail_b,
-        cotangent,
-    ) = copy_in(
-        (gate([neigh_weight], sent[-1])[0], 1, None),
-        (combine_weight, 0, (0, width)),
-        (combine_weight, 1, (0, width)),
-        (combine_weight, 0, (width, 2 * width)),
-        (combine_weight, 1, (width, 2 * width)),
-        (head_weight, None, None),
-        (tail_weight, None, None),
-        (neigh_bias, None, None),
-        (combine_bias, None, None),
-        (head_bias[None], None, None),
-        (tail_bias[None], None, None),
-        (cotangent, None, None),
-    )
-    late = gate(blocks_0, sent[-1])
     counts, counts_t = call(
         counts_kernel,
         [((nodes, pool_size), bf16), ((pool_size, nodes), bf16)],
         own_counts,
-        swap(*gate([own_counts], sent[-1]), "cols", 1),
-    )
-    self_raw_0, neigh_pre_0 = call(
-        form(neigh_save_kernel, cols, False),
-        [(block, f32), (block, f32)],
-        *late,
-        neigh_w0,
-        neigh_b[0:1],
-        self_w0,
-        flops=2 * square,
-    )
-    *chunks, self_raw_0, neigh_pre_0 = tie(*chunks, self_raw_0, neigh_pre_0)
+        other_counts,
+    )
     (gathered,) = call(
         form(aggregate_kernel, row_count),
         [(block, bf16)],
@@ -777,15 +730,24 @@
         inv_total,
         flops=spread_flops,
     )
-    (board_pre,) = call(
-        form(board_kernel, cols, True),
-        [(block, f32)],
-        *gate(board_blocks, gathered),
-        proj_in,
-        proj_bias_in,
-        flops=square // 2,
-    )
-    gathered_0, (board_pre,) = gather_cols(gathered, (board_pre,))
+    self_w0, gather_w0, neigh_b, combine_b = copy_in(
+        (gate([combine_weight], gathered)[0], 0, (0, width)),
+        (combine_weight, 0, (width, 2 * width)),
+        (neigh_bias, None, None),
+        (combine_bias, None, None),
+    )
+    self_raw_0, neigh_pre_0 = call(
+        form(neigh_save_kernel, cols, False),
+        [(block, f32), (block, f32)],
+        *gate(blocks_0, gathered),
+        neigh_w0,
+        neigh_b[0:1],
+        self_w0,
+        flops=2 * square,
+    )
+    gathered_0, (self_raw_0, neigh_pre_0, gather_w0) = gather_cols(
+        gathered, (self_raw_0, neigh_pre_0, gather_w0)
+    )
     fixed = (gather_w0, combine_b[0:1], self_raw_0)
     (act,) = call(
         form(combine_kernel, cols, False, False),
@@ -800,8 +762,21 @@
         *gate([*gathered_0, *fixed], act),
         flops=square,
     )
-
-    blocks_1, (combine_pre_0,) = gather_cols(act, (combine_pre_0,))
+    (neigh_w1, *weights) = copy_in(
+        (gate([neigh_weight], act)[0], 1, None),
+        (combine_weight, 1, (0, width)),
+        (combine_weight, 1, (width, 2 * width)),
+        (head_weight, None, None),
+        (tail_weight, None, None),
+        (head_bias[None], None, None),
+        (tail_bias[None], None, None),
+        (cotangent, None, None),
+    )
+
+    blocks_1, (combine_pre_0, neigh_w1, *weights) = gather_cols(
+        act, (combine_pre_0, neigh_w1, *weights)
+    )
+    self_w1, gather_w1, head_w, tail_w, head_b, tail_b, cotangent = weights
     sent = both_halves(
         selector,
         call(
@@ -815,11 +790,19 @@
         ),
     )
     chunks = exchange(sent)
-    *late, requested_late = gate([*blocks_1, requested], sent[-1])
     inner_near, pairs = pair_sums(
         call(rt_kernel, block_outs, *gate([cotangent], sent[-1]), tail_w, flops=square)
     )
     inner_parts = parts_of(inner_near, pairs)
+    (gathered,) = call(
+        form(aggregate_kernel, row_count),
+        [(block, bf16)],
+        *chunks,
+        counts,
+        inv_total,
+        flops=spread_flops,
+    )
+    *late, requested_late = gate([*blocks_1, requested], gathered)
     self_raw_1, neigh_pre_1, scale_1, neigh_raw_1 = call(
         form(neigh_save_kernel, cols, True),
         [(block, f32), (block, f32), (lanes, f32), (block, f32)],
@@ -830,18 +813,20 @@
         flops=2 * square,
     )
     select_t = (local[:, None] == requested_late[None, :]).astype(bf16)
-    *chunks, self_raw_1, neigh_pre_1, scale_1, neigh_raw_1, select_t = tie(
-        *chunks, self_raw_1, neigh_pre_1, scale_1, neigh_raw_1, select_t
-    )
-    (gathered,) = call(
-        form(aggregate_kernel, row_count),
-        [(block, bf16)],
-        *chunks,
-        counts,
-        inv_total,
-        flops=spread_flops,
-    )
-    gathered_1, inner_parts = gather_cols(gathered, inner_parts)
+    (board_pre,) = call(
+        form(board_kernel, cols, True),
+        [(block, f32)],
+        *gate(board_blocks, gathered),
+        proj_in,
+        proj_bias_in,
+        flops=square // 2,
+    )
+    gathered_1, (self_raw_1, neigh_pre_1, scale_1, neigh_raw_1, select_t, board_pre) = (
+        gather_cols(
+            gathered,
+            (self_raw_1, neigh_pre_1, scale_1, neigh_raw_1, select_t, board_pre),
+        )
+    )
     fixed = (gather_w1, combine_b[1:2], self_raw_1, scale_1)
     (act,) = call(
         form(combine_kernel, cols, True, False),
@@ -857,7 +842,9 @@
         flops=square,
     )
 
-    blocks_2, (combine_pre_1,) = gather_cols(act, (combine_pre_1,))
+    blocks_2, (combine_pre_1, *inner_parts) = gather_cols(
+        act, (combine_pre_1, *inner_parts)
+    )
     *blocks, dot, head_grad, scale_2, inner_act = call(
         form(head_kernel, cols),
         block_outs + [(lanes, f32), (block, bf16), (lanes, f32), (block, bf16)],
@@ -903,28 +890,17 @@
     combine_grad, near, pairs = combine_back(
         parts, dots, gather_w1, scale_2, combine_pre_1
     )
-    head_going = fold(head_going.after(pairs[0]))
-    parts, (head_going.keep,) = parts_of(near, pairs, (head_going.keep,))
+    combine_going, combine_bias_1 = terms(
+        [(cols, True), (cols, False)],
+        [*blocks_1, *gathered_1],
+        *gate([combine_grad], pairs[0]),
+        scale_1,
+    )
+    parts, (combine_going.keep,) = parts_of(near, pairs, (combine_going.keep,))
     sent = pool_back(parts)
     chunks = exchange(sent)
-    (inner_late,) = gate([inner_act], sent[-1])
-    (combine_late,) = gate([combine_grad], *chunks[: middle + 1])
-    combine_going, combine_bias_1 = terms(
-        [(cols, True), (cols, False)], [*blocks_1, *gathered_1], combine_late, scale_1
-    )
-    inner_blocks = gather_cols(inner_late, chunks[: middle + 1])[0]
-    tail_rows = (width // 2, channels)
-    tail_keep, tail_send, tail_bias_grad, embeddings = call(
-        form(tail_kernel, cols, row_count),
-        [(tail_rows, bf16), (tail_rows, bf16), row_vector],
-        *inner_blocks,
-        tail_w,
-        tail_b,
-        cotangent,
-        saved=[(block, f32)],
-        flops=2 * square,
-    )
-    *chunks, combine_going.keep = tie(*chunks, combine_going.keep)
+    inner_blocks = gather_cols(*gate([inner_act], sent[-1]))
+    *chunks, inner_blocks[-2] = tie(*chunks, inner_blocks[-2])
 
     neigh_in = (select_t, neigh_pre_1, combine_grad, self_w1, neigh_w1)
     *blocks, neigh_grad_1, dot = call(
@@ -937,29 +913,39 @@
         flops=spread_flops + 2 * square,
     )
     near, pairs, dot = pair_sums(blocks, dot)
-    head_going = fold(head_going.after(pairs[0]))
-    combine_going = fold(combine_going.after(pairs[0]))
-    tail_keep, tail_send = gate([tail_keep, tail_send], pairs[0])
-    tail_going = Going([(row_count // 2, width // row_count)], tail_keep, tail_send, 0)
-    parts, (combine_going.keep, head_going.keep) = parts_of(
-        near, pairs, (combine_going.keep, head_going.keep)
+    first_going = fold(head_going.after(pairs[0]), combine_going.after(pairs[0]))
+    tail_rows = (width // 2, channels)
+    tail_keep, tail_send, tail_bias_grad, embeddings = call(
+        form(tail_kernel, cols, row_count),
+        [(tail_rows, bf16), (tail_rows, bf16), row_vector],
+        *gate(inner_blocks, pairs[0]),
+        tail_w,
+        tail_b,
+        cotangent,
+        saved=[(block, f32)],
+        flops=2 * square,
+    )
+    parts, (first_going.keep, tail_keep) = parts_of(
+        near, pairs, (first_going.keep, tail_keep)
     )
     dots = all_chips(dot)
 
     combine_grad, near, pairs = combine_back(
         parts, dots, gather_w0, scale_1, combine_pre_0
     )
-    first_going = fold(combine_going.after(pairs[0]))
-    tail_going = fold(tail_going.after(pairs[0]))
-    parts, (tail_going.keep, head_going.came, first_going.keep) = parts_of(
-        near, pairs, (tail_going.keep, head_going.came, first_going.keep)
-    )
+    combine_going, combine_bias_0 = terms(
+        [(cols, False), (cols, False)],
+        [*blocks_0, *gathered_0],
+        *gate([combine_grad], pairs[0]),
+        joined=([(row_count // 2, width // row_count)], (tail_keep, tail_send)),
+    )
+    parts, (combine_going.keep,) = parts_of(near, pairs, (combine_going.keep,))
     sent = pool_back(parts)
     chunks = exchange(sent)
-    combine_late, neigh_late = gate([combine_grad, neigh_grad_1], sent[-1])
-    combine_going, combine_bias_0, neigh_bias_1 = both_terms(
-        [*blocks_0, *gathered_0], combine_late, blocks_1, neigh_late, scale_1
-    )
+    pieces_1, halves_1, neigh_bias_1 = term_halves(
+        [(cols, True)], blocks_1, *gate([neigh_grad_1], sent[-1]), scale_1
+    )
+    *chunks, halves_1[0] = tie(*chunks, halves_1[0])
 
     neigh_in = (select_t, neigh_pre_0, combine_grad, self_w0, neigh_w0)
     *blocks, neigh_grad = call(
@@ -970,46 +956,54 @@
         flops=spread_flops + 2 * square,
     )
     near, pairs = pair_sums(blocks)
+    first_going = fold(first_going.after(pairs[0]))
     second_going = fold(combine_going.after(pairs[0]))
     neigh_going_0, neigh_bias_0 = terms(
-        [(cols, False)], blocks_0, *gate([neigh_grad], pairs[0])
-    )
-    parts, (second_going.keep, neigh_going_0.keep, first_going.came, tail_going.came) = (
-        parts_of(
-            near,
-            pairs,
-            (second_going.keep, neigh_going_0.keep, first_going.came, tail_going.came),
-        )
+        [(cols, False)],
+        blocks_0,
+        *gate([neigh_grad], pairs[0]),
+        joined=(pieces_1, halves_1),
+    )
+    parts, (second_going.keep, neigh_going_0.keep, first_going.keep) = parts_of(
+        near, pairs, (second_going.keep, neigh_going_0.keep, first_going.keep)
     )
 
     board_block = ((nodes, board_feats.shape[1]), bf16)
     proj_rows = proj_weight.shape[0]
     pieces = [(row_count // 2, proj_rows // row_count), VECTORS]
-    *blocks, keep, send, _, grad_pin = call(
+    keep, send, _, board_grad = call(
         form(board_back_kernel, cols, row_count),
-        [board_block] * cols + [((rows_of(pieces), channels), bf16)] * 2 + [row_vector],
+        [((rows_of(pieces), channels), bf16)] * 2 + [row_vector, (block, bf16)],
         *parts,
         *board_blocks,
         board_pre,
         kinds,
-        proj_in,
         neigh_bias_0,
         neigh_bias_1,
         combine_bias_0,
         combine_bias_1,
         head_bias_grad,
         tail_bias_grad,
+        flops=square // 2,
+    )
+    third_going = fold(second_going.after(keep))
+    proj_going = Going(pieces, keep, send, 0)
+    last_going = fold(neigh_going_0.after(keep), proj_going)
+    *blocks, grad_pin = call(
+        form(board_rest_kernel, cols),
+        [board_block] * cols,
+        *gate(parts, last_going.keep),
+        kinds,
+        board_grad,
+        proj_in,
         saved=[(block, f32)],
-        flops=square,
-    )
-    proj_going = Going(pieces, keep, send, 0)
-    third_going = fold(second_going.after(keep), tail_going.after(keep))
-    last_going = fold(neigh_going_0.after(keep), proj_going)
+        flops=square // 2,
+    )
     near, pairs = pair_sums(blocks)
     grad_board = sum(p.astype(f32) for p in parts_of(near, pairs))
-    (head_out,), (combine_out_1,) = close(head_going), close(first_going)
-    combine_out_0, neigh_out_1, tail_out = close(third_going)
-    neigh_out_0, proj_out, biases = close(last_going)
+    head_out, combine_out_1 = close(first_going)
+    combine_out_0, tail_out = close(third_going)
+    neigh_out_0, neigh_out_1, proj_out, biases = close(last_going)
     return (
         embeddings,
         grad_pin,

time: 325 us -> 308 us (0.948)
  waiting for transfers between devices: 123 us -> 103 us
    ppermute x90 -> x86, waiting for transfers between devices: 120 us -> 101 us  [swap(): return lax.ppermute(array, axis, [(i, i ^ distance) for i in range(size)])]
    ppermute x90 -> x86, starting transfers between devices: 109 us -> 112 us  [swap(): return lax.ppermute(array, axis, [(i, i ^ distance) for i in range(size)])]
    pallas_call x48 -> x47, Pallas kernels: 65.7 us -> 65.2 us  [call(): pl.pallas_call(run, out_shape=shapes + placed, in_specs=[pl.BlockSpec(mem...]
  transfers between devices with their start and end apart: 91 -> 87, of which waited for: 42 -> 41; matrix products, arithmetic and copies ran while one was open for 4% -> 4% of each run, Pallas kernels for 17% -> 19%
where the time goes in v4:
time: 308 us
  starting transfers between devices  118 us (38%)
  waiting for transfers between devices  103 us (33%)
  Pallas kernels  70.4 us (23%)
  other arithmetic  5.2 us (2%)
  matrix products  5 us (2%)
  local copies, waits for them, and re-layouts  4.43 us (1%)
    ppermute x86, starting transfers between devices, swap(): return lax.ppermute(array, axis, [(i, i ^ distance) for i in range(size)])  112 us
    ppermute x86, waiting for transfers between devices, swap(): return lax.ppermute(array, axis, [(i, i ^ distance) for i in range(size)])  101 us
    pallas_call x47, Pallas kernels, call(): pl.pallas_call(run, out_shape=shapes + placed, in_specs=[pl.BlockSpec(mem...  65.2 us
  transfers between devices with their start and end apart: 87, of which 41 were waited for; matrix products, arithmetic and copies ran while one was open for 4% of the time, Pallas kernels for 19%

profile of v4, /device:TPU:0, one launch (start us, length us, event | category | flops | bytes accessed | tf_op | source)
XLA Modules:
  0.0 307.8 jit_solution(16292904228100312990)
XLA Ops:
  3.7 5.8 %all-to-all-start = ((s32[8,1,256]{2,1,0:T(1,128)}), s32[8,1,256]{2,1,0:T(1,128)S(1)}, u32[]{:S(2)}, u32[]{:S(2)}) async-start(s32[8,1,256]{2,1,0:T(1,128)} %bitcast.26), calls=%async_computation | async-start | bytes 16384 | tf_op jit(solution)/shard_map/all_to_all | solution.py:97
  19.4 5.0 %fusion = f32[256,16,128]{2,1,0:T(8,128)S(1)} fusion(s32[256,50]{1,0:T(8,128)S(1)} %copy.35, s32[256,50]{1,0:T(8,128)S(1)} %copy.34, s32[256,50]{1,0:T(8,128)S(1)} %copy.33), kind=kOutput, calls=%fused_computation.1 | convolution fusion | flops 54681600 | bytes 2250752 | tf_op jit(solution)/shard_map/vkh,vkl->vhl/dot_general | solution.py:605
  32.4 3.8 %collective-permute-start.9 = (bf16[256,256]{1,0:T(8,128)(2,1)S(1)}, bf16[256,256]{1,0:T(8,128)(2,1)S(1)}, u32[]{:S(2)}, u32[]{:S(2)}) collective-permute-start(bf16[256,256]{1,0:T(8,128)(2,1)S(1)} %get-tuple-element.312), channel_id=1, source_target_pairs={{0,16},{4,20},{8,24},{12,28},{16,0},{20,4},{24,8},{28,12},{1,17},{... | collective-permute-start | bytes 393224 | tf_op jit(solution)/shard_map/ppermute | solution.py:55
  37.6 9.9 %collective-permute-start.10 = (bf16[256,256]{1,0:T(8,128)(2,1)S(1)}, bf16[256,256]{1,0:T(8,128)(2,1)S(1)}, u32[]{:S(2)}, u32[]{:S(2)}) collective-permute-start(bf16[256,256]{1,0:T(8,128)(2,1)S(1)} %get-tuple-element.314), channel_id=1, source_target_pairs={{0,12},{4,8},{8,4},{12,0},{16,28},{20,24},{24,20},{28,16},{1,13},{... | collective-permute-start | bytes 393224 | tf_op jit(solution)/shard_map/ppermute | solution.py:55
  64.2 3.3 %collective-permute-done.15.refs_2_.refs_6_ = bf16[512,256]{1,0:T(8,128)(2,1)S(1)} collective-permute-done((bf16[512,256]{1,0:T(8,128)(2,1)S(1)}, bf16[512,256]{1,0:T(8,128)(2,1)S(1)}, u32[]{:S(2)}, u32[]{:S(2)}) %collective-permute-start.15) | collective-permute-done | bytes 262176 | tf_op jit(solution)/shard_map/ppermute | solution.py:55
  74.6 4.0 %collective-permute-done.18.refs_2_ = bf16[512,256]{1,0:T(8,128)(2,1)S(1)} collective-permute-done((bf16[512,256]{1,0:T(8,128)(2,1)S(1)}, bf16[512,256]{1,0:T(8,128)(2,1)S(1)}, u32[]{:S(2)}, u32[]{:S(2)}) %collective-permute-start.18) | collective-permute-done | bytes 262176 | tf_op jit(solution)/shard_map/ppermute | solution.py:55
  85.9 3.8 %collective-permute-start.23 = (bf16[256,256]{1,0:T(8,128)(2,1)S(1)}, bf16[256,256]{1,0:T(8,128)(2,1)S(1)}, u32[]{:S(2)}, u32[]{:S(2)}) collective-permute-start(bf16[256,256]{1,0:T(8,128)(2,1)S(1)} %get-tuple-element.355), channel_id=1, source_target_pairs={{0,16},{4,20},{8,24},{12,28},{16,0},{20,4},{24,8},{28,12},{1,17},{... | collective-permute-start | bytes 393224 | tf_op jit(solution)/shard_map/ppermute | solution.py:55
  91.2 9.1 %collective-permute-start.25 = (bf16[256,256]{1,0:T(8,128)(2,1)S(1)}, bf16[256,256]{1,0:T(8,128)(2,1)S(1)}, u32[]{:S(2)}, u32[]{:S(2)}) collective-permute-start(bf16[256,256]{1,0:T(8,128)(2,1)S(1)} %get-tuple-element.358), channel_id=1, source_target_pairs={{0,8},{4,12},{8,0},{12,4},{16,24},{20,28},{24,16},{28,20},{1,9},{5... | collective-permute-start | bytes 393224 | tf_op jit(solution)/shard_map/ppermute | solution.py:55
  101.9 3.4 %collective-permute-done.22.refs_2_ = bf16[256,256]{1,0:T(8,128)(2,1)S(1)} collective-permute-done((bf16[256,256]{1,0:T(8,128)(2,1)S(1)}, bf16[256,256]{1,0:T(8,128)(2,1)S(1)}, u32[]{:S(2)}, u32[]{:S(2)}) %collective-permute-start.22) | collective-permute-done | bytes 131104 | tf_op jit(solution)/shard_map/ppermute | solution.py:55
  119.9 5.9 %collective-permute-done.34.refs_6_ = bf16[512,256]{1,0:T(8,128)(2,1)S(1)} collective-permute-done((bf16[512,256]{1,0:T(8,128)(2,1)S(1)}, bf16[512,256]{1,0:T(8,128)(2,1)S(1)}, u32[]{:S(2)}, u32[]{:S(2)}) %collective-permute-start.34) | collective-permute-done | bytes 262176 | tf_op jit(solution)/shard_map/ppermute | solution.py:55
  126.9 3.6 %collective-permute-done.31.refs_2_ = bf16[512,256]{1,0:T(8,128)(2,1)S(1)} collective-permute-done((bf16[512,256]{1,0:T(8,128)(2,1)S(1)}, bf16[512,256]{1,0:T(8,128)(2,1)S(1)}, u32[]{:S(2)}, u32[]{:S(2)}) %collective-permute-start.31) | collective-permute-done | bytes 262176 | tf_op jit(solution)/shard_map/ppermute | solution.py:55
  140.8 4.2 %collective-permute-done.39.refs_2_ = bf16[512,256]{1,0:T(8,128)(2,1)S(1)} collective-permute-done((bf16[512,256]{1,0:T(8,128)(2,1)S(1)}, bf16[512,256]{1,0:T(8,128)(2,1)S(1)}, u32[]{:S(2)}, u32[]{:S(2)}) %collective-permute-start.39) | collective-permute-done | bytes 262176 | tf_op jit(solution)/shard_map/ppermute | solution.py:55
  150.3 3.3 %terms_kernel.6 = (bf16[1024,256]{1,0:T(8,128)(2,1)S(1)}, bf16[1024,256]{1,0:T(8,128)(2,1)S(1)}, f32[1,256]{1,0:T(1,128)S(1)}) custom-call(s32[2]{0:T(128)S(1)} %pad_add_fusion.me_ref, bf16[512,256]{1,0:T(8,128)(2,1)S(1)} %combine_kernel.4.refs_0_, bf16[512,256]{1,0:T(8,128)(2,1)S(1)} %collective-permute-done.17.refs_1_, ...), custom_call_target="tpu_custom_call" | custom-call | flops 536870912 | bytes 3410944 | tf_op jit(solution)/shard_map/terms_kernel/pallas_call | solution.py:187
  153.7 3.5 %collective-permute-done.43.refs_2_ = bf16[512,256]{1,0:T(8,128)(2,1)S(1)} collective-permute-done((bf16[512,256]{1,0:T(8,128)(2,1)S(1)}, bf16[512,256]{1,0:T(8,128)(2,1)S(1)}, u32[]{:S(2)}, u32[]{:S(2)}) %collective-permute-start.43) | collective-permute-done | bytes 262176 | tf_op jit(solution)/shard_map/ppermute | solution.py:55
  168.7 8.5 %collective-permute-start.49 = (bf16[256,256]{1,0:T(8,128)(2,1)S(1)}, bf16[256,256]{1,0:T(8,128)(2,1)S(1)}, u32[]{:S(2)}, u32[]{:S(2)}) collective-permute-start(bf16[256,256]{1,0:T(8,128)(2,1)S(1)} %get-tuple-element.437), channel_id=1, source_target_pairs={{0,12},{4,8},{8,4},{12,0},{16,28},{20,24},{24,20},{28,16},{1,13},{... | collective-permute-start | bytes 393224 | tf_op jit(solution)/shard_map/ppermute | solution.py:55
  209.4 3.3 %terms_kernel.7 = (bf16[1536,256]{1,0:T(8,128)(2,1)S(1)}, bf16[1536,256]{1,0:T(8,128)(2,1)S(1)}, f32[1,256]{1,0:T(1,128)S(1)}) custom-call(s32[2]{0:T(128)S(1)} %pad_add_fusion.me_ref, bf16[512,256]{1,0:T(8,128)(2,1)S(1)} %board_kernel.2.refs_0_, bf16[512,256]{1,0:T(8,128)(2,1)S(1)} %collective-permute-done.3.refs_1_, ...), custom_call_target="tpu_custom_call" | custom-call | flops 536870912 | bytes 4457472 | tf_op jit(solution)/shard_map/terms_kernel/pallas_call | solution.py:187
  212.7 3.5 %collective-permute-done.63.refs_2_ = bf16[512,256]{1,0:T(8,128)(2,1)S(1)} collective-permute-done((bf16[512,256]{1,0:T(8,128)(2,1)S(1)}, bf16[512,256]{1,0:T(8,128)(2,1)S(1)}, u32[]{:S(2)}, u32[]{:S(2)}) %collective-permute-start.63) | collective-permute-done | bytes 262176 | tf_op jit(solution)/shard_map/ppermute | solution.py:55
  222.8 3.2 %collective-permute-start.67 = (bf16[256,256]{1,0:T(8,128)(2,1)S(1)}, bf16[256,256]{1,0:T(8,128)(2,1)S(1)}, u32[]{:S(2)}, u32[]{:S(2)}) collective-permute-start(bf16[256,256]{1,0:T(8,128)(2,1)S(1)} %get-tuple-element.494), channel_id=1, source_target_pairs={{0,16},{4,20},{8,24},{12,28},{16,0},{20,4},{24,8},{28,12},{1,17},{... | collective-permute-start | bytes 393224 | tf_op jit(solution)/shard_map/ppermute | solution.py:55
  227.0 4.6 %collective-permute-start.68 = (bf16[256,256]{1,0:T(8,128)(2,1)S(1)}, bf16[256,256]{1,0:T(8,128)(2,1)S(1)}, u32[]{:S(2)}, u32[]{:S(2)}) collective-permute-start(bf16[256,256]{1,0:T(8,128)(2,1)S(1)} %get-tuple-element.496), channel_id=1, source_target_pairs={{0,12},{4,8},{8,4},{12,0},{16,28},{20,24},{24,20},{28,16},{1,13},{... | collective-permute-start | bytes 393224 | tf_op jit(solution)/shard_map/ppermute | solution.py:55
  231.6 4.5 %collective-permute-start.69 = (bf16[256,256]{1,0:T(8,128)(2,1)S(1)}, bf16[256,256]{1,0:T(8,128)(2,1)S(1)}, u32[]{:S(2)}, u32[]{:S(2)}) collective-permute-start(bf16[256,256]{1,0:T(8,128)(2,1)S(1)} %get-tuple-element.497), channel_id=1, source_target_pairs={{0,8},{4,12},{8,0},{12,4},{16,24},{20,28},{24,16},{28,20},{1,9},{5... | collective-permute-start | bytes 393224 | tf_op jit(solution)/shard_map/ppermute | solution.py:55
  242.0 8.3 %collective-permute-done.70.refs_6_ = bf16[256,256]{1,0:T(8,128)(2,1)S(1)} collective-permute-done((bf16[256,256]{1,0:T(8,128)(2,1)S(1)}, bf16[256,256]{1,0:T(8,128)(2,1)S(1)}, u32[]{:S(2)}, u32[]{:S(2)}) %collective-permute-start.70) | collective-permute-done | bytes 131104 | tf_op jit(solution)/shard_map/ppermute | solution.py:55
  263.4 3.6 %collective-permute-done.73.refs_2_ = bf16[512,256]{1,0:T(8,128)(2,1)S(1)} collective-permute-done((bf16[512,256]{1,0:T(8,128)(2,1)S(1)}, bf16[512,256]{1,0:T(8,128)(2,1)S(1)}, u32[]{:S(2)}, u32[]{:S(2)}) %collective-permute-start.73) | collective-permute-done | bytes 262176 | tf_op jit(solution)/shard_map/ppermute | solution.py:55
  282.8 7.7 %collective-permute-done.84 = bf16[384,256]{1,0:T(8,128)(2,1)S(1)} collective-permute-done((bf16[384,256]{1,0:T(8,128)(2,1)S(1)}, bf16[384,256]{1,0:T(8,128)(2,1)S(1)}, u32[]{:S(2)}, u32[]{:S(2)}) %collective-permute-start.84) | collective-permute-done | bytes 196640 | tf_op jit(solution)/shard_map/ppermute | solution.py:55
  295.9 9.3 %collective-permute-done.82 = bf16[336,256]{1,0:T(8,128)(2,1)S(1)} collective-permute-done((bf16[336,256]{1,0:T(8,128)(2,1)S(1)}, bf16[336,256]{1,0:T(8,128)(2,1)S(1)}, u32[]{:S(2)}, u32[]{:S(2)}) %collective-permute-start.82) | collective-permute-done | bytes 172064 | tf_op jit(solution)/shard_map/ppermute | solution.py:55
  (241 shorter events, 181.2 us)
Async XLA Ops:
  26.4 23.0 %collective-permute-start.13 = (bf16[256,2048]{1,0:T(8,128)(2,1)S(1)}, bf16[256,2048]{1,0:T(8,128)(2,1)S(1)}, u32[]{:S(2)}, u32[]{:S(2)}) collective-permute-start(bf16[256,2048]{1,0:T(8,128)(2,1)S(1)} %flat_kernel.1.refs_0_), channel_id=1, source_target_pairs={{0,1},{1,0},{2,3},{3,2},{4,5},{5,4},{6,7},{7,6},{8,9},{9,8},{10,11... | collective-permute-start | bytes 3145736 | tf_op jit(solution)/shard_map/ppermute | solution.py:55
  30.9 16.6 %collective-permute-start.7 = (bf16[256,256]{1,0:T(8,128)(2,1)S(1)}, bf16[256,256]{1,0:T(8,128)(2,1)S(1)}, u32[]{:S(2)}, u32[]{:S(2)}) collective-permute-start(bf16[256,256]{1,0:T(8,128)(2,1)S(1)} %get-tuple-element.310), channel_id=1, source_target_pairs={{0,24},{4,28},{8,16},{12,20},{16,8},{20,12},{24,0},{28,4},{1,25},{... | collective-permute-start | bytes 393224 | tf_op jit(solution)/shard_map/ppermute | solution.py:55
  32.3 20.3 %collective-permute-start.8 = (bf16[256,256]{1,0:T(8,128)(2,1)S(1)}, bf16[256,256]{1,0:T(8,128)(2,1)S(1)}, u32[]{:S(2)}, u32[]{:S(2)}) collective-permute-start(bf16[256,256]{1,0:T(8,128)(2,1)S(1)} %get-tuple-element.311), channel_id=1, source_target_pairs={{0,20},{4,16},{8,28},{12,24},{16,4},{20,0},{24,12},{28,8},{1,21},{... | collective-permute-start | bytes 393224 | tf_op jit(solution)/shard_map/ppermute | solution.py:55
  32.4 21.7 %collective-permute-start.9 = (bf16[256,256]{1,0:T(8,128)(2,1)S(1)}, bf16[256,256]{1,0:T(8,128)(2,1)S(1)}, u32[]{:S(2)}, u32[]{:S(2)}) collective-permute-start(bf16[256,256]{1,0:T(8,128)(2,1)S(1)} %get-tuple-element.312), channel_id=1, source_target_pairs={{0,16},{4,20},{8,24},{12,28},{16,0},{20,4},{24,8},{28,12},{1,17},{... | collective-permute-start | bytes 393224 | tf_op jit(solution)/shard_map/ppermute | solution.py:55
  37.6 19.4 %collective-permute-start.10 = (bf16[256,256]{1,0:T(8,128)(2,1)S(1)}, bf16[256,256]{1,0:T(8,128)(2,1)S(1)}, u32[]{:S(2)}, u32[]{:S(2)}) collective-permute-start(bf16[256,256]{1,0:T(8,128)(2,1)S(1)} %get-tuple-element.314), channel_id=1, source_target_pairs={{0,12},{4,8},{8,4},{12,0},{16,28},{20,24},{24,20},{28,16},{1,13},{... | collective-permute-start | bytes 393224 | tf_op jit(solution)/shard_map/ppermute | solution.py:55
  83.6 16.7 %collective-permute-start.21 = (bf16[256,256]{1,0:T(8,128)(2,1)S(1)}, bf16[256,256]{1,0:T(8,128)(2,1)S(1)}, u32[]{:S(2)}, u32[]{:S(2)}) collective-permute-start(bf16[256,256]{1,0:T(8,128)(2,1)S(1)} %get-tuple-element.353), channel_id=1, source_target_pairs={{0,24},{4,28},{8,16},{12,20},{16,8},{20,12},{24,0},{28,4},{1,25},{... | collective-permute-start | bytes 393224 | tf_op jit(solution)/shard_map/ppermute | solution.py:55
  85.9 19.3 %collective-permute-start.22 = (bf16[256,256]{1,0:T(8,128)(2,1)S(1)}, bf16[256,256]{1,0:T(8,128)(2,1)S(1)}, u32[]{:S(2)}, u32[]{:S(2)}) collective-permute-start(bf16[256,256]{1,0:T(8,128)(2,1)S(1)} %get-tuple-element.354), channel_id=1, source_target_pairs={{0,20},{4,16},{8,28},{12,24},{16,4},{20,0},{24,12},{28,8},{1,21},{... | collective-permute-start | bytes 393224 | tf_op jit(solution)/shard_map/ppermute | solution.py:55
  85.9 20.5 %collective-permute-start.23 = (bf16[256,256]{1,0:T(8,128)(2,1)S(1)}, bf16[256,256]{1,0:T(8,128)(2,1)S(1)}, u32[]{:S(2)}, u32[]{:S(2)}) collective-permute-start(bf16[256,256]{1,0:T(8,128)(2,1)S(1)} %get-tuple-element.355), channel_id=1, source_target_pairs={{0,16},{4,20},{8,24},{12,28},{16,0},{20,4},{24,8},{28,12},{1,17},{... | collective-permute-start | bytes 393224 | tf_op jit(solution)/shard_map/ppermute | solution.py:55
  90.7 15.7 %collective-permute-start.24 = (bf16[256,256]{1,0:T(8,128)(2,1)S(1)}, bf16[256,256]{1,0:T(8,128)(2,1)S(1)}, u32[]{:S(2)}, u32[]{:S(2)}) collective-permute-start(bf16[256,256]{1,0:T(8,128)(2,1)S(1)} %get-tuple-element.357), channel_id=1, source_target_pairs={{0,12},{4,8},{8,4},{12,0},{16,28},{20,24},{24,20},{28,16},{1,13},{... | collective-permute-start | bytes 393224 | tf_op jit(solution)/shard_map/ppermute | solution.py:55
  91.2 16.5 %collective-permute-start.25 = (bf16[256,256]{1,0:T(8,128)(2,1)S(1)}, bf16[256,256]{1,0:T(8,128)(2,1)S(1)}, u32[]{:S(2)}, u32[]{:S(2)}) collective-permute-start(bf16[256,256]{1,0:T(8,128)(2,1)S(1)} %get-tuple-element.358), channel_id=1, source_target_pairs={{0,8},{4,12},{8,0},{12,4},{16,24},{20,28},{24,16},{28,20},{1,9},{5... | collective-permute-start | bytes 393224 | tf_op jit(solution)/shard_map/ppermute | solution.py:55
  160.4 16.8 %collective-permute-start.46 = (bf16[256,256]{1,0:T(8,128)(2,1)S(1)}, bf16[256,256]{1,0:T(8,128)(2,1)S(1)}, u32[]{:S(2)}, u32[]{:S(2)}) collective-permute-start(bf16[256,256]{1,0:T(8,128)(2,1)S(1)} %get-tuple-element.434), channel_id=1, source_target_pairs={{0,24},{4,28},{8,16},{12,20},{16,8},{20,12},{24,0},{28,4},{1,25},{... | collective-permute-start | bytes 393224 | tf_op jit(solution)/shard_map/ppermute | solution.py:55
  163.0 18.6 %collective-permute-start.47 = (bf16[256,256]{1,0:T(8,128)(2,1)S(1)}, bf16[256,256]{1,0:T(8,128)(2,1)S(1)}, u32[]{:S(2)}, u32[]{:S(2)}) collective-permute-start(bf16[256,256]{1,0:T(8,128)(2,1)S(1)} %get-tuple-element.435), channel_id=1, source_target_pairs={{0,20},{4,16},{8,28},{12,24},{16,4},{20,0},{24,12},{28,8},{1,21},{... | collective-permute-start | bytes 393224 | tf_op jit(solution)/shard_map/ppermute | solution.py:55
  164.0 24.0 %collective-permute-start.52 = (bf16[512,256]{1,0:T(8,128)(2,1)S(1)}, bf16[512,256]{1,0:T(8,128)(2,1)S(1)}, u32[]{:S(2)}, u32[]{:S(2)}) collective-permute-start(bf16[512,256]{1,0:T(8,128)(2,1)S(1)} %get-tuple-element.456.refs_0_), channel_id=1, source_target_pairs={{0,2},{1,3},{2,0},{3,1},{4,6},{5,7},{6,4},{7,5},{8,10},{9,11},{10,... | collective-permute-start | bytes 786440 | tf_op jit(solution)/shard_map/ppermute | solution.py:55
  165.6 17.2 %collective-permute-start.48 = (bf16[256,256]{1,0:T(8,128)(2,1)S(1)}, bf16[256,256]{1,0:T(8,128)(2,1)S(1)}, u32[]{:S(2)}, u32[]{:S(2)}) collective-permute-start(bf16[256,256]{1,0:T(8,128)(2,1)S(1)} %get-tuple-element.436), channel_id=1, source_target_pairs={{0,16},{4,20},{8,24},{12,28},{16,0},{20,4},{24,8},{28,12},{1,17},{... | collective-permute-start | bytes 393224 | tf_op jit(solution)/shard_map/ppermute | solution.py:55
  168.7 15.7 %collective-permute-start.49 = (bf16[256,256]{1,0:T(8,128)(2,1)S(1)}, bf16[256,256]{1,0:T(8,128)(2,1)S(1)}, u32[]{:S(2)}, u32[]{:S(2)}) collective-permute-start(bf16[256,256]{1,0:T(8,128)(2,1)S(1)} %get-tuple-element.437), channel_id=1, source_target_pairs={{0,12},{4,8},{8,4},{12,0},{16,28},{20,24},{24,20},{28,16},{1,13},{... | collective-permute-start | bytes 393224 | tf_op jit(solution)/shard_map/ppermute | solution.py:55
  182.7 19.8 %collective-permute-start.59 = (bf16[1024,256]{1,0:T(8,128)(2,1)S(1)}, bf16[1024,256]{1,0:T(8,128)(2,1)S(1)}, u32[]{:S(2)}, u32[]{:S(2)}) collective-permute-start(bf16[1024,256]{1,0:T(8,128)(2,1)S(1)} %get-tuple-element.469), channel_id=1, source_target_pairs={{0,4},{4,0},{8,12},{12,8},{16,20},{20,16},{24,28},{28,24},{1,5},{5... | collective-permute-start | bytes 1572872 | tf_op jit(solution)/shard_map/ppermute | solution.py:55
  221.6 16.6 %collective-permute-start.66 = (bf16[256,256]{1,0:T(8,128)(2,1)S(1)}, bf16[256,256]{1,0:T(8,128)(2,1)S(1)}, u32[]{:S(2)}, u32[]{:S(2)}) collective-permute-start(bf16[256,256]{1,0:T(8,128)(2,1)S(1)} %get-tuple-element.493), channel_id=1, source_target_pairs={{0,20},{4,16},{8,28},{12,24},{16,4},{20,0},{24,12},{28,8},{1,21},{... | collective-permute-start | bytes 393224 | tf_op jit(solution)/shard_map/ppermute | solution.py:55
  221.6 40.6 %collective-permute-start.74 = (bf16[1536,256]{1,0:T(8,128)(2,1)S(1)}, bf16[1536,256]{1,0:T(8,128)(2,1)S(1)}, u32[]{:S(2)}, u32[]{:S(2)}) collective-permute-start(bf16[1536,256]{1,0:T(8,128)(2,1)S(1)} %get-tuple-element.517), channel_id=1, source_target_pairs={{0,4},{4,0},{8,12},{12,8},{16,20},{20,16},{24,28},{28,24},{1,5},{5... | collective-permute-start | bytes 2359304 | tf_op jit(solution)/shard_map/ppermute | solution.py:55
  222.8 19.1 %collective-permute-start.67 = (bf16[256,256]{1,0:T(8,128)(2,1)S(1)}, bf16[256,256]{1,0:T(8,128)(2,1)S(1)}, u32[]{:S(2)}, u32[]{:S(2)}) collective-permute-start(bf16[256,256]{1,0:T(8,128)(2,1)S(1)} %get-tuple-element.494), channel_id=1, source_target_pairs={{0,16},{4,20},{8,24},{12,28},{16,0},{20,4},{24,8},{28,12},{1,17},{... | collective-permute-start | bytes 393224 | tf_op jit(solution)/shard_map/ppermute | solution.py:55
  227.0 15.0 %collective-permute-start.68 = (bf16[256,256]{1,0:T(8,128)(2,1)S(1)}, bf16[256,256]{1,0:T(8,128)(2,1)S(1)}, u32[]{:S(2)}, u32[]{:S(2)}) collective-permute-start(bf16[256,256]{1,0:T(8,128)(2,1)S(1)} %get-tuple-element.496), channel_id=1, source_target_pairs={{0,12},{4,8},{8,4},{12,0},{16,28},{20,24},{24,20},{28,16},{1,13},{... | collective-permute-start | bytes 393224 | tf_op jit(solution)/shard_map/ppermute | solution.py:55
  241.9 17.9 %collective-permute-start.75 = (bf16[768,256]{1,0:T(8,128)(2,1)S(1)}, bf16[768,256]{1,0:T(8,128)(2,1)S(1)}, u32[]{:S(2)}, u32[]{:S(2)}) collective-permute-start(bf16[768,256]{1,0:T(8,128)(2,1)S(1)} %get-tuple-element.527), channel_id=1, source_target_pairs={{0,8},{4,12},{8,0},{12,4},{16,24},{20,28},{24,16},{28,20},{1,9},{5... | collective-permute-start | bytes 1179656 | tf_op jit(solution)/shard_map/ppermute | solution.py:55
  257.4 15.9 %collective-permute-start.76 = (bf16[1024,256]{1,0:T(8,128)(2,1)S(1)}, bf16[1024,256]{1,0:T(8,128)(2,1)S(1)}, u32[]{:S(2)}, u32[]{:S(2)}) collective-permute-start(bf16[1024,256]{1,0:T(8,128)(2,1)S(1)} %get-tuple-element.535), channel_id=1, source_target_pairs={{0,4},{4,0},{8,12},{12,8},{16,20},{20,16},{24,28},{28,24},{1,5},{5... | collective-permute-start | bytes 1572872 | tf_op jit(solution)/shard_map/ppermute | solution.py:55
  262.9 15.1 %collective-permute-start.83 = (bf16[768,256]{1,0:T(8,128)(2,1)S(1)}, bf16[768,256]{1,0:T(8,128)(2,1)S(1)}, u32[]{:S(2)}, u32[]{:S(2)}) collective-permute-start(bf16[768,256]{1,0:T(8,128)(2,1)S(1)} %get-tuple-element.564), channel_id=1, source_target_pairs={{0,8},{4,12},{8,0},{12,4},{16,24},{20,28},{24,16},{28,20},{1,9},{5... | collective-permute-start | bytes 1179656 | tf_op jit(solution)/shard_map/ppermute | solution.py:55
  280.2 14.2 %collective-permute-start.81 = (bf16[656,256]{1,0:T(8,128)(2,1)S(1)}, bf16[656,256]{1,0:T(8,128)(2,1)S(1)}, u32[]{:S(2)}, u32[]{:S(2)}) collective-permute-start(bf16[656,256]{1,0:T(8,128)(2,1)S(1)} %get-tuple-element.560), channel_id=1, source_target_pairs={{0,8},{4,12},{8,0},{12,4},{16,24},{20,28},{24,16},{28,20},{1,9},{5... | collective-permute-start | bytes 1007624 | tf_op jit(solution)/shard_map/ppermute | solution.py:55
  (68 other events, 484.9 us)

commit v5 on v4

--- a/solution.py
+++ b/solution.py
@@ -541,6 +541,39 @@
         blocks = blocks[n:]
 
 
+def turn_kernel(count, me_ref, *refs):
+    for blocks, out in zip(
+        [refs[i : i + count] for i in range(0, len(refs) - len(refs) // (count + 1), count)],
+        refs[-(len(refs) // (count + 1)) :],
+    ):
+        for j, ref in enumerate(blocks):
+            out[block_rows(me_ref, j, ref.shape[1]), :] = ref[...].T
+
+
+def turned_kernel(scaled, row_count, joined, me_ref, *refs):
+    *refs, keep, send, sum_out = refs
+    arrays, refs = refs[: len(scaled)], refs[len(scaled) :]
+    rows = sum(ref.shape[0] for ref in arrays) // 2
+    if joined:
+        for other, out in zip(refs[-2:], (keep, send)):
+            out[pl.ds(rows, other.shape[0]), :] = other[...]
+    grad = refs[0][...]
+    wide = grad.astype(f32)
+    sum_out[...] = jnp.sum(wide, axis=0, keepdims=True)
+    chunk = 2 * rows // row_count
+    bit = me_ref[1] & 1
+    base = 0
+    for ref, by_scale in zip(arrays, scaled):
+        value = (from_lanes(refs[1]) * wide).astype(bf16) if by_scale else grad
+        step = 2 * chunk
+        for p in range(ref.shape[0] // step):
+            at = base + p * chunk
+            for out, place in ((keep, bit), (send, 1 - bit)):
+                span = pl.ds(pl.multiple_of(p * step + place * chunk, 16), chunk)
+                out[at : at + chunk, :] = product(ref[span, :], value).astype(bf16)
+        base += ref.shape[0] // 2
+
+
 def tail_kernel(count, row_count, me_ref, *refs):
     blocks, refs = refs[:count], refs[count:]
     weight, bias, cotangent, keep, send, sum_out, out = refs
@@ -662,6 +695,32 @@
         pieces, halves_of, sums = term_halves(*args, joined=joined)
         return Going(pieces, *halves_of, 0), sums
 
+    def turn(*runs):
+        return call(
+            form(turn_kernel, cols),
+            [((sum(b.shape[1] for b in run), nodes), bf16) for run in runs],
+            *[b for run in runs for b in run],
+        )
+
+    def turned_halves(scaled, arrays, grad, scale=None, joined=None):
+        rows = sum(a.shape[0] for a in arrays)
+        pieces, others = ([], ()) if joined is None else joined
+        pieces = [(row_count // 2, rows // row_count), *pieces]
+        keep, send, sums = call(
+            form(turned_kernel, scaled, row_count, joined is not None),
+            [((rows_of(pieces), channels), bf16)] * 2 + [row_vector],
+            *arrays,
+            grad,
+            *(() if scale is None else (scale,)),
+            *others,
+            flops=2 * nodes * rows * channels,
+        )
+        return pieces, [keep, send], sums
+
+    def turned_terms(*args, joined=None):
+        pieces, halves_of, sums = turned_halves(*args, joined=joined)
+        return Going(pieces, *halves_of, 0), sums
+
     def both_halves(matrix, first):
         value, *sent = first
         rest = call(rest_kernel, half_outs, value, matrix, flops=spread_flops // 2)
@@ -722,6 +781,8 @@
         own_counts,
         other_counts,
     )
+    (turned_0,) = turn(gate(blocks_0, sent[-1]))
+    *chunks, turned_0 = tie(*chunks, turned_0)
     (gathered,) = call(
         form(aggregate_kernel, row_count),
         [(block, bf16)],
@@ -794,6 +855,10 @@
         call(rt_kernel, block_outs, *gate([cotangent], sent[-1]), tail_w, flops=square)
     )
     inner_parts = parts_of(inner_near, pairs)
+    turned_1, turned_gathered_0 = turn(
+        gate(blocks_1, sent[-1]), gate(gathered_0, sent[-1])
+    )
+    *chunks, turned_1, turned_gathered_0 = tie(*chunks, turned_1, turned_gathered_0)
     (gathered,) = call(
         form(aggregate_kernel, row_count),
         [(block, bf16)],
@@ -842,8 +907,9 @@
         flops=square,
     )
 
-    blocks_2, (combine_pre_1, *inner_parts) = gather_cols(
-        act, (combine_pre_1, *inner_parts)
+    (turned_gathered_1,) = turn(gate(gathered_1, act))
+    blocks_2, (combine_pre_1, turned_gathered_1, *inner_parts) = gather_cols(
+        act, (combine_pre_1, turned_gathered_1, *inner_parts)
     )
     *blocks, dot, head_grad, scale_2, inner_act = call(
         form(head_kernel, cols),
@@ -890,17 +956,21 @@
     combine_grad, near, pairs = combine_back(
         parts, dots, gather_w1, scale_2, combine_pre_1
     )
-    combine_going, combine_bias_1 = terms(
-        [(cols, True), (cols, False)],
-        [*blocks_1, *gathered_1],
+    combine_going, combine_bias_1 = turned_terms(
+        (True, False),
+        [turned_1, turned_gathered_1],
         *gate([combine_grad], pairs[0]),
         scale_1,
     )
-    parts, (combine_going.keep,) = parts_of(near, pairs, (combine_going.keep,))
+    parts, (combine_going.keep, head_going.came) = parts_of(
+        near, pairs, (combine_going.keep, head_going.came)
+    )
     sent = pool_back(parts)
     chunks = exchange(sent)
     inner_blocks = gather_cols(*gate([inner_act], sent[-1]))
-    *chunks, inner_blocks[-2] = tie(*chunks, inner_blocks[-2])
+    *chunks, inner_blocks[-2], combine_going.came = tie(
+        *chunks, inner_blocks[-2], combine_going.came
+    )
 
     neigh_in = (select_t, neigh_pre_1, combine_grad, self_w1, neigh_w1)
     *blocks, neigh_grad_1, dot = call(
@@ -925,27 +995,32 @@
         saved=[(block, f32)],
         flops=2 * square,
     )
-    parts, (first_going.keep, tail_keep) = parts_of(
-        near, pairs, (first_going.keep, tail_keep)
+    pieces_1, halves_1, neigh_bias_1 = turned_halves(
+        (True,),
+        [turned_1],
+        *gate([neigh_grad_1], pairs[0]),
+        scale_1,
+        joined=([(row_count // 2, width // row_count)], (tail_keep, tail_send)),
+    )
+    parts, (first_going.keep, halves_1[0]) = parts_of(
+        near, pairs, (first_going.keep, halves_1[0])
     )
     dots = all_chips(dot)
 
     combine_grad, near, pairs = combine_back(
         parts, dots, gather_w0, scale_1, combine_pre_0
     )
-    combine_going, combine_bias_0 = terms(
-        [(cols, False), (cols, False)],
-        [*blocks_0, *gathered_0],
-        *gate([combine_grad], pairs[0]),
-        joined=([(row_count // 2, width // row_count)], (tail_keep, tail_send)),
-    )
-    parts, (combine_going.keep,) = parts_of(near, pairs, (combine_going.keep,))
+    combine_going, combine_bias_0 = turned_terms(
+        (False, False),
+        [turned_0, turned_gathered_0],
+        combine_grad,
+        joined=(pieces_1, halves_1),
+    )
+    parts, (combine_going.keep, first_going.came) = parts_of(
+        near, pairs, (combine_going.keep, first_going.came)
+    )
     sent = pool_back(parts)
     chunks = exchange(sent)
-    pieces_1, halves_1, neigh_bias_1 = term_halves(
-        [(cols, True)], blocks_1, *gate([neigh_grad_1], sent[-1]), scale_1
-    )
-    *chunks, halves_1[0] = tie(*chunks, halves_1[0])
 
     neigh_in = (select_t, neigh_pre_0, combine_grad, self_w0, neigh_w0)
     *blocks, neigh_grad = call(
@@ -958,11 +1033,8 @@
     near, pairs = pair_sums(blocks)
     first_going = fold(first_going.after(pairs[0]))
     second_going = fold(combine_going.after(pairs[0]))
-    neigh_going_0, neigh_bias_0 = terms(
-        [(cols, False)],
-        blocks_0,
-        *gate([neigh_grad], pairs[0]),
-        joined=(pieces_1, halves_1),
+    neigh_going_0, neigh_bias_0 = turned_terms(
+        (False,), [turned_0], *gate([neigh_grad], pairs[0])
     )
     parts, (second_going.keep, neigh_going_0.keep, first_going.keep) = parts_of(
         near, pairs, (second_going.keep, neigh_going_0.keep, first_going.keep)
@@ -986,13 +1058,14 @@
         tail_bias_grad,
         flops=square // 2,
     )
-    third_going = fold(second_going.after(keep))
     proj_going = Going(pieces, keep, send, 0)
     last_going = fold(neigh_going_0.after(keep), proj_going)
+    last_going.came, second_going.came = tie(last_going.came, second_going.came)
+    third_going = fold(second_going)
     *blocks, grad_pin = call(
         form(board_rest_kernel, cols),
         [board_block] * cols,
-        *gate(parts, last_going.keep),
+        *gate(parts, last_going.came, third_going.keep),
         kinds,
         board_grad,
         proj_in,
@@ -1001,9 +1074,10 @@
     )
     near, pairs = pair_sums(blocks)
     grad_board = sum(p.astype(f32) for p in parts_of(near, pairs))
+    third_going.came, grad_board = tie(third_going.came, grad_board)
     head_out, combine_out_1 = close(first_going)
-    combine_out_0, tail_out = close(third_going)
-    neigh_out_0, neigh_out_1, proj_out, biases = close(last_going)
+    combine_out_0, neigh_out_1, tail_out = close(third_going)
+    neigh_out_0, proj_out, biases = close(last_going)
     return (
         embeddings,
         grad_pin,

time: 308 us -> 302 us (0.981)
  waiting for transfers between devices: 103 us -> 97.4 us
    ppermute x86, waiting for transfers between devices: 101 us -> 95.1 us  [swap(): return lax.ppermute(array, axis, [(i, i ^ distance) for i in range(size)])]
    pallas_call x47 -> x50, Pallas kernels: 65.2 us -> 62.4 us  [call(): pl.pallas_call(run, out_shape=shapes + placed, in_specs=[pl.BlockSpec(mem...]
  transfers between devices with their start and end apart: 87 -> 87, of which waited for: 41 -> 47; matrix products, arithmetic and copies ran while one was open for 4% -> 4% of each run, Pallas kernels for 19% -> 18%
where the time goes in v5:
time: 302 us
  starting transfers between devices  121 us (40%)
  waiting for transfers between devices  97.4 us (32%)
  Pallas kernels  67.6 us (22%)
  other arithmetic  5.19 us (2%)
  matrix products  5 us (2%)
  local copies, waits for them, and re-layouts  4.44 us (1%)
    ppermute x86, starting transfers between devices, swap(): return lax.ppermute(array, axis, [(i, i ^ distance) for i in range(size)])  115 us
    ppermute x86, waiting for transfers between devices, swap(): return lax.ppermute(array, axis, [(i, i ^ distance) for i in range(size)])  95.1 us
    pallas_call x50, Pallas kernels, call(): pl.pallas_call(run, out_shape=shapes + placed, in_specs=[pl.BlockSpec(mem...  62.4 us
  transfers between devices with their start and end apart: 87, of which 47 were waited for; matrix products, arithmetic and copies ran while one was open for 4% of the time, Pallas kernels for 18%

profile of v5, /device:TPU:0, one launch (start us, length us, event | category | flops | bytes accessed | tf_op | source)
XLA Modules:
  0.0 301.6 jit_solution(12602854559455173946)
XLA Ops:
  3.7 5.8 %all-to-all-start = ((s32[8,1,256]{2,1,0:T(1,128)}), s32[8,1,256]{2,1,0:T(1,128)S(1)}, u32[]{:S(2)}, u32[]{:S(2)}) async-start(s32[8,1,256]{2,1,0:T(1,128)} %bitcast.26), calls=%async_computation | async-start | bytes 16384 | tf_op jit(solution)/shard_map/all_to_all | solution.py:97
  19.4 5.0 %fusion = f32[256,16,128]{2,1,0:T(8,128)S(1)} fusion(s32[256,50]{1,0:T(8,128)S(1)} %copy.35, s32[256,50]{1,0:T(8,128)S(1)} %copy.34, s32[256,50]{1,0:T(8,128)S(1)} %copy.33), kind=kOutput, calls=%fused_computation.1 | convolution fusion | flops 54681600 | bytes 2250752 | tf_op jit(solution)/shard_map/vkh,vkl->vhl/dot_general | solution.py:638
  32.3 3.9 %collective-permute-start.9 = (bf16[256,256]{1,0:T(8,128)(2,1)S(1)}, bf16[256,256]{1,0:T(8,128)(2,1)S(1)}, u32[]{:S(2)}, u32[]{:S(2)}) collective-permute-start(bf16[256,256]{1,0:T(8,128)(2,1)S(1)} %get-tuple-element.345), channel_id=1, source_target_pairs={{0,16},{4,20},{8,24},{12,28},{16,0},{20,4},{24,8},{28,12},{1,17},{... | collective-permute-start | bytes 393224 | tf_op jit(solution)/shard_map/ppermute | solution.py:55
  37.6 9.9 %collective-permute-start.10 = (bf16[256,256]{1,0:T(8,128)(2,1)S(1)}, bf16[256,256]{1,0:T(8,128)(2,1)S(1)}, u32[]{:S(2)}, u32[]{:S(2)}) collective-permute-start(bf16[256,256]{1,0:T(8,128)(2,1)S(1)} %get-tuple-element.347), channel_id=1, source_target_pairs={{0,12},{4,8},{8,4},{12,0},{16,28},{20,24},{24,20},{28,16},{1,13},{... | collective-permute-start | bytes 393224 | tf_op jit(solution)/shard_map/ppermute | solution.py:55
  49.4 3.2 %collective-permute-done.8.refs_2_ = bf16[256,256]{1,0:T(8,128)(2,1)S(1)} collective-permute-done((bf16[256,256]{1,0:T(8,128)(2,1)S(1)}, bf16[256,256]{1,0:T(8,128)(2,1)S(1)}, u32[]{:S(2)}, u32[]{:S(2)}) %collective-permute-start.8) | collective-permute-done | bytes 131104 | tf_op jit(solution)/shard_map/ppermute | solution.py:55
  65.4 3.3 %collective-permute-done.15.refs_2_.refs_6_ = bf16[512,256]{1,0:T(8,128)(2,1)S(1)} collective-permute-done((bf16[512,256]{1,0:T(8,128)(2,1)S(1)}, bf16[512,256]{1,0:T(8,128)(2,1)S(1)}, u32[]{:S(2)}, u32[]{:S(2)}) %collective-permute-start.15) | collective-permute-done | bytes 262176 | tf_op jit(solution)/shard_map/ppermute | solution.py:55
  75.8 4.0 %collective-permute-done.18.refs_2_ = bf16[512,256]{1,0:T(8,128)(2,1)S(1)} collective-permute-done((bf16[512,256]{1,0:T(8,128)(2,1)S(1)}, bf16[512,256]{1,0:T(8,128)(2,1)S(1)}, u32[]{:S(2)}, u32[]{:S(2)}) %collective-permute-start.18) | collective-permute-done | bytes 262176 | tf_op jit(solution)/shard_map/ppermute | solution.py:55
  87.5 3.4 %collective-permute-start.23 = (bf16[256,256]{1,0:T(8,128)(2,1)S(1)}, bf16[256,256]{1,0:T(8,128)(2,1)S(1)}, u32[]{:S(2)}, u32[]{:S(2)}) collective-permute-start(bf16[256,256]{1,0:T(8,128)(2,1)S(1)} %get-tuple-element.400), channel_id=1, source_target_pairs={{0,16},{4,20},{8,24},{12,28},{16,0},{20,4},{24,8},{28,12},{1,17},{... | collective-permute-start | bytes 393224 | tf_op jit(solution)/shard_map/ppermute | solution.py:55
  92.4 9.1 %collective-permute-start.25 = (bf16[256,256]{1,0:T(8,128)(2,1)S(1)}, bf16[256,256]{1,0:T(8,128)(2,1)S(1)}, u32[]{:S(2)}, u32[]{:S(2)}) collective-permute-start(bf16[256,256]{1,0:T(8,128)(2,1)S(1)} %get-tuple-element.403), channel_id=1, source_target_pairs={{0,8},{4,12},{8,0},{12,4},{16,24},{20,28},{24,16},{28,20},{1,9},{5... | collective-permute-start | bytes 393224 | tf_op jit(solution)/shard_map/ppermute | solution.py:55
  121.1 5.9 %collective-permute-done.34.refs_6_ = bf16[512,256]{1,0:T(8,128)(2,1)S(1)} collective-permute-done((bf16[512,256]{1,0:T(8,128)(2,1)S(1)}, bf16[512,256]{1,0:T(8,128)(2,1)S(1)}, u32[]{:S(2)}, u32[]{:S(2)}) %collective-permute-start.34) | collective-permute-done | bytes 262176 | tf_op jit(solution)/shard_map/ppermute | solution.py:55
  141.8 4.2 %collective-permute-done.39.refs_2_ = bf16[512,256]{1,0:T(8,128)(2,1)S(1)} collective-permute-done((bf16[512,256]{1,0:T(8,128)(2,1)S(1)}, bf16[512,256]{1,0:T(8,128)(2,1)S(1)}, u32[]{:S(2)}, u32[]{:S(2)}) %collective-permute-start.39) | collective-permute-done | bytes 262176 | tf_op jit(solution)/shard_map/ppermute | solution.py:55
  164.0 3.3 %collective-permute-start.49 = (bf16[256,256]{1,0:T(8,128)(2,1)S(1)}, bf16[256,256]{1,0:T(8,128)(2,1)S(1)}, u32[]{:S(2)}, u32[]{:S(2)}) collective-permute-start(bf16[256,256]{1,0:T(8,128)(2,1)S(1)} %get-tuple-element.506), channel_id=1, source_target_pairs={{0,16},{4,20},{8,24},{12,28},{16,0},{20,4},{24,8},{28,12},{1,17},{... | collective-permute-start | bytes 393224 | tf_op jit(solution)/shard_map/ppermute | solution.py:55
  171.3 10.0 %collective-permute-start.50 = (bf16[256,256]{1,0:T(8,128)(2,1)S(1)}, bf16[256,256]{1,0:T(8,128)(2,1)S(1)}, u32[]{:S(2)}, u32[]{:S(2)}) collective-permute-start(bf16[256,256]{1,0:T(8,128)(2,1)S(1)} %get-tuple-element.507), channel_id=1, source_target_pairs={{0,12},{4,8},{8,4},{12,0},{16,28},{20,24},{24,20},{28,16},{1,13},{... | collective-permute-start | bytes 393224 | tf_op jit(solution)/shard_map/ppermute | solution.py:55
  189.5 3.1 %neigh_back_kernel.2 = (bf16[512,256]{1,0:T(8,128)(2,1)S(1)}, bf16[512,256]{1,0:T(8,128)(2,1)S(1)}, bf16[512,256]{1,0:T(8,128)(2,1)S(1)}, bf16[512,256]{1,0:T(8,...) custom-call(s32[2]{0:T(128)S(1)} %pad_add_fusion.me_ref, ...), custom_call_target="tpu_custom_call" | custom-call | flops 1073741824 | bytes 7342080 | tf_op jit(solution)/shard_map/neigh_back_kernel/pallas_call | solution.py:187
  197.6 3.3 %tail_kernel.1 = (bf16[512,256]{1,0:T(8,128)(2,1)S(1)}, bf16[512,256]{1,0:T(8,128)(2,1)S(1)}, f32[1,256]{1,0:T(1,128)S(1)}, f32[512,256]{1,0:T(8,128)}) custom-call(s32[2]{0:T(128)S(1)} %pad_add_fusion.me_ref, bf16[512,256]{1,0:T(8,128)(2,1)S(1)} %get-tuple-element.527.refs_0_, bf16[512,256]{1,0:T(8,128)(2,1)S(1)} %collective-permute-done.45.refs_1_, ...), custom_call_target="tpu_custom_call" | custom-call | flops 536870912 | bytes 2885632 | tf_op jit(solution)/shard_map/tail_kernel/pallas_call | solution.py:187
  211.3 5.8 %collective-permute-done.64.refs_1_ = bf16[768,256]{1,0:T(8,128)(2,1)S(1)} collective-permute-done((bf16[768,256]{1,0:T(8,128)(2,1)S(1)}, bf16[768,256]{1,0:T(8,128)(2,1)S(1)}, u32[]{:S(2)}, u32[]{:S(2)}) %collective-permute-start.64) | collective-permute-done | bytes 393248 | tf_op jit(solution)/shard_map/ppermute | solution.py:55
  223.9 3.5 %collective-permute-start.68 = (bf16[256,256]{1,0:T(8,128)(2,1)S(1)}, bf16[256,256]{1,0:T(8,128)(2,1)S(1)}, u32[]{:S(2)}, u32[]{:S(2)}) collective-permute-start(bf16[256,256]{1,0:T(8,128)(2,1)S(1)} %get-tuple-element.571), channel_id=1, source_target_pairs={{0,16},{4,20},{8,24},{12,28},{16,0},{20,4},{24,8},{28,12},{1,17},{... | collective-permute-start | bytes 393224 | tf_op jit(solution)/shard_map/ppermute | solution.py:55
  228.9 10.8 %collective-permute-start.69 = (bf16[256,256]{1,0:T(8,128)(2,1)S(1)}, bf16[256,256]{1,0:T(8,128)(2,1)S(1)}, u32[]{:S(2)}, u32[]{:S(2)}) collective-permute-start(bf16[256,256]{1,0:T(8,128)(2,1)S(1)} %get-tuple-element.573), channel_id=1, source_target_pairs={{0,12},{4,8},{8,4},{12,0},{16,28},{20,24},{24,20},{28,16},{1,13},{... | collective-permute-start | bytes 393224 | tf_op jit(solution)/shard_map/ppermute | solution.py:55
  241.7 3.0 %collective-permute-done.67.refs_2_ = bf16[256,256]{1,0:T(8,128)(2,1)S(1)} collective-permute-done((bf16[256,256]{1,0:T(8,128)(2,1)S(1)}, bf16[256,256]{1,0:T(8,128)(2,1)S(1)}, u32[]{:S(2)}, u32[]{:S(2)}) %collective-permute-start.67) | collective-permute-done | bytes 131104 | tf_op jit(solution)/shard_map/ppermute | solution.py:55
  245.6 3.1 %collective-permute-done.69.refs_4_ = bf16[256,256]{1,0:T(8,128)(2,1)S(1)} collective-permute-done((bf16[256,256]{1,0:T(8,128)(2,1)S(1)}, bf16[256,256]{1,0:T(8,128)(2,1)S(1)}, u32[]{:S(2)}, u32[]{:S(2)}) %collective-permute-start.69) | collective-permute-done | bytes 131104 | tf_op jit(solution)/shard_map/ppermute | solution.py:55
  267.1 4.1 %collective-permute-done.77.refs_3_ = bf16[272,256]{1,0:T(8,128)(2,1)S(1)} collective-permute-done((bf16[272,256]{1,0:T(8,128)(2,1)S(1)}, bf16[272,256]{1,0:T(8,128)(2,1)S(1)}, u32[]{:S(2)}, u32[]{:S(2)}) %collective-permute-start.77) | collective-permute-done | bytes 139296 | tf_op jit(solution)/shard_map/ppermute | solution.py:55
  274.1 5.7 %collective-permute-done.78.refs_1_ = bf16[400,256]{1,0:T(8,128)(2,1)S(1)} collective-permute-done((bf16[400,256]{1,0:T(8,128)(2,1)S(1)}, bf16[400,256]{1,0:T(8,128)(2,1)S(1)}, u32[]{:S(2)}, u32[]{:S(2)}) %collective-permute-start.78) | collective-permute-done | bytes 204832 | tf_op jit(solution)/shard_map/ppermute | solution.py:55
  290.6 3.2 %collective-permute-done.83 = bf16[512,128]{1,0:T(8,128)(2,1)S(1)} collective-permute-done((bf16[512,128]{1,0:T(8,128)(2,1)S(1)}, bf16[512,128]{1,0:T(8,128)(2,1)S(1)}, u32[]{:S(2)}, u32[]{:S(2)}) %collective-permute-start.83) | collective-permute-done | bytes 131104 | tf_op jit(solution)/shard_map/ppermute | solution.py:55
  294.6 4.8 %collective-permute-done.80 = bf16[512,256]{1,0:T(8,128)(2,1)S(1)} collective-permute-done((bf16[512,256]{1,0:T(8,128)(2,1)S(1)}, bf16[512,256]{1,0:T(8,128)(2,1)S(1)}, u32[]{:S(2)}, u32[]{:S(2)}) %collective-permute-start.80) | collective-permute-done | bytes 262176 | tf_op jit(solution)/shard_map/ppermute | solution.py:55
  (244 shorter events, 178.7 us)
Async XLA Ops:
  3.7 12.3 %all-to-all-start = ((s32[8,1,256]{2,1,0:T(1,128)}), s32[8,1,256]{2,1,0:T(1,128)S(1)}, u32[]{:S(2)}, u32[]{:S(2)}) async-start(s32[8,1,256]{2,1,0:T(1,128)} %bitcast.26), calls=%async_computation | async-start | bytes 16384 | tf_op jit(solution)/shard_map/all_to_all | solution.py:97
  26.4 32.4 %collective-permute-start.13 = (bf16[256,2048]{1,0:T(8,128)(2,1)S(1)}, bf16[256,2048]{1,0:T(8,128)(2,1)S(1)}, u32[]{:S(2)}, u32[]{:S(2)}) collective-permute-start(bf16[256,2048]{1,0:T(8,128)(2,1)S(1)} %flat_kernel.1.refs_0_), channel_id=1, source_target_pairs={{0,1},{1,0},{2,3},{3,2},{4,5},{5,4},{6,7},{7,6},{8,9},{9,8},{10,11... | collective-permute-start | bytes 3145736 | tf_op jit(solution)/shard_map/ppermute | solution.py:55
  30.9 16.6 %collective-permute-start.7 = (bf16[256,256]{1,0:T(8,128)(2,1)S(1)}, bf16[256,256]{1,0:T(8,128)(2,1)S(1)}, u32[]{:S(2)}, u32[]{:S(2)}) collective-permute-start(bf16[256,256]{1,0:T(8,128)(2,1)S(1)} %get-tuple-element.343), channel_id=1, source_target_pairs={{0,24},{4,28},{8,16},{12,20},{16,8},{20,12},{24,0},{28,4},{1,25},{... | collective-permute-start | bytes 393224 | tf_op jit(solution)/shard_map/ppermute | solution.py:55
  32.3 20.3 %collective-permute-start.8 = (bf16[256,256]{1,0:T(8,128)(2,1)S(1)}, bf16[256,256]{1,0:T(8,128)(2,1)S(1)}, u32[]{:S(2)}, u32[]{:S(2)}) collective-permute-start(bf16[256,256]{1,0:T(8,128)(2,1)S(1)} %get-tuple-element.344), channel_id=1, source_target_pairs={{0,20},{4,16},{8,28},{12,24},{16,4},{20,0},{24,12},{28,8},{1,21},{... | collective-permute-start | bytes 393224 | tf_op jit(solution)/shard_map/ppermute | solution.py:55
  32.3 21.8 %collective-permute-start.9 = (bf16[256,256]{1,0:T(8,128)(2,1)S(1)}, bf16[256,256]{1,0:T(8,128)(2,1)S(1)}, u32[]{:S(2)}, u32[]{:S(2)}) collective-permute-start(bf16[256,256]{1,0:T(8,128)(2,1)S(1)} %get-tuple-element.345), channel_id=1, source_target_pairs={{0,16},{4,20},{8,24},{12,28},{16,0},{20,4},{24,8},{28,12},{1,17},{... | collective-permute-start | bytes 393224 | tf_op jit(solution)/shard_map/ppermute | solution.py:55
  37.6 19.4 %collective-permute-start.10 = (bf16[256,256]{1,0:T(8,128)(2,1)S(1)}, bf16[256,256]{1,0:T(8,128)(2,1)S(1)}, u32[]{:S(2)}, u32[]{:S(2)}) collective-permute-start(bf16[256,256]{1,0:T(8,128)(2,1)S(1)} %get-tuple-element.347), channel_id=1, source_target_pairs={{0,12},{4,8},{8,4},{12,0},{16,28},{20,24},{24,20},{28,16},{1,13},{... | collective-permute-start | bytes 393224 | tf_op jit(solution)/shard_map/ppermute | solution.py:55
  84.8 16.7 %collective-permute-start.21 = (bf16[256,256]{1,0:T(8,128)(2,1)S(1)}, bf16[256,256]{1,0:T(8,128)(2,1)S(1)}, u32[]{:S(2)}, u32[]{:S(2)}) collective-permute-start(bf16[256,256]{1,0:T(8,128)(2,1)S(1)} %get-tuple-element.398), channel_id=1, source_target_pairs={{0,24},{4,28},{8,16},{12,20},{16,8},{20,12},{24,0},{28,4},{1,25},{... | collective-permute-start | bytes 393224 | tf_op jit(solution)/shard_map/ppermute | solution.py:55
  87.5 18.9 %collective-permute-start.22 = (bf16[256,256]{1,0:T(8,128)(2,1)S(1)}, bf16[256,256]{1,0:T(8,128)(2,1)S(1)}, u32[]{:S(2)}, u32[]{:S(2)}) collective-permute-start(bf16[256,256]{1,0:T(8,128)(2,1)S(1)} %get-tuple-element.399), channel_id=1, source_target_pairs={{0,20},{4,16},{8,28},{12,24},{16,4},{20,0},{24,12},{28,8},{1,21},{... | collective-permute-start | bytes 393224 | tf_op jit(solution)/shard_map/ppermute | solution.py:55
  87.5 20.0 %collective-permute-start.23 = (bf16[256,256]{1,0:T(8,128)(2,1)S(1)}, bf16[256,256]{1,0:T(8,128)(2,1)S(1)}, u32[]{:S(2)}, u32[]{:S(2)}) collective-permute-start(bf16[256,256]{1,0:T(8,128)(2,1)S(1)} %get-tuple-element.400), channel_id=1, source_target_pairs={{0,16},{4,20},{8,24},{12,28},{16,0},{20,4},{24,8},{28,12},{1,17},{... | collective-permute-start | bytes 393224 | tf_op jit(solution)/shard_map/ppermute | solution.py:55
  91.9 15.7 %collective-permute-start.24 = (bf16[256,256]{1,0:T(8,128)(2,1)S(1)}, bf16[256,256]{1,0:T(8,128)(2,1)S(1)}, u32[]{:S(2)}, u32[]{:S(2)}) collective-permute-start(bf16[256,256]{1,0:T(8,128)(2,1)S(1)} %get-tuple-element.402), channel_id=1, source_target_pairs={{0,12},{4,8},{8,4},{12,0},{16,28},{20,24},{24,20},{28,16},{1,13},{... | collective-permute-start | bytes 393224 | tf_op jit(solution)/shard_map/ppermute | solution.py:55
  92.4 16.5 %collective-permute-start.25 = (bf16[256,256]{1,0:T(8,128)(2,1)S(1)}, bf16[256,256]{1,0:T(8,128)(2,1)S(1)}, u32[]{:S(2)}, u32[]{:S(2)}) collective-permute-start(bf16[256,256]{1,0:T(8,128)(2,1)S(1)} %get-tuple-element.403), channel_id=1, source_target_pairs={{0,8},{4,12},{8,0},{12,4},{16,24},{20,28},{24,16},{28,20},{1,9},{5... | collective-permute-start | bytes 393224 | tf_op jit(solution)/shard_map/ppermute | solution.py:55
  152.9 36.6 %collective-permute-start.54 = (bf16[1024,256]{1,0:T(8,128)(2,1)S(1)}, bf16[1024,256]{1,0:T(8,128)(2,1)S(1)}, u32[]{:S(2)}, u32[]{:S(2)}) collective-permute-start(bf16[1024,256]{1,0:T(8,128)(2,1)S(1)} %get-tuple-element.510), channel_id=1, source_target_pairs={{0,4},{4,0},{8,12},{12,8},{16,20},{20,16},{24,28},{28,24},{1,5},{5... | collective-permute-start | bytes 1572872 | tf_op jit(solution)/shard_map/ppermute | solution.py:55
  164.0 19.3 %collective-permute-start.48 = (bf16[256,256]{1,0:T(8,128)(2,1)S(1)}, bf16[256,256]{1,0:T(8,128)(2,1)S(1)}, u32[]{:S(2)}, u32[]{:S(2)}) collective-permute-start(bf16[256,256]{1,0:T(8,128)(2,1)S(1)} %get-tuple-element.505), channel_id=1, source_target_pairs={{0,20},{4,16},{8,28},{12,24},{16,4},{20,0},{24,12},{28,8},{1,21},{... | collective-permute-start | bytes 393224 | tf_op jit(solution)/shard_map/ppermute | solution.py:55
  164.0 20.4 %collective-permute-start.49 = (bf16[256,256]{1,0:T(8,128)(2,1)S(1)}, bf16[256,256]{1,0:T(8,128)(2,1)S(1)}, u32[]{:S(2)}, u32[]{:S(2)}) collective-permute-start(bf16[256,256]{1,0:T(8,128)(2,1)S(1)} %get-tuple-element.506), channel_id=1, source_target_pairs={{0,16},{4,20},{8,24},{12,28},{16,0},{20,4},{24,8},{28,12},{1,17},{... | collective-permute-start | bytes 393224 | tf_op jit(solution)/shard_map/ppermute | solution.py:55
  168.9 20.6 %collective-permute-start.53 = (bf16[512,256]{1,0:T(8,128)(2,1)S(1)}, bf16[512,256]{1,0:T(8,128)(2,1)S(1)}, u32[]{:S(2)}, u32[]{:S(2)}) collective-permute-start(bf16[512,256]{1,0:T(8,128)(2,1)S(1)} %get-tuple-element.527.refs_0_), channel_id=1, source_target_pairs={{0,2},{1,3},{2,0},{3,1},{4,6},{5,7},{6,4},{7,5},{8,10},{9,11},{10,... | collective-permute-start | bytes 786440 | tf_op jit(solution)/shard_map/ppermute | solution.py:55
  171.3 16.3 %collective-permute-start.50 = (bf16[256,256]{1,0:T(8,128)(2,1)S(1)}, bf16[256,256]{1,0:T(8,128)(2,1)S(1)}, u32[]{:S(2)}, u32[]{:S(2)}) collective-permute-start(bf16[256,256]{1,0:T(8,128)(2,1)S(1)} %get-tuple-element.507), channel_id=1, source_target_pairs={{0,12},{4,8},{8,4},{12,0},{16,28},{20,24},{24,20},{28,16},{1,13},{... | collective-permute-start | bytes 393224 | tf_op jit(solution)/shard_map/ppermute | solution.py:55
  207.8 48.9 %collective-permute-start.75 = (bf16[2048,256]{1,0:T(8,128)(2,1)S(1)}, bf16[2048,256]{1,0:T(8,128)(2,1)S(1)}, u32[]{:S(2)}, u32[]{:S(2)}) collective-permute-start(bf16[2048,256]{1,0:T(8,128)(2,1)S(1)} %get-tuple-element.583), channel_id=1, source_target_pairs={{0,4},{4,0},{8,12},{12,8},{16,20},{20,16},{24,28},{28,24},{1,5},{5... | collective-permute-start | bytes 3145736 | tf_op jit(solution)/shard_map/ppermute | solution.py:55
  221.4 18.4 %collective-permute-start.66 = (bf16[256,256]{1,0:T(8,128)(2,1)S(1)}, bf16[256,256]{1,0:T(8,128)(2,1)S(1)}, u32[]{:S(2)}, u32[]{:S(2)}) collective-permute-start(bf16[256,256]{1,0:T(8,128)(2,1)S(1)} %get-tuple-element.569), channel_id=1, source_target_pairs={{0,24},{4,28},{8,16},{12,20},{16,8},{20,12},{24,0},{28,4},{1,25},{... | collective-permute-start | bytes 393224 | tf_op jit(solution)/shard_map/ppermute | solution.py:55
  223.9 20.8 %collective-permute-start.67 = (bf16[256,256]{1,0:T(8,128)(2,1)S(1)}, bf16[256,256]{1,0:T(8,128)(2,1)S(1)}, u32[]{:S(2)}, u32[]{:S(2)}) collective-permute-start(bf16[256,256]{1,0:T(8,128)(2,1)S(1)} %get-tuple-element.570), channel_id=1, source_target_pairs={{0,20},{4,16},{8,28},{12,24},{16,4},{20,0},{24,12},{28,8},{1,21},{... | collective-permute-start | bytes 393224 | tf_op jit(solution)/shard_map/ppermute | solution.py:55
  223.9 21.7 %collective-permute-start.68 = (bf16[256,256]{1,0:T(8,128)(2,1)S(1)}, bf16[256,256]{1,0:T(8,128)(2,1)S(1)}, u32[]{:S(2)}, u32[]{:S(2)}) collective-permute-start(bf16[256,256]{1,0:T(8,128)(2,1)S(1)} %get-tuple-element.571), channel_id=1, source_target_pairs={{0,16},{4,20},{8,24},{12,28},{16,0},{20,4},{24,8},{28,12},{1,17},{... | collective-permute-start | bytes 393224 | tf_op jit(solution)/shard_map/ppermute | solution.py:55
  228.9 19.8 %collective-permute-start.69 = (bf16[256,256]{1,0:T(8,128)(2,1)S(1)}, bf16[256,256]{1,0:T(8,128)(2,1)S(1)}, u32[]{:S(2)}, u32[]{:S(2)}) collective-permute-start(bf16[256,256]{1,0:T(8,128)(2,1)S(1)} %get-tuple-element.573), channel_id=1, source_target_pairs={{0,12},{4,8},{8,4},{12,0},{16,28},{20,24},{24,20},{28,16},{1,13},{... | collective-permute-start | bytes 393224 | tf_op jit(solution)/shard_map/ppermute | solution.py:55
  257.5 22.4 %collective-permute-start.79 = (bf16[1024,256]{1,0:T(8,128)(2,1)S(1)}, bf16[1024,256]{1,0:T(8,128)(2,1)S(1)}, u32[]{:S(2)}, u32[]{:S(2)}) collective-permute-start(bf16[1024,256]{1,0:T(8,128)(2,1)S(1)} %get-tuple-element.612), channel_id=1, source_target_pairs={{0,8},{4,12},{8,0},{12,4},{16,24},{20,28},{24,16},{28,20},{1,9},{5... | collective-permute-start | bytes 1572872 | tf_op jit(solution)/shard_map/ppermute | solution.py:55
  260.2 13.9 %collective-permute-start.85 = (bf16[384,256]{1,0:T(8,128)(2,1)S(1)}, bf16[384,256]{1,0:T(8,128)(2,1)S(1)}, u32[]{:S(2)}, u32[]{:S(2)}) collective-permute-start(bf16[384,256]{1,0:T(8,128)(2,1)S(1)} %get-tuple-element.636), channel_id=1, source_target_pairs={{0,16},{4,20},{8,24},{12,28},{16,0},{20,4},{24,8},{28,12},{1,17},{... | collective-permute-start | bytes 589832 | tf_op jit(solution)/shard_map/ppermute | solution.py:55
  284.3 15.1 %collective-permute-start.80 = (bf16[512,256]{1,0:T(8,128)(2,1)S(1)}, bf16[512,256]{1,0:T(8,128)(2,1)S(1)}, u32[]{:S(2)}, u32[]{:S(2)}) collective-permute-start(bf16[512,256]{1,0:T(8,128)(2,1)S(1)} %get-tuple-element.622), channel_id=1, source_target_pairs={{0,16},{4,20},{8,24},{12,28},{16,0},{20,4},{24,8},{28,12},{1,17},{... | collective-permute-start | bytes 786440 | tf_op jit(solution)/shard_map/ppermute | solution.py:55
  (68 other events, 451.1 us)

commit v6 on v5

--- a/solution.py
+++ b/solution.py
@@ -774,7 +774,6 @@
             flops=square + spread_flops // 2,
         ),
     )
-    chunks = exchange(sent)
     counts, counts_t = call(
         counts_kernel,
         [((nodes, pool_size), bf16), ((pool_size, nodes), bf16)],
@@ -782,7 +781,8 @@
         other_counts,
     )
     (turned_0,) = turn(gate(blocks_0, sent[-1]))
-    *chunks, turned_0 = tie(*chunks, turned_0)
+    sent[-2], counts, counts_t, turned_0 = tie(sent[-2], counts, counts_t, turned_0)
+    chunks = exchange(sent)
     (gathered,) = call(
         form(aggregate_kernel, row_count),
         [(block, bf16)],
@@ -850,7 +850,6 @@
             flops=square + spread_flops // 2,
         ),
     )
-    chunks = exchange(sent)
     inner_near, pairs = pair_sums(
         call(rt_kernel, block_outs, *gate([cotangent], sent[-1]), tail_w, flops=square)
     )
@@ -858,7 +857,8 @@
     turned_1, turned_gathered_0 = turn(
         gate(blocks_1, sent[-1]), gate(gathered_0, sent[-1])
     )
-    *chunks, turned_1, turned_gathered_0 = tie(*chunks, turned_1, turned_gathered_0)
+    sent[-2], turned_1, turned_gathered_0 = tie(sent[-2], turned_1, turned_gathered_0)
+    chunks = exchange(sent)
     (gathered,) = call(
         form(aggregate_kernel, row_count),
         [(block, bf16)],

time: 302 us -> 298 us (0.987)
  transfers between devices with their start and end apart: 87 -> 87, of which waited for: 47 -> 44; matrix products, arithmetic and copies ran while one was open for 4% -> 4% of each run, Pallas kernels for 18% -> 18%
where the time goes in v6:
time: 298 us; the launch traced here: 297 us
  starting transfers between devices  118 us (40%)
  waiting for transfers between devices  95.9 us (32%)
  Pallas kernels  67.6 us (23%)
  other arithmetic  5.21 us (2%)
  matrix products  5 us (2%)
  local copies, waits for them, and re-layouts  4.44 us (1%)
    ppermute x86, starting transfers between devices, swap(): return lax.ppermute(array, axis, [(i, i ^ distance) for i in range(size)])  112 us
    ppermute x86, waiting for transfers between devices, swap(): return lax.ppermute(array, axis, [(i, i ^ distance) for i in range(size)])  93.5 us
    pallas_call x50, Pallas kernels, call(): pl.pallas_call(run, out_shape=shapes + placed, in_specs=[pl.BlockSpec(mem...  62.4 us
  transfers between devices with their start and end apart: 87, of which 44 were waited for; matrix products, arithmetic and copies ran while one was open for 4% of the time, Pallas kernels for 18%

profile of v6, /device:TPU:0, one launch (start us, length us, event | category | flops | bytes accessed | tf_op | source)
XLA Modules:
  0.0 297.3 jit_solution(15892450323669324905)
XLA Ops:
  0.7 3.0 %collective-permute-start.1 = (bf16[512,128]{1,0:T(8,128)(2,1)}, bf16[512,128]{1,0:T(8,128)(2,1)S(1)}, u32[]{:S(2)}, u32[]{:S(2)}) collective-permute-start(bf16[512,128]{1,0:T(8,128)(2,1)} %refs_3_.5), channel_id=1, source_target_pairs={{0,2},{1,3},{2,0},{3,1},{4,6},{5,7},{6,4},{7,5},{8,10},{9,11},{10,... | collective-permute-start | bytes 393224 | tf_op jit(solution)/shard_map/ppermute | solution.py:55
  3.7 5.8 %all-to-all-start = ((s32[8,1,256]{2,1,0:T(1,128)}), s32[8,1,256]{2,1,0:T(1,128)S(1)}, u32[]{:S(2)}, u32[]{:S(2)}) async-start(s32[8,1,256]{2,1,0:T(1,128)} %bitcast.26), calls=%async_computation | async-start | bytes 16384 | tf_op jit(solution)/shard_map/all_to_all | solution.py:97
  19.4 5.0 %fusion = f32[256,16,128]{2,1,0:T(8,128)S(1)} fusion(s32[256,50]{1,0:T(8,128)S(1)} %copy.35, s32[256,50]{1,0:T(8,128)S(1)} %copy.34, s32[256,50]{1,0:T(8,128)S(1)} %copy.33), kind=kOutput, calls=%fused_computation.1 | convolution fusion | flops 54681600 | bytes 2250752 | tf_op jit(solution)/shard_map/vkh,vkl->vhl/dot_general | solution.py:638
  32.4 3.8 %collective-permute-start.9 = (bf16[256,256]{1,0:T(8,128)(2,1)S(1)}, bf16[256,256]{1,0:T(8,128)(2,1)S(1)}, u32[]{:S(2)}, u32[]{:S(2)}) collective-permute-start(bf16[256,256]{1,0:T(8,128)(2,1)S(1)} %get-tuple-element.333), channel_id=1, source_target_pairs={{0,16},{4,20},{8,24},{12,28},{16,0},{20,4},{24,8},{28,12},{1,17},{... | collective-permute-start | bytes 393224 | tf_op jit(solution)/shard_map/ppermute | solution.py:55
  39.4 8.7 %collective-permute-start.11 = (bf16[256,256]{1,0:T(8,128)(2,1)S(1)}, bf16[256,256]{1,0:T(8,128)(2,1)S(1)}, u32[]{:S(2)}, u32[]{:S(2)}) collective-permute-start(bf16[256,256]{1,0:T(8,128)(2,1)S(1)} %get-tuple-element.336), channel_id=1, source_target_pairs={{0,8},{4,12},{8,0},{12,4},{16,24},{20,28},{24,16},{28,20},{1,9},{5... | collective-permute-start | bytes 393224 | tf_op jit(solution)/shard_map/ppermute | solution.py:55
  48.6 4.0 %collective-permute-done.8.refs_2_ = bf16[256,256]{1,0:T(8,128)(2,1)S(1)} collective-permute-done((bf16[256,256]{1,0:T(8,128)(2,1)S(1)}, bf16[256,256]{1,0:T(8,128)(2,1)S(1)}, u32[]{:S(2)}, u32[]{:S(2)}) %collective-permute-start.8) | collective-permute-done | bytes 131104 | tf_op jit(solution)/shard_map/ppermute | solution.py:55
  61.6 3.4 %collective-permute-done.15.refs_2_.refs_6_ = bf16[512,256]{1,0:T(8,128)(2,1)S(1)} collective-permute-done((bf16[512,256]{1,0:T(8,128)(2,1)S(1)}, bf16[512,256]{1,0:T(8,128)(2,1)S(1)}, u32[]{:S(2)}, u32[]{:S(2)}) %collective-permute-start.15) | collective-permute-done | bytes 262176 | tf_op jit(solution)/shard_map/ppermute | solution.py:55
  72.1 4.0 %collective-permute-done.18.refs_2_ = bf16[512,256]{1,0:T(8,128)(2,1)S(1)} collective-permute-done((bf16[512,256]{1,0:T(8,128)(2,1)S(1)}, bf16[512,256]{1,0:T(8,128)(2,1)S(1)}, u32[]{:S(2)}, u32[]{:S(2)}) %collective-permute-start.18) | collective-permute-done | bytes 262176 | tf_op jit(solution)/shard_map/ppermute | solution.py:55
  83.7 4.6 %collective-permute-start.23 = (bf16[256,256]{1,0:T(8,128)(2,1)S(1)}, bf16[256,256]{1,0:T(8,128)(2,1)S(1)}, u32[]{:S(2)}, u32[]{:S(2)}) collective-permute-start(bf16[256,256]{1,0:T(8,128)(2,1)S(1)} %get-tuple-element.383), channel_id=1, source_target_pairs={{0,16},{4,20},{8,24},{12,28},{16,0},{20,4},{24,8},{28,12},{1,17},{... | collective-permute-start | bytes 393224 | tf_op jit(solution)/shard_map/ppermute | solution.py:55
  89.4 8.1 %collective-permute-start.25 = (bf16[256,256]{1,0:T(8,128)(2,1)S(1)}, bf16[256,256]{1,0:T(8,128)(2,1)S(1)}, u32[]{:S(2)}, u32[]{:S(2)}) collective-permute-start(bf16[256,256]{1,0:T(8,128)(2,1)S(1)} %get-tuple-element.386), channel_id=1, source_target_pairs={{0,8},{4,12},{8,0},{12,4},{16,24},{20,28},{24,16},{28,20},{1,9},{5... | collective-permute-start | bytes 393224 | tf_op jit(solution)/shard_map/ppermute | solution.py:55
  98.5 4.2 %collective-permute-done.22.refs_2_ = bf16[256,256]{1,0:T(8,128)(2,1)S(1)} collective-permute-done((bf16[256,256]{1,0:T(8,128)(2,1)S(1)}, bf16[256,256]{1,0:T(8,128)(2,1)S(1)}, u32[]{:S(2)}, u32[]{:S(2)}) %collective-permute-start.22) | collective-permute-done | bytes 131104 | tf_op jit(solution)/shard_map/ppermute | solution.py:55
  117.3 5.9 %collective-permute-done.34.refs_6_ = bf16[512,256]{1,0:T(8,128)(2,1)S(1)} collective-permute-done((bf16[512,256]{1,0:T(8,128)(2,1)S(1)}, bf16[512,256]{1,0:T(8,128)(2,1)S(1)}, u32[]{:S(2)}, u32[]{:S(2)}) %collective-permute-start.34) | collective-permute-done | bytes 262176 | tf_op jit(solution)/shard_map/ppermute | solution.py:55
  138.0 4.2 %collective-permute-done.39.refs_2_ = bf16[512,256]{1,0:T(8,128)(2,1)S(1)} collective-permute-done((bf16[512,256]{1,0:T(8,128)(2,1)S(1)}, bf16[512,256]{1,0:T(8,128)(2,1)S(1)}, u32[]{:S(2)}, u32[]{:S(2)}) %collective-permute-start.39) | collective-permute-done | bytes 262176 | tf_op jit(solution)/shard_map/ppermute | solution.py:55
  160.3 3.3 %collective-permute-start.49 = (bf16[256,256]{1,0:T(8,128)(2,1)S(1)}, bf16[256,256]{1,0:T(8,128)(2,1)S(1)}, u32[]{:S(2)}, u32[]{:S(2)}) collective-permute-start(bf16[256,256]{1,0:T(8,128)(2,1)S(1)} %get-tuple-element.482), channel_id=1, source_target_pairs={{0,16},{4,20},{8,24},{12,28},{16,0},{20,4},{24,8},{28,12},{1,17},{... | collective-permute-start | bytes 393224 | tf_op jit(solution)/shard_map/ppermute | solution.py:55
  167.6 9.3 %collective-permute-start.50 = (bf16[256,256]{1,0:T(8,128)(2,1)S(1)}, bf16[256,256]{1,0:T(8,128)(2,1)S(1)}, u32[]{:S(2)}, u32[]{:S(2)}) collective-permute-start(bf16[256,256]{1,0:T(8,128)(2,1)S(1)} %get-tuple-element.483), channel_id=1, source_target_pairs={{0,12},{4,8},{8,4},{12,0},{16,28},{20,24},{24,20},{28,16},{1,13},{... | collective-permute-start | bytes 393224 | tf_op jit(solution)/shard_map/ppermute | solution.py:55
  185.4 3.1 %neigh_back_kernel.2 = (bf16[512,256]{1,0:T(8,128)(2,1)S(1)}, bf16[512,256]{1,0:T(8,128)(2,1)S(1)}, bf16[512,256]{1,0:T(8,128)(2,1)S(1)}, bf16[512,256]{1,0:T(8,...) custom-call(s32[2]{0:T(128)S(1)} %pad_add_fusion.me_ref, ...), custom_call_target="tpu_custom_call" | custom-call | flops 1073741824 | bytes 7342080 | tf_op jit(solution)/shard_map/neigh_back_kernel/pallas_call | solution.py:187
  193.5 3.3 %tail_kernel.1 = (bf16[512,256]{1,0:T(8,128)(2,1)S(1)}, bf16[512,256]{1,0:T(8,128)(2,1)S(1)}, f32[1,256]{1,0:T(1,128)S(1)}, f32[512,256]{1,0:T(8,128)}) custom-call(s32[2]{0:T(128)S(1)} %pad_add_fusion.me_ref, bf16[512,256]{1,0:T(8,128)(2,1)S(1)} %get-tuple-element.503.refs_0_, bf16[512,256]{1,0:T(8,128)(2,1)S(1)} %collective-permute-done.45.refs_1_, ...), custom_call_target="tpu_custom_call" | custom-call | flops 536870912 | bytes 2885632 | tf_op jit(solution)/shard_map/tail_kernel/pallas_call | solution.py:187
  206.8 6.3 %collective-permute-done.64.refs_1_ = bf16[768,256]{1,0:T(8,128)(2,1)S(1)} collective-permute-done((bf16[768,256]{1,0:T(8,128)(2,1)S(1)}, bf16[768,256]{1,0:T(8,128)(2,1)S(1)}, u32[]{:S(2)}, u32[]{:S(2)}) %collective-permute-start.64) | collective-permute-done | bytes 393248 | tf_op jit(solution)/shard_map/ppermute | solution.py:55
  219.7 3.2 %collective-permute-start.68 = (bf16[256,256]{1,0:T(8,128)(2,1)S(1)}, bf16[256,256]{1,0:T(8,128)(2,1)S(1)}, u32[]{:S(2)}, u32[]{:S(2)}) collective-permute-start(bf16[256,256]{1,0:T(8,128)(2,1)S(1)} %get-tuple-element.547), channel_id=1, source_target_pairs={{0,16},{4,20},{8,24},{12,28},{16,0},{20,4},{24,8},{28,12},{1,17},{... | collective-permute-start | bytes 393224 | tf_op jit(solution)/shard_map/ppermute | solution.py:55
  224.4 11.2 %collective-permute-start.69 = (bf16[256,256]{1,0:T(8,128)(2,1)S(1)}, bf16[256,256]{1,0:T(8,128)(2,1)S(1)}, u32[]{:S(2)}, u32[]{:S(2)}) collective-permute-start(bf16[256,256]{1,0:T(8,128)(2,1)S(1)} %get-tuple-element.549), channel_id=1, source_target_pairs={{0,12},{4,8},{8,4},{12,0},{16,28},{20,24},{24,20},{28,16},{1,13},{... | collective-permute-start | bytes 393224 | tf_op jit(solution)/shard_map/ppermute | solution.py:55
  262.8 3.9 %collective-permute-done.77.refs_3_ = bf16[272,256]{1,0:T(8,128)(2,1)S(1)} collective-permute-done((bf16[272,256]{1,0:T(8,128)(2,1)S(1)}, bf16[272,256]{1,0:T(8,128)(2,1)S(1)}, u32[]{:S(2)}, u32[]{:S(2)}) %collective-permute-start.77) | collective-permute-done | bytes 139296 | tf_op jit(solution)/shard_map/ppermute | solution.py:55
  269.6 5.7 %collective-permute-done.78.refs_1_ = bf16[400,256]{1,0:T(8,128)(2,1)S(1)} collective-permute-done((bf16[400,256]{1,0:T(8,128)(2,1)S(1)}, bf16[400,256]{1,0:T(8,128)(2,1)S(1)}, u32[]{:S(2)}, u32[]{:S(2)}) %collective-permute-start.78) | collective-permute-done | bytes 204832 | tf_op jit(solution)/shard_map/ppermute | solution.py:55
  286.1 3.2 %collective-permute-done.83 = bf16[512,128]{1,0:T(8,128)(2,1)S(1)} collective-permute-done((bf16[512,128]{1,0:T(8,128)(2,1)S(1)}, bf16[512,128]{1,0:T(8,128)(2,1)S(1)}, u32[]{:S(2)}, u32[]{:S(2)}) %collective-permute-start.83) | collective-permute-done | bytes 131104 | tf_op jit(solution)/shard_map/ppermute | solution.py:55
  290.1 4.9 %collective-permute-done.80 = bf16[512,256]{1,0:T(8,128)(2,1)S(1)} collective-permute-done((bf16[512,256]{1,0:T(8,128)(2,1)S(1)}, bf16[512,256]{1,0:T(8,128)(2,1)S(1)}, u32[]{:S(2)}, u32[]{:S(2)}) %collective-permute-start.80) | collective-permute-done | bytes 262176 | tf_op jit(solution)/shard_map/ppermute | solution.py:55
  (244 shorter events, 173.8 us)
Async XLA Ops:
  3.7 12.3 %all-to-all-start = ((s32[8,1,256]{2,1,0:T(1,128)}), s32[8,1,256]{2,1,0:T(1,128)S(1)}, u32[]{:S(2)}, u32[]{:S(2)}) async-start(s32[8,1,256]{2,1,0:T(1,128)} %bitcast.26), calls=%async_computation | async-start | bytes 16384 | tf_op jit(solution)/shard_map/all_to_all | solution.py:97
  30.9 17.2 %collective-permute-start.7 = (bf16[256,256]{1,0:T(8,128)(2,1)S(1)}, bf16[256,256]{1,0:T(8,128)(2,1)S(1)}, u32[]{:S(2)}, u32[]{:S(2)}) collective-permute-start(bf16[256,256]{1,0:T(8,128)(2,1)S(1)} %get-tuple-element.331), channel_id=1, source_target_pairs={{0,24},{4,28},{8,16},{12,20},{16,8},{20,12},{24,0},{28,4},{1,25},{... | collective-permute-start | bytes 393224 | tf_op jit(solution)/shard_map/ppermute | solution.py:55
  32.3 20.3 %collective-permute-start.8 = (bf16[256,256]{1,0:T(8,128)(2,1)S(1)}, bf16[256,256]{1,0:T(8,128)(2,1)S(1)}, u32[]{:S(2)}, u32[]{:S(2)}) collective-permute-start(bf16[256,256]{1,0:T(8,128)(2,1)S(1)} %get-tuple-element.332), channel_id=1, source_target_pairs={{0,20},{4,16},{8,28},{12,24},{16,4},{20,0},{24,12},{28,8},{1,21},{... | collective-permute-start | bytes 393224 | tf_op jit(solution)/shard_map/ppermute | solution.py:55
  32.4 21.8 %collective-permute-start.9 = (bf16[256,256]{1,0:T(8,128)(2,1)S(1)}, bf16[256,256]{1,0:T(8,128)(2,1)S(1)}, u32[]{:S(2)}, u32[]{:S(2)}) collective-permute-start(bf16[256,256]{1,0:T(8,128)(2,1)S(1)} %get-tuple-element.333), channel_id=1, source_target_pairs={{0,16},{4,20},{8,24},{12,28},{16,0},{20,4},{24,8},{28,12},{1,17},{... | collective-permute-start | bytes 393224 | tf_op jit(solution)/shard_map/ppermute | solution.py:55
  38.1 16.1 %collective-permute-start.10 = (bf16[256,256]{1,0:T(8,128)(2,1)S(1)}, bf16[256,256]{1,0:T(8,128)(2,1)S(1)}, u32[]{:S(2)}, u32[]{:S(2)}) collective-permute-start(bf16[256,256]{1,0:T(8,128)(2,1)S(1)} %get-tuple-element.335), channel_id=1, source_target_pairs={{0,12},{4,8},{8,4},{12,0},{16,28},{20,24},{24,20},{28,16},{1,13},{... | collective-permute-start | bytes 393224 | tf_op jit(solution)/shard_map/ppermute | solution.py:55
  39.4 16.8 %collective-permute-start.11 = (bf16[256,256]{1,0:T(8,128)(2,1)S(1)}, bf16[256,256]{1,0:T(8,128)(2,1)S(1)}, u32[]{:S(2)}, u32[]{:S(2)}) collective-permute-start(bf16[256,256]{1,0:T(8,128)(2,1)S(1)} %get-tuple-element.336), channel_id=1, source_target_pairs={{0,8},{4,12},{8,0},{12,4},{16,24},{20,28},{24,16},{28,20},{1,9},{5... | collective-permute-start | bytes 393224 | tf_op jit(solution)/shard_map/ppermute | solution.py:55
  80.3 17.2 %collective-permute-start.21 = (bf16[256,256]{1,0:T(8,128)(2,1)S(1)}, bf16[256,256]{1,0:T(8,128)(2,1)S(1)}, u32[]{:S(2)}, u32[]{:S(2)}) collective-permute-start(bf16[256,256]{1,0:T(8,128)(2,1)S(1)} %get-tuple-element.381), channel_id=1, source_target_pairs={{0,24},{4,28},{8,16},{12,20},{16,8},{20,12},{24,0},{28,4},{1,25},{... | collective-permute-start | bytes 393224 | tf_op jit(solution)/shard_map/ppermute | solution.py:55
  83.6 19.1 %collective-permute-start.22 = (bf16[256,256]{1,0:T(8,128)(2,1)S(1)}, bf16[256,256]{1,0:T(8,128)(2,1)S(1)}, u32[]{:S(2)}, u32[]{:S(2)}) collective-permute-start(bf16[256,256]{1,0:T(8,128)(2,1)S(1)} %get-tuple-element.382), channel_id=1, source_target_pairs={{0,20},{4,16},{8,28},{12,24},{16,4},{20,0},{24,12},{28,8},{1,21},{... | collective-permute-start | bytes 393224 | tf_op jit(solution)/shard_map/ppermute | solution.py:55
  83.7 19.2 %collective-permute-start.23 = (bf16[256,256]{1,0:T(8,128)(2,1)S(1)}, bf16[256,256]{1,0:T(8,128)(2,1)S(1)}, u32[]{:S(2)}, u32[]{:S(2)}) collective-permute-start(bf16[256,256]{1,0:T(8,128)(2,1)S(1)} %get-tuple-element.383), channel_id=1, source_target_pairs={{0,16},{4,20},{8,24},{12,28},{16,0},{20,4},{24,8},{28,12},{1,17},{... | collective-permute-start | bytes 393224 | tf_op jit(solution)/shard_map/ppermute | solution.py:55
  88.3 14.6 %collective-permute-start.24 = (bf16[256,256]{1,0:T(8,128)(2,1)S(1)}, bf16[256,256]{1,0:T(8,128)(2,1)S(1)}, u32[]{:S(2)}, u32[]{:S(2)}) collective-permute-start(bf16[256,256]{1,0:T(8,128)(2,1)S(1)} %get-tuple-element.385), channel_id=1, source_target_pairs={{0,12},{4,8},{8,4},{12,0},{16,28},{20,24},{24,20},{28,16},{1,13},{... | collective-permute-start | bytes 393224 | tf_op jit(solution)/shard_map/ppermute | solution.py:55
  89.4 14.8 %collective-permute-start.25 = (bf16[256,256]{1,0:T(8,128)(2,1)S(1)}, bf16[256,256]{1,0:T(8,128)(2,1)S(1)}, u32[]{:S(2)}, u32[]{:S(2)}) collective-permute-start(bf16[256,256]{1,0:T(8,128)(2,1)S(1)} %get-tuple-element.386), channel_id=1, source_target_pairs={{0,8},{4,12},{8,0},{12,4},{16,24},{20,28},{24,16},{28,20},{1,9},{5... | collective-permute-start | bytes 393224 | tf_op jit(solution)/shard_map/ppermute | solution.py:55
  149.1 36.3 %collective-permute-start.54 = (bf16[1024,256]{1,0:T(8,128)(2,1)S(1)}, bf16[1024,256]{1,0:T(8,128)(2,1)S(1)}, u32[]{:S(2)}, u32[]{:S(2)}) collective-permute-start(bf16[1024,256]{1,0:T(8,128)(2,1)S(1)} %get-tuple-element.486), channel_id=1, source_target_pairs={{0,4},{4,0},{8,12},{12,8},{16,20},{20,16},{24,28},{28,24},{1,5},{5... | collective-permute-start | bytes 1572872 | tf_op jit(solution)/shard_map/ppermute | solution.py:55
  160.3 18.9 %collective-permute-start.48 = (bf16[256,256]{1,0:T(8,128)(2,1)S(1)}, bf16[256,256]{1,0:T(8,128)(2,1)S(1)}, u32[]{:S(2)}, u32[]{:S(2)}) collective-permute-start(bf16[256,256]{1,0:T(8,128)(2,1)S(1)} %get-tuple-element.481), channel_id=1, source_target_pairs={{0,20},{4,16},{8,28},{12,24},{16,4},{20,0},{24,12},{28,8},{1,21},{... | collective-permute-start | bytes 393224 | tf_op jit(solution)/shard_map/ppermute | solution.py:55
  160.3 19.6 %collective-permute-start.49 = (bf16[256,256]{1,0:T(8,128)(2,1)S(1)}, bf16[256,256]{1,0:T(8,128)(2,1)S(1)}, u32[]{:S(2)}, u32[]{:S(2)}) collective-permute-start(bf16[256,256]{1,0:T(8,128)(2,1)S(1)} %get-tuple-element.482), channel_id=1, source_target_pairs={{0,16},{4,20},{8,24},{12,28},{16,0},{20,4},{24,8},{28,12},{1,17},{... | collective-permute-start | bytes 393224 | tf_op jit(solution)/shard_map/ppermute | solution.py:55
  165.1 20.2 %collective-permute-start.53 = (bf16[512,256]{1,0:T(8,128)(2,1)S(1)}, bf16[512,256]{1,0:T(8,128)(2,1)S(1)}, u32[]{:S(2)}, u32[]{:S(2)}) collective-permute-start(bf16[512,256]{1,0:T(8,128)(2,1)S(1)} %get-tuple-element.503.refs_0_), channel_id=1, source_target_pairs={{0,2},{1,3},{2,0},{3,1},{4,6},{5,7},{6,4},{7,5},{8,10},{9,11},{10,... | collective-permute-start | bytes 786440 | tf_op jit(solution)/shard_map/ppermute | solution.py:55
  167.6 15.9 %collective-permute-start.50 = (bf16[256,256]{1,0:T(8,128)(2,1)S(1)}, bf16[256,256]{1,0:T(8,128)(2,1)S(1)}, u32[]{:S(2)}, u32[]{:S(2)}) collective-permute-start(bf16[256,256]{1,0:T(8,128)(2,1)S(1)} %get-tuple-element.483), channel_id=1, source_target_pairs={{0,12},{4,8},{8,4},{12,0},{16,28},{20,24},{24,20},{28,16},{1,13},{... | collective-permute-start | bytes 393224 | tf_op jit(solution)/shard_map/ppermute | solution.py:55
  203.6 48.6 %collective-permute-start.75 = (bf16[2048,256]{1,0:T(8,128)(2,1)S(1)}, bf16[2048,256]{1,0:T(8,128)(2,1)S(1)}, u32[]{:S(2)}, u32[]{:S(2)}) collective-permute-start(bf16[2048,256]{1,0:T(8,128)(2,1)S(1)} %get-tuple-element.559), channel_id=1, source_target_pairs={{0,4},{4,0},{8,12},{12,8},{16,20},{20,16},{24,28},{28,24},{1,5},{5... | collective-permute-start | bytes 3145736 | tf_op jit(solution)/shard_map/ppermute | solution.py:55
  217.4 18.2 %collective-permute-start.66 = (bf16[256,256]{1,0:T(8,128)(2,1)S(1)}, bf16[256,256]{1,0:T(8,128)(2,1)S(1)}, u32[]{:S(2)}, u32[]{:S(2)}) collective-permute-start(bf16[256,256]{1,0:T(8,128)(2,1)S(1)} %get-tuple-element.545), channel_id=1, source_target_pairs={{0,24},{4,28},{8,16},{12,20},{16,8},{20,12},{24,0},{28,4},{1,25},{... | collective-permute-start | bytes 393224 | tf_op jit(solution)/shard_map/ppermute | solution.py:55
  219.7 20.4 %collective-permute-start.67 = (bf16[256,256]{1,0:T(8,128)(2,1)S(1)}, bf16[256,256]{1,0:T(8,128)(2,1)S(1)}, u32[]{:S(2)}, u32[]{:S(2)}) collective-permute-start(bf16[256,256]{1,0:T(8,128)(2,1)S(1)} %get-tuple-element.546), channel_id=1, source_target_pairs={{0,20},{4,16},{8,28},{12,24},{16,4},{20,0},{24,12},{28,8},{1,21},{... | collective-permute-start | bytes 393224 | tf_op jit(solution)/shard_map/ppermute | solution.py:55
  219.7 21.8 %collective-permute-start.68 = (bf16[256,256]{1,0:T(8,128)(2,1)S(1)}, bf16[256,256]{1,0:T(8,128)(2,1)S(1)}, u32[]{:S(2)}, u32[]{:S(2)}) collective-permute-start(bf16[256,256]{1,0:T(8,128)(2,1)S(1)} %get-tuple-element.547), channel_id=1, source_target_pairs={{0,16},{4,20},{8,24},{12,28},{16,0},{20,4},{24,8},{28,12},{1,17},{... | collective-permute-start | bytes 393224 | tf_op jit(solution)/shard_map/ppermute | solution.py:55
  224.4 19.7 %collective-permute-start.69 = (bf16[256,256]{1,0:T(8,128)(2,1)S(1)}, bf16[256,256]{1,0:T(8,128)(2,1)S(1)}, u32[]{:S(2)}, u32[]{:S(2)}) collective-permute-start(bf16[256,256]{1,0:T(8,128)(2,1)S(1)} %get-tuple-element.549), channel_id=1, source_target_pairs={{0,12},{4,8},{8,4},{12,0},{16,28},{20,24},{24,20},{28,16},{1,13},{... | collective-permute-start | bytes 393224 | tf_op jit(solution)/shard_map/ppermute | solution.py:55
  253.0 22.4 %collective-permute-start.79 = (bf16[1024,256]{1,0:T(8,128)(2,1)S(1)}, bf16[1024,256]{1,0:T(8,128)(2,1)S(1)}, u32[]{:S(2)}, u32[]{:S(2)}) collective-permute-start(bf16[1024,256]{1,0:T(8,128)(2,1)S(1)} %get-tuple-element.588), channel_id=1, source_target_pairs={{0,8},{4,12},{8,0},{12,4},{16,24},{20,28},{24,16},{28,20},{1,9},{5... | collective-permute-start | bytes 1572872 | tf_op jit(solution)/shard_map/ppermute | solution.py:55
  255.9 13.7 %collective-permute-start.85 = (bf16[384,256]{1,0:T(8,128)(2,1)S(1)}, bf16[384,256]{1,0:T(8,128)(2,1)S(1)}, u32[]{:S(2)}, u32[]{:S(2)}) collective-permute-start(bf16[384,256]{1,0:T(8,128)(2,1)S(1)} %get-tuple-element.612), channel_id=1, source_target_pairs={{0,16},{4,20},{8,24},{12,28},{16,0},{20,4},{24,8},{28,12},{1,17},{... | collective-permute-start | bytes 589832 | tf_op jit(solution)/shard_map/ppermute | solution.py:55
  280.2 14.8 %collective-permute-start.80 = (bf16[512,256]{1,0:T(8,128)(2,1)S(1)}, bf16[512,256]{1,0:T(8,128)(2,1)S(1)}, u32[]{:S(2)}, u32[]{:S(2)}) collective-permute-start(bf16[512,256]{1,0:T(8,128)(2,1)S(1)} %get-tuple-element.598), channel_id=1, source_target_pairs={{0,16},{4,20},{8,24},{12,28},{16,0},{20,4},{24,8},{28,12},{1,17},{... | collective-permute-start | bytes 786440 | tf_op jit(solution)/shard_map/ppermute | solution.py:55
  (68 other events, 457.6 us)
